TPU v7x, 256 devices: a whole 4x4x8 slice. The times are simulated.
256 devices in a mesh: seq: 64 (over y, z, core), mp: 4 (over x).
Axes of the slice: x: 4, y: 4, z: 8, core: 2. Of those that a mesh axis runs over, the one named last changes fastest.
Arguments:
- query: bfloat16 [16384, 8192], P('seq', 'mp'), may hold values from -5 to 5
- image_key_values: bfloat16 [2, 64, 64, 1024], P(None, 'seq', 'mp'), may hold values from -5 to 5
- image_count: int32 [64], P('seq'), may hold values from 2 to 64, as said below
- block_images: int32 [128, 6], P('seq'), may hold values from 0 to 63, as said below
- block_reads: int32 [128], P('seq'), may hold values from 3 to 6
- output_gradient: bfloat16 [16384, 8192], P('seq', 'mp'), may hold values from -6 to 6
Outputs:
- attended: bfloat16 [16384, 8192], P('seq', 'mp')
- grad_query: bfloat16 [16384, 8192], P('seq', 'mp')
- grad_kv: float32 [2, 64, 64, 1024], P(None, 'seq', 'mp')
Inputs may be any that keep to these rules, and one draw needn't show every extreme that they name: Slots j >= image_count[i] of image i hold padding. `block_images`: the ids in one row are different; only the first block_reads[b] entries of row b are read.
All inputs are finite; a program needn't handle non-finite values.
Results may differ from a plain program's by a relative error of at most 0.03.
Values may be sent and summed in bfloat16 or wider, within the bound.
No kernel may reach another device: no remote copies, remote signals or barrier semaphores. Data moves between devices by JAX's collectives and lax.ppermute only.
A program may use at most 128 MiB of HBM per device.

v0:
```python
import jax
import jax.numpy as jnp
from jax import lax
from jax.sharding import PartitionSpec as P

QUERY_HEADS = 64
KEY_VALUE_HEADS = 8
HEAD_WIDTH = 128
MAX_BLOCK_READS = 6


def attend_block(q_block, g_block, image_indices, reads, local_kv, valid_tok):
    scale = HEAD_WIDTH ** (-0.5)
    ntok = local_kv.shape[2]
    width = local_kv.shape[3]
    kv_heads = width // HEAD_WIDTH
    image_keys = local_kv[0][image_indices].reshape(MAX_BLOCK_READS * ntok, kv_heads, HEAD_WIDTH)
    image_values = local_kv[1][image_indices].reshape(MAX_BLOCK_READS * ntok, kv_heads, HEAD_WIDTH)
    live = (jnp.arange(MAX_BLOCK_READS, dtype=jnp.int32)[:, None] < reads) & valid_tok[
        image_indices
    ]
    live = live.reshape(MAX_BLOCK_READS * ntok)
    scores = (
        jnp.einsum("tgad,lgd->gatl", q_block, image_keys, preferred_element_type=jnp.float32)
        * scale
    )
    scores = jnp.where(live, scores, -jnp.inf)
    top = jnp.max(scores, axis=-1, keepdims=True)
    expo = jnp.exp(scores - top)
    probs = expo / jnp.sum(expo, axis=-1, keepdims=True)
    probs_b = probs.astype(jnp.bfloat16)
    attention_output = jnp.einsum(
        "gatl,lgd->tgad", probs_b, image_values, preferred_element_type=jnp.float32
    ).astype(jnp.bfloat16)
    delta = jnp.einsum(
        "tgad,tgad->gat", g_block.astype(jnp.float32), attention_output.astype(jnp.float32)
    )
    dprobs = jnp.einsum("tgad,lgd->gatl", g_block, image_values, preferred_element_type=jnp.float32)
    dscores = (probs * (dprobs - delta[..., None]) * scale).astype(jnp.bfloat16)
    query_gradient = jnp.einsum(
        "gatl,lgd->tgad", dscores, image_keys, preferred_element_type=jnp.float32
    ).astype(jnp.bfloat16)
    key_gradient = jnp.einsum(
        "gatl,tgad->lgd", dscores, q_block, preferred_element_type=jnp.float32
    )
    value_gradient = jnp.einsum(
        "gatl,tgad->lgd", probs_b, g_block, preferred_element_type=jnp.float32
    )
    rows = q_block.shape[0]
    return (
        attention_output.reshape(rows, -1),
        query_gradient.reshape(rows, -1),
        key_gradient.reshape(MAX_BLOCK_READS, ntok, width),
        value_gradient.reshape(MAX_BLOCK_READS, ntok, width),
    )


def local(query, image_key_values, image_count, block_images, block_reads, output_gradient):
    collected = lax.all_gather(image_key_values, "seq", axis=1, tiled=True)
    local_kv = lax.all_to_all(collected, "mp", split_axis=3, concat_axis=2, tiled=True)
    counts = lax.all_gather(image_count, "seq", axis=0, tiled=True)
    ntok = local_kv.shape[2]
    width = local_kv.shape[3]
    kv_heads = width // HEAD_WIDTH
    head_group = QUERY_HEADS // KEY_VALUE_HEADS
    valid_tok = jnp.arange(ntok, dtype=jnp.int32)[None, :] < counts[:, None]
    nblocks = block_images.shape[0]
    rows = query.shape[0] // nblocks
    query_blocks = query.reshape(nblocks, rows, kv_heads, head_group, HEAD_WIDTH)
    gradient_blocks = output_gradient.reshape(nblocks, rows, kv_heads, head_group, HEAD_WIDTH)

    def per_block(item):
        q_block, g_block, image_indices, reads = item
        return attend_block(q_block, g_block, image_indices, reads, local_kv, valid_tok)

    outs, dqs, dks, dvs = lax.map(
        per_block, (query_blocks, gradient_blocks, block_images, block_reads)
    )
    flat_ids = block_images.reshape(-1)
    partial_value = jnp.zeros(local_kv.shape, jnp.float32)
    partial_value = partial_value.at[0, flat_ids].add(dks.reshape(-1, ntok, width))
    partial_value = partial_value.at[1, flat_ids].add(dvs.reshape(-1, ntok, width))
    owned = lax.psum_scatter(partial_value, "seq", scatter_dimension=1, tiled=True)
    grad_kv = lax.all_to_all(owned, "mp", split_axis=2, concat_axis=3, tiled=True)
    attended = outs.reshape(query.shape)
    grad_query = dqs.reshape(query.shape)
    return (attended, grad_query, grad_kv)


def solution(mesh):
    placed = (
        P("seq", "mp"),
        P(None, "seq", "mp", None),
        P("seq"),
        P("seq", None),
        P("seq"),
        P("seq", "mp"),
    )
    return jax.shard_map(
        local,
        mesh=mesh,
        in_specs=placed,
        out_specs=(P("seq", "mp"), P("seq", "mp"), P(None, "seq", "mp", None)),
        check_vma=False,
    )
```

profile of v0, /device:TPU:2, one launch (start us, length us, event | category | flops | bytes accessed | tf_op | source)
XLA Modules:
  0.0 475.9 jit_solution(2153160692349483454)
XLA Ops:
  7.9 84.9 %all-gather.2.cloned.1.call-done = bf16[2,64,16,1024]{3,2,0,1:T(8,128)(2,1)} async-done(((bf16[2,1,16,1024]{3,2,0,1:T(8,128)(2,1)}), bf16[2,64,16,1024]{3,2,0,1:T(8,128)(2,1)}) %all-gather.2.cloned.1.call-update) | async-done | bytes 4194320 | tf_op jit(solution)/shard_map/all_gather | solution.py:59
  92.8 15.5 %copy.93 = bf16[2,64,16,1024]{1,2,0,3:T(8,128)(2,1)} copy(bf16[2,64,16,1024]{3,2,0,1:T(8,128)(2,1)} %all-gather.2.cloned.1.call-done) | data formatting | bytes 8388608 | tf_op jit(solution)/shard_map/all_gather | solution.py:59
  108.4 9.5 %reshape.179 = bf16[4,2,262144]{2,1,0:T(2,128)(2,1)} reshape(bf16[1024,2,16,64]{3,2,1,0:T(8,128)(2,1)} %bitcast.160) | data formatting | bytes 8388608
  117.9 5.6 %all-to-all-start = ((bf16[4,2,262144]{2,1,0:T(2,128)(2,1)}), bf16[4,2,262144]{2,1,0:T(2,128)(2,1)}, u32[]{:S(2)}, u32[]{:S(2)}) async-start(bf16[4,2,262144]{2,1,0:T(2,128)(2,1)} %reshape.179), calls=%async_computation | async-start | bytes 8388608 | tf_op jit(solution)/shard_map/all_to_all | solution.py:60
  125.4 1.2 copy.139
  128.1 18.0 %all-reduce.2 = s32[64]{0:T(128)S(1)} all-reduce(s32[64]{0:T(128)S(1)} %dynamic-update-slice), channel_id=1, replica_groups=mesh['seq'=64,'mp'=4] {'seq'}, use_global_device_ids=true, to_apply=%add.2 | all-reduce | flops 64 | bytes 512
  146.1 25.5 %all-to-all-done = bf16[4,2,262144]{2,1,0:T(2,128)(2,1)} async-done(((bf16[4,2,262144]{2,1,0:T(2,128)(2,1)}), bf16[4,2,262144]{2,1,0:T(2,128)(2,1)}, u32[]{:S(2)}, u32[]{:S(2)}) %all-to-all-start) | async-done | bytes 4194336 | tf_op jit(solution)/shard_map/all_to_all | solution.py:60
  171.6 9.3 %reshape.180 = bf16[1024,2,16,64]{3,2,1,0:T(8,128)(2,1)} reshape(bf16[4,2,262144]{2,1,0:T(2,128)(2,1)} %all-to-all-done) | data formatting | bytes 8388608
  180.9 13.5 %copy.94 = bf16[2,64,4,16,256]{4,3,2,1,0:T(8,128)(2,1)} copy(bf16[2,64,4,16,256]{1,3,0,4,2:T(8,128)(2,1)} %bitcast.161) | data formatting | bytes 8388608 | tf_op jit(solution)/shard_map/all_to_all | solution.py:60
  194.4 50.6 %while.17 = (s32[]{:T(128)}, bf16[2,128,2048]{2,1,0:T(8,128)(2,1)}, bf16[2,128,2048]{2,1,0:T(8,128)(2,1)}, f32[2,6,64,256]{3,2,1,0:T(8,128)}, f32[2,6,64,256]{3,...) while((s32[]{:T(128)}, bf16[2,128,2048]{2,1,0:T(8,128)(2,1)}, ...), condition=%wide.region_3.4_spmd.clone, body=%wide.region_0.3_spmd.clone.sunk | while | flops 1219759872 | bytes 68603096 | solution.py:76
  199.1 4.8 slice_bitcast_fusion.3
  203.9 2.1 gather_fusion
  206.0 2.1 gather_fusion.2
  213.0 2.7 fusion.60
  224.4 4.8 slice_bitcast_fusion.3
  229.2 2.1 gather_fusion
  231.3 2.1 gather_fusion.2
  238.3 2.7 fusion.60
  245.0 4.3 broadcast_in_dim.36
  249.3 3.2 scatter_fusion
  252.5 3.2 scatter_fusion.1
  255.6 201.9 %all-reduce.6.cloned.1.call-done = f32[2,64,64,256]{3,2,1,0:T(8,128)} async-done(((f32[2,64,64,256]{3,2,1,0:T(8,128)}), f32[2,64,64,256]{3,2,1,0:T(8,128)}) %all-reduce.6.cloned.1.call-update) | async-done | bytes 8388624
  457.5 1.6 constant_dynamic-slice_fusion.3
  459.3 9.1 %all_to_all.36 = f32[2,1,64,256]{3,1,0,2:T(1,128)S(1)} all-to-all(f32[2,1,64,256]{3,1,0,2:T(1,128)S(1)} %copy.99), channel_id=1, replica_groups=mesh['seq'=64,'mp'=4] {'mp'}, dimensions={2} | all-to-all | bytes 262144 | tf_op jit(solution)/shard_map/all_to_all | solution.py:84
  (95 shorter events, 31.1 us)
Async XLA Ops:
  7.2 85.6 %all-gather.2.cloned.1.call-start = ((), (), s32[]{:S(2)}) async-start(), calls=%async_computation.2 | async-start | bytes 4259840 | tf_op jit(solution)/shard_map/all_gather | solution.py:59
  117.9 6.2 %copy-start.6 = (s32[2,6]{1,0:T(2,128)S(1)}, s32[2,6]{1,0:T(2,128)}, u32[]{:S(2)}) copy-start(s32[2,6]{1,0:T(2,128)} %param.11) | copy-start | bytes 148
  117.9 6.3 %copy-start.1 = (bf16[256,2048]{1,0:T(8,128)(2,1)S(1)}, bf16[256,2048]{1,0:T(8,128)(2,1)}, u32[]{:S(2)}) copy-start(bf16[256,2048]{1,0:T(8,128)(2,1)} %param.8) | copy-start | bytes 3145732
  117.9 7.5 %copy-start.2 = (bf16[256,2048]{1,0:T(8,128)(2,1)S(1)}, bf16[256,2048]{1,0:T(8,128)(2,1)}, u32[]{:S(2)}) copy-start(bf16[256,2048]{1,0:T(8,128)(2,1)} %param.13) | copy-start | bytes 3145732
  117.9 53.7 %all-to-all-start = ((bf16[4,2,262144]{2,1,0:T(2,128)(2,1)}), bf16[4,2,262144]{2,1,0:T(2,128)(2,1)}, u32[]{:S(2)}, u32[]{:S(2)}) async-start(bf16[4,2,262144]{2,1,0:T(2,128)(2,1)} %reshape.179), calls=%async_computation | async-start | bytes 8388608 | tf_op jit(solution)/shard_map/all_to_all | solution.py:60
  123.4 3.2 copy-start.5
  123.4 334.1 %all-reduce.6.cloned.1.call-start = ((), (), s32[]{:S(2)}) async-start(), calls=%async_computation.3 | async-start | bytes 16777216
  180.9 13.5 %copy-start.7 = (s32[2]{0:T(128)S(1)}, s32[2]{0:T(128)}, u32[]{:S(2)}) copy-start(s32[2]{0:T(128)} %param.12) | copy-start | bytes 28
  210.1 1.6 copy-start
  235.5 1.6 copy-start
  245.0 4.3 copy-start.4
  245.0 7.5 %copy-start.3 = (f32[2,6,64,256]{3,2,1,0:T(8,128)S(1)}, f32[2,6,64,256]{3,2,1,0:T(8,128)}, u32[]{:S(2)}) copy-start(f32[2,6,64,256]{3,2,1,0:T(8,128)} %get-tuple-element.66) | copy-start | bytes 2359300
Sparse Core Ops, SparseCore 0:
  10.8 81.9 all-gather.1
  255.8 201.7 all-reduce.5
where the time goes:
time: 478 us; the launch traced here: 476 us
  waiting for transfers between devices  313 us (65%)
  local copies, waits for them, and re-layouts  93 us (19%)
  blocking collectives  27.1 us (6%)
  between operations  14.7 us (3%)
  other arithmetic  11 us (2%)
  matrix products  11 us (2%)
  starting transfers between devices  5.61 us (1%)
    unnamed x3, waiting for transfers between devices  203 us
    all_gather x1, waiting for transfers between devices, local(): collected = lax.all_gather(image_key_values, 'seq', axis=1, tiled=True)  84.9 us
    all_to_all x1, waiting for transfers between devices, local(): lax.all_to_all(collected, 'mp', split_axis=3, concat_axis=2, tiled=True)  25.5 us
    unnamed x22, local copies, waits for them, and re-layouts  24.3 us
    unnamed x1, blocking collectives  18 us
    all_gather x1, local copies, waits for them, and re-layouts, local(): collected = lax.all_gather(image_key_values, 'seq', axis=1, tiled=True)  15.5 us
    all_to_all x1, local copies, waits for them, and re-layouts, local(): lax.all_to_all(collected, 'mp', split_axis=3, concat_axis=2, tiled=True)  13.5 us
  transfers between devices with their start and end apart: 3, of which 3 were waited for; matrix products, arithmetic and copies ran while one was open for 1% of the time, Pallas kernels for 0%

commit v1 on v0

v1 whole, which is shorter than its diff:
```python
import functools

import jax
import jax.numpy as jnp
import numpy as np
from jax import lax
from jax.experimental import pallas as pl
from jax.experimental.pallas import tpu as pltpu
from jax.sharding import Mesh, PartitionSpec as P

QUERY_HEADS = 64
KEY_VALUE_HEADS = 8
HEAD_WIDTH = 128
MAX_BLOCK_READS = 6
IMAGE_TOKENS = 64
GROUP = QUERY_HEADS // KEY_VALUE_HEADS
ROWS = 128
KEYS = MAX_BLOCK_READS * IMAGE_TOKENS
SCALE = HEAD_WIDTH**-0.5
LOG2E = 1.4426950408889634
MARKER = 2.0**20
DEAD = -1e30
SEQ = ("y", "z", "c")
Z = 8

f32 = jnp.float32
bf16 = jnp.bfloat16


def mm(a, b, ca, cb):
    return lax.dot_general(a, b, (((ca,), (cb,)), ((), ())), preferred_element_type=f32)


def attend_kernel(
    images, reads, pos, q_ref, g_ref, own_ref, sib_ref,
    att_ref, dq_ref, gown_ref, gsib_ref,
    k_s, v_s, kt_s, vt_s, bias_s, dk_s, dv_s,
):
    b = pl.program_id(0)
    h = pl.program_id(1)

    @pl.when((b == 0) & (h == 0))
    def _():
        gown_ref[...] = jnp.zeros(gown_ref.shape, gown_ref.dtype)
        gsib_ref[...] = jnp.zeros(gsib_ref.shape, gsib_ref.dtype)

    places = []
    for r in range(MAX_BLOCK_READS):
        image = images[b, r]
        rel = ((image >> 1) + Z - pos[0]) & (Z - 1)
        places.append(((image & 1) == pos[1], rel, image >> 4))
    for r, (mine, rel, y) in enumerate(places):
        rows = pl.ds(r * IMAGE_TOKENS, IMAGE_TOKENS)

        def fetch(ref, rel=rel, y=y, rows=rows, r=r):
            k = ref[rel, y, :, 0, h].reshape(IMAGE_TOKENS, HEAD_WIDTH).astype(f32)
            dead = k > 0.5 * MARKER
            k_s[rows, :] = jnp.where(dead, 0.0, k).astype(bf16)
            unread = jnp.where(r < reads[b], 0.0, DEAD)
            bias_s[rows, :] = jnp.where(dead, DEAD, unread)
            v_s[rows, :] = ref[rel, y, :, 1, h].reshape(IMAGE_TOKENS, HEAD_WIDTH)

        pl.when(mine)(functools.partial(fetch, own_ref))
        pl.when(jnp.logical_not(mine))(functools.partial(fetch, sib_ref))
    kt_s[...] = k_s[...].T
    vt_s[...] = v_s[...].T

    k, v, kt, vt = k_s[...], v_s[...], kt_s[...], vt_s[...]
    for i in range(GROUP // 2):
        c0, c1, c2 = 2 * i * HEAD_WIDTH, (2 * i + 1) * HEAD_WIDTH, (2 * i + 2) * HEAD_WIDTH
        q2 = jnp.concatenate([q_ref[:, c0:c1], q_ref[:, c1:c2]], axis=0)
        g2 = jnp.concatenate([g_ref[:, c0:c1], g_ref[:, c1:c2]], axis=0)
        bias = bias_s[...]
        t = mm(k, q2, 1, 1) * (SCALE * LOG2E) + jnp.concatenate([bias, bias], axis=1)
        e = jnp.exp2(t - jnp.max(t, axis=0, keepdims=True))
        p = e * (1.0 / jnp.sum(e, axis=0, keepdims=True))
        pb = p.astype(bf16)
        dp = mm(v, g2, 1, 1)
        delta = jnp.sum(p * dp, axis=0, keepdims=True)
        ds = (p * (dp - delta)).astype(bf16)
        o = mm(vt, pb, 1, 0).astype(bf16).T
        dq = (mm(kt, ds, 1, 0) * SCALE).astype(bf16).T
        att_ref[:, c0:c1], att_ref[:, c1:c2] = o[:ROWS], o[ROWS:]
        dq_ref[:, c0:c1], dq_ref[:, c1:c2] = dq[:ROWS], dq[ROWS:]
        dk, dv = mm(ds, q2, 1, 0), mm(pb, g2, 1, 0)
        if i == 0:
            dk_s[...], dv_s[...] = dk, dv
        else:
            dk_s[...] += dk
            dv_s[...] += dv

    for r, (mine, rel, y) in enumerate(places):
        rows = pl.ds(r * IMAGE_TOKENS, IMAGE_TOKENS)

        def add(ref, rel=rel, y=y, rows=rows):
            shape = (4, IMAGE_TOKENS // 4, HEAD_WIDTH)
            dk = (dk_s[rows, :] * SCALE).reshape(shape)
            dv = dv_s[rows, :].reshape(shape)
            ref[rel, y, :, 0, h] = (ref[rel, y, :, 0, h].astype(f32) + dk).astype(bf16)
            ref[rel, y, :, 1, h] = (ref[rel, y, :, 1, h].astype(f32) + dv).astype(bf16)

        pl.when(mine)(functools.partial(add, gown_ref))
        pl.when(jnp.logical_not(mine))(functools.partial(add, gsib_ref))


def attend(images, reads, pos, query, gradient, own, sib):
    blocks = images.shape[0]
    heads = query.shape[1] // (GROUP * HEAD_WIDTH)
    smem = pl.BlockSpec(memory_space=pltpu.SMEM)
    whole = pl.BlockSpec(memory_space=pltpu.VMEM)
    text = pl.BlockSpec((ROWS, GROUP * HEAD_WIDTH), lambda b, h: (b, h))
    pairs = blocks * heads * GROUP * ROWS * KEYS
    return pl.pallas_call(
        attend_kernel,
        grid=(blocks, heads),
        in_specs=[smem, smem, smem, text, text, whole, whole],
        out_specs=[text, text, whole, whole],
        out_shape=[
            jax.ShapeDtypeStruct(query.shape, bf16),
            jax.ShapeDtypeStruct(query.shape, bf16),
            jax.ShapeDtypeStruct(own.shape, bf16),
            jax.ShapeDtypeStruct(own.shape, bf16),
        ],
        scratch_shapes=[
            pltpu.VMEM((KEYS, HEAD_WIDTH), bf16),
            pltpu.VMEM((KEYS, HEAD_WIDTH), bf16),
            pltpu.VMEM((HEAD_WIDTH, KEYS), bf16),
            pltpu.VMEM((HEAD_WIDTH, KEYS), bf16),
            pltpu.VMEM((KEYS, HEAD_WIDTH), f32),
            pltpu.VMEM((KEYS, HEAD_WIDTH), f32),
            pltpu.VMEM((KEYS, HEAD_WIDTH), f32),
        ],
        compiler_params=pltpu.CompilerParams(
            dimension_semantics=("arbitrary", "arbitrary"), vmem_limit_bytes=40 * 2**20
        ),
        cost_estimate=pl.CostEstimate(
            flops=12 * HEAD_WIDTH * pairs, bytes_accessed=12 * 2**20, transcendentals=pairs
        ),
    )(images, reads, pos, query, gradient, own, sib)


def shift(x, axis, size, by):
    return lax.ppermute(x, axis, [(i, (i + by) % size) for i in range(size)])


def gather_z(unit):
    half = unit.shape[0] // 2
    up, down = [unit], [unit]
    for _ in range(3):
        up.append(shift(up[-1], "z", Z, 1))
        down.append(shift(down[-1], "z", Z, -1))
    far = jnp.concatenate([shift(up[3][:half], "z", Z, 1), shift(down[3][half:], "z", Z, -1)])
    return jnp.stack([unit, down[1], down[2], down[3], far, up[3], up[2], up[1]])


def add(a, b):
    return (a.astype(f32) + b.astype(f32)).astype(bf16)


def reduce_z(part):
    half = part.shape[1] // 2
    up = shift(part[4][:half], "z", Z, 1)
    down = shift(part[4][half:], "z", Z, -1)
    up = jnp.concatenate([add(part[3][:half], up), part[3][half:]])
    down = jnp.concatenate([part[5][:half], add(part[5][half:], down)])
    up, down = shift(up, "z", Z, 1), shift(down, "z", Z, -1)
    up, down = shift(add(part[2], up), "z", Z, 1), shift(add(part[6], down), "z", Z, -1)
    up, down = shift(add(part[1], up), "z", Z, 1), shift(add(part[7], down), "z", Z, -1)
    return part[0].astype(f32) + up.astype(f32) + down.astype(f32)


def local(query, image_key_values, image_count, block_images, block_reads, output_gradient):
    z, c = lax.axis_index("z"), lax.axis_index("c")
    slots = image_key_values.shape[2]
    slot = lax.axis_index("mp") * slots + jnp.arange(slots, dtype=jnp.int32)
    dead = (slot >= image_count[0])[None, :, None] & (jnp.arange(2) == 0)[:, None, None]
    kv = jnp.where(dead, MARKER, image_key_values[:, 0]).astype(bf16)
    kv = kv.reshape(2, slots, 4, 2, HEAD_WIDTH).transpose(2, 0, 3, 1, 4)
    kv = jnp.broadcast_to(kv[None], (4,) + kv.shape).reshape((16,) + kv.shape[1:])
    unit = lax.all_to_all(kv, ("y", "mp"), 0, 0, tiled=True)
    unit = unit.reshape((4, 4) + unit.shape[1:])
    own = gather_z(unit)
    sib = shift(own, "c", 2, 1)
    pos = jnp.stack([z, c]).astype(jnp.int32)
    attended, grad_query, gown, gsib = attend(
        block_images, block_reads, pos, query, output_gradient, own, sib
    )
    part = add(gown, shift(gsib, "c", 2, 1))
    total = reduce_z(part).astype(bf16)
    total = total.reshape((16,) + total.shape[2:])
    total = lax.all_to_all(total, ("y", "mp"), 0, 0, tiled=True)
    total = jnp.sum(total.reshape((4, 4) + total.shape[1:]).astype(f32), axis=0)
    grad_kv = total.transpose(1, 3, 0, 2, 4).reshape(image_key_values.shape)
    return attended, grad_query, grad_kv


def solution(mesh):
    fine = Mesh(np.asarray(mesh.devices).reshape(4, Z, 2, 4), SEQ + ("mp",))
    placed = (
        P(SEQ, "mp"),
        P(None, SEQ, "mp", None),
        P(SEQ),
        P(SEQ, None),
        P(SEQ),
        P(SEQ, "mp"),
    )
    return jax.shard_map(
        local,
        mesh=fine,
        in_specs=placed,
        out_specs=(P(SEQ, "mp"), P(SEQ, "mp"), P(None, SEQ, "mp", None)),
        check_vma=False,
    )
```

time: 478 us -> 126 us (0.26)
  waiting for transfers between devices: 313 us -> 51.8 us
  local copies, waits for them, and re-layouts: 93 us -> 3.29 us
  starting transfers between devices: 5.61 us -> 27.2 us
  Pallas kernels: 0 us -> 13.8 us
  between operations: 14.7 us -> 1.55 us
  matrix products: 11 us -> 0 us
  other arithmetic: 11 us -> 1.88 us
    unnamed x3 -> x0, waiting for transfers between devices: 203 us -> none
    all_gather x1 -> x0, waiting for transfers between devices: 84.9 us -> none  [local(): collected = lax.all_gather(image_key_values, 'seq', axis=1, tiled=True)]
    ppermute x0 -> x18, waiting for transfers between devices: none -> 51.8 us  [shift(): return lax.ppermute(x, axis, [(i, (i + by) % size) for i in range(size)])]
    ppermute x0 -> x18, starting transfers between devices: none -> 27.2 us  [shift(): return lax.ppermute(x, axis, [(i, (i + by) % size) for i in range(size)])]
    all_to_all x1 -> x0, waiting for transfers between devices: 25.5 us -> none  [local(): lax.all_to_all(collected, 'mp', split_axis=3, concat_axis=2, tiled=True)]
    unnamed x22 -> x14, local copies, waits for them, and re-layouts: 24.3 us -> 1.44 us
    unnamed x1 -> x0, blocking collectives: 18 us -> none
    all_to_all x1 -> x2, blocking collectives: 9.12 us -> 26.2 us  [the longest x1 14.6 us: local(): unit = lax.all_to_all(kv, ('y', 'mp'), 0, 0, tiled=True)]
  transfers between devices with their start and end apart: 3 -> 18, of which waited for: 3 -> 11; matrix products, arithmetic and copies ran while one was open for 1% -> 0% of each run, Pallas kernels for 0% -> 0%
where the time goes in v1:
time: 126 us
  waiting for transfers between devices  51.8 us (41%)
  starting transfers between devices  27.2 us (22%)
  blocking collectives  26.2 us (21%)
  Pallas kernels  13.8 us (11%)
  local copies, waits for them, and re-layouts  3.29 us (3%)
  other arithmetic  1.88 us (1%)
  between operations  1.55 us (1%)
    ppermute x18, waiting for transfers between devices, shift(): return lax.ppermute(x, axis, [(i, (i + by) % size) for i in range(size)])  51.8 us
    ppermute x18, starting transfers between devices, shift(): return lax.ppermute(x, axis, [(i, (i + by) % size) for i in range(size)])  27.2 us
    all_to_all x1, blocking collectives, local(): unit = lax.all_to_all(kv, ('y', 'mp'), 0, 0, tiled=True)  14.6 us
    pallas_call x1, Pallas kernels, attend(): pl.pallas_call(attend_kernel, grid=(blocks, heads), in_specs=[smem, smem,...  13.8 us
    all_to_all x1, blocking collectives, local(): total = lax.all_to_all(total, ('y', 'mp'), 0, 0, tiled=True)  11.6 us
  transfers between devices with their start and end apart: 18, of which 11 were waited for; matrix products, arithmetic and copies ran while one was open for 0% of the time, Pallas kernels for 0%

profile of v1, /device:TPU:2, one launch (start us, length us, event | category | flops | bytes accessed | tf_op | source)
XLA Modules:
  0.0 125.7 jit_solution(6795325219250302912)
XLA Ops:
  2.5 14.6 %all_to_all.10 = bf16[16,2,2,16,128]{4,3,2,1,0:T(8,128)(2,1)S(1)} all-to-all(bf16[16,2,2,16,128]{4,3,2,1,0:T(8,128)(2,1)S(1)} %bitcast.75), channel_id=1, replica_groups=mesh['y'=4,'z'=8,'c'=2,'mp'=4] {'y','mp'}, dimensions={0} | all-to-all | bytes 524288 | tf_op jit(solution)/shard_map/all_to_all | solution.py:180
  17.1 1.9 %collective-permute-start.3 = (bf16[4,4,2,2,16,128]{5,4,3,2,1,0:T(8,128)(2,1)S(1)}, bf16[4,4,2,2,16,128]{5,4,3,2,1,0:T(8,128)(2,1)S(1)}, u32[]{:S(2)}, u32[]{:S(2)}) collective-permute-start(bf16[4,4,2,2,16,128]{5,4,3,2,1,0:T(8,128)(2,1)S(1)} %bitcast.76), channel_id=1, source_target_pairs={{0,8},{8,16},{16,24},{24,32},{32,40},{40,48},{48,56},{56,0},{1,9},... | collective-permute-start | bytes 786440 | tf_op jit(solution)/shard_map/ppermute | solution.py:143
  19.0 3.9 %collective-permute-start = (bf16[4,4,2,2,16,128]{5,4,3,2,1,0:T(8,128)(2,1)S(1)}, bf16[4,4,2,2,16,128]{5,4,3,2,1,0:T(8,128)(2,1)S(1)}, u32[]{:S(2)}, u32[]{:S(2)}) collective-permute-start(bf16[4,4,2,2,16,128]{5,4,3,2,1,0:T(8,128)(2,1)S(1)} %bitcast.77), channel_id=1, source_target_pairs={{0,56},{8,0},{16,8},{24,16},{32,24},{40,32},{48,40},{56,48},{1,57}... | collective-permute-start | bytes 786440 | tf_op jit(solution)/shard_map/ppermute | solution.py:143
  22.9 5.2 %collective-permute-done.3 = bf16[4,4,2,2,16,128]{5,4,3,2,1,0:T(8,128)(2,1)S(1)} collective-permute-done((bf16[4,4,2,2,16,128]{5,4,3,2,1,0:T(8,128)(2,1)S(1)}, bf16[4,4,2,2,16,128]{5,4,3,2,1,0:T(8,128)(2,1)S(1)}, u32[]{:S(2)}, u32[]{:S(2)}) %collective-permute-start.3) | collective-permute-done | bytes 262176 | tf_op jit(solution)/shard_map/ppermute | solution.py:143
  28.1 3.2 %collective-permute-start.1 = (bf16[4,4,2,2,16,128]{5,4,3,2,1,0:T(8,128)(2,1)S(1)}, bf16[4,4,2,2,16,128]{5,4,3,2,1,0:T(8,128)(2,1)S(1)}, u32[]{:S(2)}, u32[]{:S(2)}) collective-permute-start(bf16[4,4,2,2,16,128]{5,4,3,2,1,0:T(8,128)(2,1)S(1)} %collective-permute-done), channel_id=1, source_target_pairs={{0,56},{8,0},{16,8},{24,16},{32,24},{40,32},{48,40},{56,48},{1,57}... | collective-permute-start | bytes 786440 | tf_op jit(solution)/shard_map/ppermute | solution.py:143
  31.4 4.3 %collective-permute-done.4 = bf16[4,4,2,2,16,128]{5,4,3,2,1,0:T(8,128)(2,1)S(1)} collective-permute-done((bf16[4,4,2,2,16,128]{5,4,3,2,1,0:T(8,128)(2,1)S(1)}, bf16[4,4,2,2,16,128]{5,4,3,2,1,0:T(8,128)(2,1)S(1)}, u32[]{:S(2)}, u32[]{:S(2)}) %collective-permute-start.4) | collective-permute-done | bytes 262176 | tf_op jit(solution)/shard_map/ppermute | solution.py:143
  35.7 3.2 %collective-permute-start.2 = (bf16[4,4,2,2,16,128]{5,4,3,2,1,0:T(8,128)(2,1)S(1)}, bf16[4,4,2,2,16,128]{5,4,3,2,1,0:T(8,128)(2,1)S(1)}, u32[]{:S(2)}, u32[]{:S(2)}) collective-permute-start(bf16[4,4,2,2,16,128]{5,4,3,2,1,0:T(8,128)(2,1)S(1)} %collective-permute-done.1), channel_id=1, source_target_pairs={{0,56},{8,0},{16,8},{24,16},{32,24},{40,32},{48,40},{56,48},{1,57}... | collective-permute-start | bytes 786440 | tf_op jit(solution)/shard_map/ppermute | solution.py:143
  39.0 4.5 %collective-permute-done.5 = bf16[4,4,2,2,16,128]{5,4,3,2,1,0:T(8,128)(2,1)S(1)} collective-permute-done((bf16[4,4,2,2,16,128]{5,4,3,2,1,0:T(8,128)(2,1)S(1)}, bf16[4,4,2,2,16,128]{5,4,3,2,1,0:T(8,128)(2,1)S(1)}, u32[]{:S(2)}, u32[]{:S(2)}) %collective-permute-start.5) | collective-permute-done | bytes 262176 | tf_op jit(solution)/shard_map/ppermute | solution.py:143
  43.7 3.4 %collective-permute-start.7 = (bf16[2,4,2,2,16,128]{5,4,3,2,1,0:T(8,128)(2,1)S(1)}, bf16[2,4,2,2,16,128]{5,4,3,2,1,0:T(8,128)(2,1)S(1)}, u32[]{:S(2)}, u32[]{:S(2)}) collective-permute-start(bf16[2,4,2,2,16,128]{5,4,3,2,1,0:T(8,128)(2,1)S(1)} %slice.83), channel_id=1, source_target_pairs={{0,56},{8,0},{16,8},{24,16},{32,24},{40,32},{48,40},{56,48},{1,57}... | collective-permute-start | bytes 393224 | tf_op jit(solution)/shard_map/ppermute | solution.py:143
  47.1 2.7 %collective-permute-done.6 = bf16[2,4,2,2,16,128]{5,4,3,2,1,0:T(8,128)(2,1)S(1)} collective-permute-done((bf16[2,4,2,2,16,128]{5,4,3,2,1,0:T(8,128)(2,1)S(1)}, bf16[2,4,2,2,16,128]{5,4,3,2,1,0:T(8,128)(2,1)S(1)}, u32[]{:S(2)}, u32[]{:S(2)}) %collective-permute-start.6) | collective-permute-done | bytes 131104 | tf_op jit(solution)/shard_map/ppermute | solution.py:143
  50.2 4.2 %collective-permute-done.8.sib_ref = bf16[8,4,4,2,2,16,128]{6,5,4,3,2,1,0:T(8,128)(2,1)} collective-permute-done((bf16[8,4,4,2,2,16,128]{6,5,4,3,2,1,0:T(8,128)(2,1)S(1)}, bf16[8,4,4,2,2,16,128]{6,5,4,3,2,1,0:T(8,128)(2,1)}, u32[]{:S(2)}, u32[]{:S(2)}) %collective-permute-start.8) | collective-permute-done | bytes 2097184 | tf_op jit(solution)/shard_map/ppermute | solution.py:143
  54.4 1.2 copy-done.1
  55.6 13.8 %shard_map.85 = (bf16[256,2048]{1,0:T(8,128)(2,1)}, bf16[256,2048]{1,0:T(8,128)(2,1)}, bf16[8,4,4,2,2,16,128]{6,5,4,3,2,1,0:T(8,128)(2,1)S(1)}, bf16[8,4,4,2,2,16,128]{6,5,4,3,2,1,0:T(8,128)(2,1)S(1)}) custom-call(s32[2,6]{1,0:T(2,128)S(1)} %copy-done.2, s32[2]{0:T(128)S(1)} %copy-done.3, s32[2]{0:T(128)S(1)} %pad_add_fusion.pos, ...), custom_call_target="tpu_custom_call" | custom-call | flops 2415919104 | bytes 12582912 | tf_op jit(solution)/shard_map/pallas_call | solution.py:113
  69.6 4.0 %collective-permute-done.9 = bf16[8,4,4,2,2,16,128]{6,5,4,3,2,1,0:T(8,128)(2,1)S(1)} collective-permute-done((bf16[8,4,4,2,2,16,128]{6,5,4,3,2,1,0:T(8,128)(2,1)S(1)}, bf16[8,4,4,2,2,16,128]{6,5,4,3,2,1,0:T(8,128)(2,1)S(1)}, u32[]{:S(2)}, u32[]{:S(2)}) %collective-permute-start.9) | collective-permute-done | bytes 2097184 | tf_op jit(solution)/shard_map/ppermute | solution.py:143
  74.6 3.5 %collective-permute-start.14 = (bf16[2,4,2,2,16,128]{5,4,3,2,1,0:T(8,128)(2,1)S(1)}, bf16[2,4,2,2,16,128]{5,4,3,2,1,0:T(8,128)(2,1)S(1)}, u32[]{:S(2)}, u32[]{:S(2)}) collective-permute-start(bf16[2,4,2,2,16,128]{5,4,3,2,1,0:T(8,128)(2,1)S(1)} %get-tuple-element.19), channel_id=1, source_target_pairs={{0,56},{8,0},{16,8},{24,16},{32,24},{40,32},{48,40},{56,48},{1,57}... | collective-permute-start | bytes 393224 | tf_op jit(solution)/shard_map/ppermute | solution.py:143
  78.2 3.7 %collective-permute-done.10 = bf16[2,4,2,2,16,128]{5,4,3,2,1,0:T(8,128)(2,1)S(1)} collective-permute-done((bf16[2,4,2,2,16,128]{5,4,3,2,1,0:T(8,128)(2,1)S(1)}, bf16[2,4,2,2,16,128]{5,4,3,2,1,0:T(8,128)(2,1)S(1)}, u32[]{:S(2)}, u32[]{:S(2)}) %collective-permute-start.10) | collective-permute-done | bytes 131104 | tf_op jit(solution)/shard_map/ppermute | solution.py:143
  82.0 2.8 %collective-permute-start.11 = (bf16[4,4,2,2,16,128]{5,4,3,2,1,0:T(8,128)(2,1)S(1)}, bf16[4,4,2,2,16,128]{5,4,3,2,1,0:T(8,128)(2,1)S(1)}, u32[]{:S(2)}, u32[]{:S(2)}) collective-permute-start(bf16[4,4,2,2,16,128]{5,4,3,2,1,0:T(8,128)(2,1)S(1)} %pad_maximum_fusion), channel_id=1, source_target_pairs={{0,8},{8,16},{16,24},{24,32},{32,40},{40,48},{48,56},{56,0},{1,9},... | collective-permute-start | bytes 786440 | tf_op jit(solution)/shard_map/ppermute | solution.py:143
  85.4 5.7 %collective-permute-done.11 = bf16[4,4,2,2,16,128]{5,4,3,2,1,0:T(8,128)(2,1)S(1)} collective-permute-done((bf16[4,4,2,2,16,128]{5,4,3,2,1,0:T(8,128)(2,1)S(1)}, bf16[4,4,2,2,16,128]{5,4,3,2,1,0:T(8,128)(2,1)S(1)}, u32[]{:S(2)}, u32[]{:S(2)}) %collective-permute-start.11) | collective-permute-done | bytes 262176 | tf_op jit(solution)/shard_map/ppermute | solution.py:143
  91.2 1.3 %collective-permute-start.12 = (bf16[4,4,2,2,16,128]{5,4,3,2,1,0:T(8,128)(2,1)S(1)}, bf16[4,4,2,2,16,128]{5,4,3,2,1,0:T(8,128)(2,1)S(1)}, u32[]{:S(2)}, u32[]{:S(2)}) collective-permute-start(bf16[4,4,2,2,16,128]{5,4,3,2,1,0:T(8,128)(2,1)S(1)} %fusion.2), channel_id=1, source_target_pairs={{0,8},{8,16},{16,24},{24,32},{32,40},{40,48},{48,56},{56,0},{1,9},... | collective-permute-start | bytes 786440 | tf_op jit(solution)/shard_map/ppermute | solution.py:143
  92.5 7.0 %collective-permute-done.12 = bf16[4,4,2,2,16,128]{5,4,3,2,1,0:T(8,128)(2,1)S(1)} collective-permute-done((bf16[4,4,2,2,16,128]{5,4,3,2,1,0:T(8,128)(2,1)S(1)}, bf16[4,4,2,2,16,128]{5,4,3,2,1,0:T(8,128)(2,1)S(1)}, u32[]{:S(2)}, u32[]{:S(2)}) %collective-permute-start.12) | collective-permute-done | bytes 262176 | tf_op jit(solution)/shard_map/ppermute | solution.py:143
  99.7 2.0 %collective-permute-start.13 = (bf16[4,4,2,2,16,128]{5,4,3,2,1,0:T(8,128)(2,1)S(1)}, bf16[4,4,2,2,16,128]{5,4,3,2,1,0:T(8,128)(2,1)S(1)}, u32[]{:S(2)}, u32[]{:S(2)}) collective-permute-start(bf16[4,4,2,2,16,128]{5,4,3,2,1,0:T(8,128)(2,1)S(1)} %get-tuple-element.14), channel_id=1, source_target_pairs={{0,8},{8,16},{16,24},{24,32},{32,40},{40,48},{48,56},{56,0},{1,9},... | collective-permute-start | bytes 786440 | tf_op jit(solution)/shard_map/ppermute | solution.py:143
  101.7 4.9 %collective-permute-done.16 = bf16[4,4,2,2,16,128]{5,4,3,2,1,0:T(8,128)(2,1)S(1)} collective-permute-done((bf16[4,4,2,2,16,128]{5,4,3,2,1,0:T(8,128)(2,1)S(1)}, bf16[4,4,2,2,16,128]{5,4,3,2,1,0:T(8,128)(2,1)S(1)}, u32[]{:S(2)}, u32[]{:S(2)}) %collective-permute-start.16) | collective-permute-done | bytes 262176 | tf_op jit(solution)/shard_map/ppermute | solution.py:143
  107.5 5.7 %collective-permute-done.17 = bf16[4,4,2,2,16,128]{5,4,3,2,1,0:T(8,128)(2,1)S(1)} collective-permute-done((bf16[4,4,2,2,16,128]{5,4,3,2,1,0:T(8,128)(2,1)S(1)}, bf16[4,4,2,2,16,128]{5,4,3,2,1,0:T(8,128)(2,1)S(1)}, u32[]{:S(2)}, u32[]{:S(2)}) %collective-permute-start.17) | collective-permute-done | bytes 262176 | tf_op jit(solution)/shard_map/ppermute | solution.py:143
  113.2 11.6 %all_to_all.11 = bf16[16,2,2,16,128]{4,3,2,1,0:T(8,128)(2,1)S(1)} all-to-all(bf16[16,2,2,16,128]{4,3,2,1,0:T(8,128)(2,1)S(1)} %bitcast.80), channel_id=1, replica_groups=mesh['y'=4,'z'=8,'c'=2,'mp'=4] {'y','mp'}, dimensions={0} | all-to-all | bytes 524288 | tf_op jit(solution)/shard_map/all_to_all | solution.py:191
  (53 shorter events, 5.8 us)
Async XLA Ops:
  17.1 11.0 %collective-permute-start.3 = (bf16[4,4,2,2,16,128]{5,4,3,2,1,0:T(8,128)(2,1)S(1)}, bf16[4,4,2,2,16,128]{5,4,3,2,1,0:T(8,128)(2,1)S(1)}, u32[]{:S(2)}, u32[]{:S(2)}) collective-permute-start(bf16[4,4,2,2,16,128]{5,4,3,2,1,0:T(8,128)(2,1)S(1)} %bitcast.76), channel_id=1, source_target_pairs={{0,8},{8,16},{16,24},{24,32},{32,40},{40,48},{48,56},{56,0},{1,9},... | collective-permute-start | bytes 786440 | tf_op jit(solution)/shard_map/ppermute | solution.py:143
  19.0 9.1 %collective-permute-start = (bf16[4,4,2,2,16,128]{5,4,3,2,1,0:T(8,128)(2,1)S(1)}, bf16[4,4,2,2,16,128]{5,4,3,2,1,0:T(8,128)(2,1)S(1)}, u32[]{:S(2)}, u32[]{:S(2)}) collective-permute-start(bf16[4,4,2,2,16,128]{5,4,3,2,1,0:T(8,128)(2,1)S(1)} %bitcast.77), channel_id=1, source_target_pairs={{0,56},{8,0},{16,8},{24,16},{32,24},{40,32},{48,40},{56,48},{1,57}... | collective-permute-start | bytes 786440 | tf_op jit(solution)/shard_map/ppermute | solution.py:143
  28.1 7.6 %collective-permute-start.4 = (bf16[4,4,2,2,16,128]{5,4,3,2,1,0:T(8,128)(2,1)S(1)}, bf16[4,4,2,2,16,128]{5,4,3,2,1,0:T(8,128)(2,1)S(1)}, u32[]{:S(2)}, u32[]{:S(2)}) collective-permute-start(bf16[4,4,2,2,16,128]{5,4,3,2,1,0:T(8,128)(2,1)S(1)} %collective-permute-done.3), channel_id=1, source_target_pairs={{0,8},{8,16},{16,24},{24,32},{32,40},{40,48},{48,56},{56,0},{1,9},... | collective-permute-start | bytes 786440 | tf_op jit(solution)/shard_map/ppermute | solution.py:143
  28.1 7.6 %collective-permute-start.1 = (bf16[4,4,2,2,16,128]{5,4,3,2,1,0:T(8,128)(2,1)S(1)}, bf16[4,4,2,2,16,128]{5,4,3,2,1,0:T(8,128)(2,1)S(1)}, u32[]{:S(2)}, u32[]{:S(2)}) collective-permute-start(bf16[4,4,2,2,16,128]{5,4,3,2,1,0:T(8,128)(2,1)S(1)} %collective-permute-done), channel_id=1, source_target_pairs={{0,56},{8,0},{16,8},{24,16},{32,24},{40,32},{48,40},{56,48},{1,57}... | collective-permute-start | bytes 786440 | tf_op jit(solution)/shard_map/ppermute | solution.py:143
  31.4 23.0 %copy-start = (bf16[256,2048]{1,0:T(8,128)(2,1)S(1)}, bf16[256,2048]{1,0:T(8,128)(2,1)}, u32[]{:S(2)}) copy-start(bf16[256,2048]{1,0:T(8,128)(2,1)} %q_ref.1) | copy-start | bytes 3145732
  31.4 23.0 %copy-start.2 = (s32[2,6]{1,0:T(2,128)S(1)}, s32[2,6]{1,0:T(2,128)}, u32[]{:S(2)}) copy-start(s32[2,6]{1,0:T(2,128)} %images.1) | copy-start | bytes 148
  31.4 23.0 %copy-start.3 = (s32[2]{0:T(128)S(1)}, s32[2]{0:T(128)}, u32[]{:S(2)}) copy-start(s32[2]{0:T(128)} %reads.1) | copy-start | bytes 28
  35.7 7.9 %collective-permute-start.5 = (bf16[4,4,2,2,16,128]{5,4,3,2,1,0:T(8,128)(2,1)S(1)}, bf16[4,4,2,2,16,128]{5,4,3,2,1,0:T(8,128)(2,1)S(1)}, u32[]{:S(2)}, u32[]{:S(2)}) collective-permute-start(bf16[4,4,2,2,16,128]{5,4,3,2,1,0:T(8,128)(2,1)S(1)} %collective-permute-done.4), channel_id=1, source_target_pairs={{0,8},{8,16},{16,24},{24,32},{32,40},{40,48},{48,56},{56,0},{1,9},... | collective-permute-start | bytes 786440 | tf_op jit(solution)/shard_map/ppermute | solution.py:143
  35.7 8.0 %collective-permute-start.2 = (bf16[4,4,2,2,16,128]{5,4,3,2,1,0:T(8,128)(2,1)S(1)}, bf16[4,4,2,2,16,128]{5,4,3,2,1,0:T(8,128)(2,1)S(1)}, u32[]{:S(2)}, u32[]{:S(2)}) collective-permute-start(bf16[4,4,2,2,16,128]{5,4,3,2,1,0:T(8,128)(2,1)S(1)} %collective-permute-done.1), channel_id=1, source_target_pairs={{0,56},{8,0},{16,8},{24,16},{32,24},{40,32},{48,40},{56,48},{1,57}... | collective-permute-start | bytes 786440 | tf_op jit(solution)/shard_map/ppermute | solution.py:143
  43.6 6.3 %collective-permute-start.6 = (bf16[2,4,2,2,16,128]{5,4,3,2,1,0:T(8,128)(2,1)S(1)}, bf16[2,4,2,2,16,128]{5,4,3,2,1,0:T(8,128)(2,1)S(1)}, u32[]{:S(2)}, u32[]{:S(2)}) collective-permute-start(bf16[2,4,2,2,16,128]{5,4,3,2,1,0:T(8,128)(2,1)S(1)} %slice.82), channel_id=1, source_target_pairs={{0,8},{8,16},{16,24},{24,32},{32,40},{40,48},{48,56},{56,0},{1,9},... | collective-permute-start | bytes 393224 | tf_op jit(solution)/shard_map/ppermute | solution.py:143
  43.7 6.1 %collective-permute-start.7 = (bf16[2,4,2,2,16,128]{5,4,3,2,1,0:T(8,128)(2,1)S(1)}, bf16[2,4,2,2,16,128]{5,4,3,2,1,0:T(8,128)(2,1)S(1)}, u32[]{:S(2)}, u32[]{:S(2)}) collective-permute-start(bf16[2,4,2,2,16,128]{5,4,3,2,1,0:T(8,128)(2,1)S(1)} %slice.83), channel_id=1, source_target_pairs={{0,56},{8,0},{16,8},{24,16},{32,24},{40,32},{48,40},{56,48},{1,57}... | collective-permute-start | bytes 393224 | tf_op jit(solution)/shard_map/ppermute | solution.py:143
  50.0 4.4 %collective-permute-start.8 = (bf16[8,4,4,2,2,16,128]{6,5,4,3,2,1,0:T(8,128)(2,1)S(1)}, bf16[8,4,4,2,2,16,128]{6,5,4,3,2,1,0:T(8,128)(2,1)}, u32[]{:S(2)}, u32[]{:S(2)}) collective-permute-start(bf16[8,4,4,2,2,16,128]{6,5,4,3,2,1,0:T(8,128)(2,1)S(1)} %bitcast_dynamic-update-slice_fusion.own_ref), channel_id=1, source_target_pairs={{0,4},{4,0},{1,5},{5,1},{2,6},{6,2},{3,7},{7,3},{8,12},{12,8},{9,1... | collective-permute-start | bytes 6291464 | tf_op jit(solution)/shard_map/ppermute | solution.py:143
  54.4 1.2 copy-start.1
  69.4 4.2 %collective-permute-start.9 = (bf16[8,4,4,2,2,16,128]{6,5,4,3,2,1,0:T(8,128)(2,1)S(1)}, bf16[8,4,4,2,2,16,128]{6,5,4,3,2,1,0:T(8,128)(2,1)S(1)}, u32[]{:S(2)}, u32[]{:S(2)}) collective-permute-start(bf16[8,4,4,2,2,16,128]{6,5,4,3,2,1,0:T(8,128)(2,1)S(1)} %get-tuple-element.10), channel_id=1, source_target_pairs={{0,4},{4,0},{1,5},{5,1},{2,6},{6,2},{3,7},{7,3},{8,12},{12,8},{9,1... | collective-permute-start | bytes 6291464 | tf_op jit(solution)/shard_map/ppermute | solution.py:143
  74.6 7.3 %collective-permute-start.10 = (bf16[2,4,2,2,16,128]{5,4,3,2,1,0:T(8,128)(2,1)S(1)}, bf16[2,4,2,2,16,128]{5,4,3,2,1,0:T(8,128)(2,1)S(1)}, u32[]{:S(2)}, u32[]{:S(2)}) collective-permute-start(bf16[2,4,2,2,16,128]{5,4,3,2,1,0:T(8,128)(2,1)S(1)} %get-tuple-element.18), channel_id=1, source_target_pairs={{0,8},{8,16},{16,24},{24,32},{32,40},{40,48},{48,56},{56,0},{1,9},... | collective-permute-start | bytes 393224 | tf_op jit(solution)/shard_map/ppermute | solution.py:143
  74.6 7.2 %collective-permute-start.14 = (bf16[2,4,2,2,16,128]{5,4,3,2,1,0:T(8,128)(2,1)S(1)}, bf16[2,4,2,2,16,128]{5,4,3,2,1,0:T(8,128)(2,1)S(1)}, u32[]{:S(2)}, u32[]{:S(2)}) collective-permute-start(bf16[2,4,2,2,16,128]{5,4,3,2,1,0:T(8,128)(2,1)S(1)} %get-tuple-element.19), channel_id=1, source_target_pairs={{0,56},{8,0},{16,8},{24,16},{32,24},{40,32},{48,40},{56,48},{1,57}... | collective-permute-start | bytes 393224 | tf_op jit(solution)/shard_map/ppermute | solution.py:143
  82.0 9.1 %collective-permute-start.11 = (bf16[4,4,2,2,16,128]{5,4,3,2,1,0:T(8,128)(2,1)S(1)}, bf16[4,4,2,2,16,128]{5,4,3,2,1,0:T(8,128)(2,1)S(1)}, u32[]{:S(2)}, u32[]{:S(2)}) collective-permute-start(bf16[4,4,2,2,16,128]{5,4,3,2,1,0:T(8,128)(2,1)S(1)} %pad_maximum_fusion), channel_id=1, source_target_pairs={{0,8},{8,16},{16,24},{24,32},{32,40},{40,48},{48,56},{56,0},{1,9},... | collective-permute-start | bytes 786440 | tf_op jit(solution)/shard_map/ppermute | solution.py:143
  84.8 7.7 %collective-permute-start.15 = (bf16[4,4,2,2,16,128]{5,4,3,2,1,0:T(8,128)(2,1)S(1)}, bf16[4,4,2,2,16,128]{5,4,3,2,1,0:T(8,128)(2,1)S(1)}, u32[]{:S(2)}, u32[]{:S(2)}) collective-permute-start(bf16[4,4,2,2,16,128]{5,4,3,2,1,0:T(8,128)(2,1)S(1)} %pad_maximum_fusion.1), channel_id=1, source_target_pairs={{0,56},{8,0},{16,8},{24,16},{32,24},{40,32},{48,40},{56,48},{1,57}... | collective-permute-start | bytes 786440 | tf_op jit(solution)/shard_map/ppermute | solution.py:143
  91.2 8.2 %collective-permute-start.12 = (bf16[4,4,2,2,16,128]{5,4,3,2,1,0:T(8,128)(2,1)S(1)}, bf16[4,4,2,2,16,128]{5,4,3,2,1,0:T(8,128)(2,1)S(1)}, u32[]{:S(2)}, u32[]{:S(2)}) collective-permute-start(bf16[4,4,2,2,16,128]{5,4,3,2,1,0:T(8,128)(2,1)S(1)} %fusion.2), channel_id=1, source_target_pairs={{0,8},{8,16},{16,24},{24,32},{32,40},{40,48},{48,56},{56,0},{1,9},... | collective-permute-start | bytes 786440 | tf_op jit(solution)/shard_map/ppermute | solution.py:143
  99.6 7.0 %collective-permute-start.16 = (bf16[4,4,2,2,16,128]{5,4,3,2,1,0:T(8,128)(2,1)S(1)}, bf16[4,4,2,2,16,128]{5,4,3,2,1,0:T(8,128)(2,1)S(1)}, u32[]{:S(2)}, u32[]{:S(2)}) collective-permute-start(bf16[4,4,2,2,16,128]{5,4,3,2,1,0:T(8,128)(2,1)S(1)} %get-tuple-element.15), channel_id=1, source_target_pairs={{0,56},{8,0},{16,8},{24,16},{32,24},{40,32},{48,40},{56,48},{1,57}... | collective-permute-start | bytes 786440 | tf_op jit(solution)/shard_map/ppermute | solution.py:143
  99.7 7.7 %collective-permute-start.13 = (bf16[4,4,2,2,16,128]{5,4,3,2,1,0:T(8,128)(2,1)S(1)}, bf16[4,4,2,2,16,128]{5,4,3,2,1,0:T(8,128)(2,1)S(1)}, u32[]{:S(2)}, u32[]{:S(2)}) collective-permute-start(bf16[4,4,2,2,16,128]{5,4,3,2,1,0:T(8,128)(2,1)S(1)} %get-tuple-element.14), channel_id=1, source_target_pairs={{0,8},{8,16},{16,24},{24,32},{32,40},{40,48},{48,56},{56,0},{1,9},... | collective-permute-start | bytes 786440 | tf_op jit(solution)/shard_map/ppermute | solution.py:143
  106.7 6.5 %collective-permute-start.17 = (bf16[4,4,2,2,16,128]{5,4,3,2,1,0:T(8,128)(2,1)S(1)}, bf16[4,4,2,2,16,128]{5,4,3,2,1,0:T(8,128)(2,1)S(1)}, u32[]{:S(2)}, u32[]{:S(2)}) collective-permute-start(bf16[4,4,2,2,16,128]{5,4,3,2,1,0:T(8,128)(2,1)S(1)} %fusion.1), channel_id=1, source_target_pairs={{0,56},{8,0},{16,8},{24,16},{32,24},{40,32},{48,40},{56,48},{1,57}... | collective-permute-start | bytes 786440 | tf_op jit(solution)/shard_map/ppermute | solution.py:143

commit v2 on v1

v2 whole, which is shorter than its diff:
```python
import functools

import jax
import jax.numpy as jnp
import numpy as np
from jax import lax
from jax.experimental import pallas as pl
from jax.experimental.pallas import tpu as pltpu
from jax.sharding import Mesh, PartitionSpec as P

QUERY_HEADS = 64
KEY_VALUE_HEADS = 8
HEAD_WIDTH = 128
MAX_BLOCK_READS = 6
IMAGE_TOKENS = 64
GROUP = QUERY_HEADS // KEY_VALUE_HEADS
ROWS = 128
KEYS = MAX_BLOCK_READS * IMAGE_TOKENS
SCALE = HEAD_WIDTH**-0.5
LOG2E = 1.4426950408889634
MARKER = 2.0**20
DEAD = -1e30
SEQ = ("y", "z", "c")
Y, Z, M = 4, 8, 4

f32 = jnp.float32
bf16 = jnp.bfloat16


def mm(a, b, ca, cb):
    return lax.dot_general(a, b, (((ca,), (cb,)), ((), ())), preferred_element_type=f32)


def attend_kernel(images, reads, pos, q_ref, g_ref, *refs):
    own, sib = refs[:2], refs[2:4]
    att_ref, dq_ref, gown_ref, gsoon_ref, glate_ref = refs[4:9]
    k_s, v_s, kt_s, vt_s, bias_s, dk_s, dv_s = refs[9:]
    b = pl.program_id(0)
    blocks, heads = dk_s.shape[:2]
    z, c = pos[0], pos[1]

    for r in range(MAX_BLOCK_READS):
        image = images[b, r]
        mine = (image & 1) == c
        rel = ((image >> 1) + Z - z) & (Z - 1)
        late = (rel >= 3) & (rel < 6)
        rows = pl.ds(r * IMAGE_TOKENS, IMAGE_TOKENS)

        def fetch(ref, at, image=image, rows=rows, r=r):
            unread = jnp.where(r < reads[b], 0.0, DEAD)
            for h in range(heads):
                k = ref[at, image >> 4, :, 0, h].reshape(IMAGE_TOKENS, HEAD_WIDTH).astype(f32)
                dead = k > 0.5 * MARKER
                k_s[h, rows, :] = jnp.where(dead, 0.0, k).astype(bf16)
                if h == 0:
                    bias_s[rows, :] = jnp.where(dead, DEAD, unread)
                v_s[h, rows, :] = ref[at, image >> 4, :, 1, h].reshape(IMAGE_TOKENS, HEAD_WIDTH)

        for group, here in ((own, mine), (sib, jnp.logical_not(mine))):
            soon = jnp.logical_not(late)
            at = jnp.where(rel < 3, rel, rel - 3)
            pl.when(here & soon)(functools.partial(fetch, group[0], at))
            pl.when(here & late)(functools.partial(fetch, group[1], rel - 3))
    for h in range(heads):
        kt_s[h] = k_s[h].T
        vt_s[h] = v_s[h].T

    N = 2
    bias = jnp.concatenate([bias_s[...]] * N, axis=1)

    def load(ref, i):
        cols = [slice((N * i + n) * HEAD_WIDTH, (N * i + n + 1) * HEAD_WIDTH) for n in range(N)]
        return jnp.concatenate([ref[:, c] for c in cols], axis=0)

    def front(i):
        h = N * i // GROUP
        return mm(k_s[h], load(q_ref, i), 1, 1), mm(v_s[h], load(g_ref, i), 1, 1)

    def middle(s, dp):
        t = s * (SCALE * LOG2E) + bias
        e = jnp.exp2(t - jnp.max(t, axis=0, keepdims=True))
        p = e * (1.0 / jnp.sum(e, axis=0, keepdims=True))
        delta = jnp.sum(p * dp, axis=0, keepdims=True)
        return p.astype(bf16), (p * (dp - delta)).astype(bf16)

    def back(i, pb, ds):
        h = N * i // GROUP
        o = mm(vt_s[h], pb, 1, 0).astype(bf16).T
        dq = (mm(kt_s[h], ds, 1, 0) * SCALE).astype(bf16).T
        for n in range(N):
            cols = slice((N * i + n) * HEAD_WIDTH, (N * i + n + 1) * HEAD_WIDTH)
            att_ref[:, cols] = o[n * ROWS : (n + 1) * ROWS]
            dq_ref[:, cols] = dq[n * ROWS : (n + 1) * ROWS]
        dk, dv = mm(ds, load(q_ref, i), 1, 0), mm(pb, load(g_ref, i), 1, 0)
        if N * i % GROUP == 0:
            dk_s[b, h], dv_s[b, h] = dk, dv
        else:
            dk_s[b, h] += dk
            dv_s[b, h] += dv

    def clear(i):
        for ref in (gown_ref, gsoon_ref, glate_ref):
            part = ref.shape[0] // blocks
            for j in range(part * i // steps, part * (i + 1) // steps):
                ref[b * part + j] = jnp.zeros(ref.shape[1:], ref.dtype)

    steps = heads * GROUP // N
    ahead, behind = front(0), None
    for i in range(steps):
        clear(i)
        now, ahead = ahead, front(i + 1) if i + 1 < steps else None
        back(i, *middle(*now))

    @pl.when(b == blocks - 1)
    def _():
        for n in range(blocks * MAX_BLOCK_READS):
            block, r = divmod(n, MAX_BLOCK_READS)
            image = images[block, r]
            mine = (image & 1) == c
            rel = ((image >> 1) + Z - z) & (Z - 1)
            row = image >> 4
            rows = pl.ds(r * IMAGE_TOKENS, IMAGE_TOKENS)

            def add(ref, at, block=block, rows=rows):
                tile = (M, IMAGE_TOKENS // M, HEAD_WIDTH)
                for h in range(heads):
                    dk = (dk_s[block, h, rows, :] * SCALE).reshape(tile)
                    dv = dv_s[block, h, rows, :].reshape(tile)
                    ref[at, :, 0, h] = (ref[at, :, 0, h].astype(f32) + dk).astype(bf16)
                    ref[at, :, 1, h] = (ref[at, :, 1, h].astype(f32) + dv).astype(bf16)

            other = jnp.logical_not(mine)
            late = (rel < 3) | (rel > 5)
            at = jnp.where(rel < 3, rel, rel - 3) * Y + row
            pl.when(mine)(functools.partial(add, gown_ref, rel * Y + row))
            pl.when(other & late)(functools.partial(add, glate_ref, at))
            pl.when(other & jnp.logical_not(late))(functools.partial(add, gsoon_ref, (rel - 3) * Y + row))


def attend(images, reads, pos, query, gradient, own, sib):
    blocks = images.shape[0]
    heads = query.shape[1] // (GROUP * HEAD_WIDTH)
    smem = pl.BlockSpec(memory_space=pltpu.SMEM)
    whole = pl.BlockSpec(memory_space=pltpu.VMEM)
    text = pl.BlockSpec((ROWS, query.shape[1]), lambda b: (b, 0))
    pairs = blocks * heads * GROUP * ROWS * KEYS
    unit = own[0].shape[2:]
    return pl.pallas_call(
        attend_kernel,
        grid=(blocks,),
        in_specs=[smem] * 3 + [text] * 2 + [whole] * 4,
        out_specs=[text] * 2 + [whole] * 3,
        out_shape=[
            jax.ShapeDtypeStruct(query.shape, bf16),
            jax.ShapeDtypeStruct(query.shape, bf16),
            jax.ShapeDtypeStruct((Y * Z,) + unit, bf16),
            jax.ShapeDtypeStruct((3 * Y,) + unit, bf16),
            jax.ShapeDtypeStruct((5 * Y,) + unit, bf16),
        ],
        scratch_shapes=[
            pltpu.VMEM((heads, KEYS, HEAD_WIDTH), bf16),
            pltpu.VMEM((heads, KEYS, HEAD_WIDTH), bf16),
            pltpu.VMEM((heads, HEAD_WIDTH, KEYS), bf16),
            pltpu.VMEM((heads, HEAD_WIDTH, KEYS), bf16),
            pltpu.VMEM((KEYS, HEAD_WIDTH), f32),
            pltpu.VMEM((blocks, heads, KEYS, HEAD_WIDTH), f32),
            pltpu.VMEM((blocks, heads, KEYS, HEAD_WIDTH), f32),
        ],
        compiler_params=pltpu.CompilerParams(
            dimension_semantics=("arbitrary",), vmem_limit_bytes=40 * 2**20
        ),
        cost_estimate=pl.CostEstimate(
            flops=12 * HEAD_WIDTH * pairs, bytes_accessed=12 * 2**20, transcendentals=pairs
        ),
    )(images, reads, pos, query, gradient, *own, *sib)


def shift(x, axis, size, by):
    return lax.ppermute(x, axis, [(i, (i + by) % size) for i in range(size)])


def swap(x):
    return shift(x, "c", 2, 1)


def add(*terms):
    return sum(t.astype(f32) for t in terms).astype(bf16)


def gather_z(unit):
    half = unit.shape[0] // 2
    up, down = [unit], [unit]
    for _ in range(3):
        up.append(shift(up[-1], "z", Z, 1))
        down.append(shift(down[-1], "z", Z, -1))
    far = jnp.concatenate([shift(up[3][:half], "z", Z, 1), shift(down[3][half:], "z", Z, -1)])
    return jnp.stack([unit, down[1], down[2], up[2], up[1]]), jnp.stack([down[3], far, up[3]])


def reduce_z(own, soon, late):
    half = Y // 2
    own, soon, late = (x.reshape((-1, Y) + x.shape[1:]) for x in (own, soon, late))

    def sides(a, b):
        return lax.optimization_barrier((shift(a, "z", Z, 1), shift(b, "z", Z, -1)))

    up, down = sides(add(own[4, :half], soon[1, :half]), add(own[4, half:], soon[1, half:]))
    up = jnp.concatenate([add(own[3, :half], soon[0, :half], up), add(own[3, half:], soon[0, half:])])
    down = jnp.concatenate([add(own[5, :half], soon[2, :half]), add(own[5, half:], soon[2, half:], down)])
    up, down = sides(up, down)
    up, down = sides(add(own[2], late[2], up), add(own[6], late[3], down))
    up, down = sides(add(own[1], late[1], up), add(own[7], late[4], down))
    return add(own[0], late[0], up, down)


def local(query, image_key_values, image_count, block_images, block_reads, output_gradient):
    pos = jnp.stack([lax.axis_index("z"), lax.axis_index("c")]).astype(jnp.int32)
    slots = image_key_values.shape[2]
    slot = lax.axis_index("mp") * slots + jnp.arange(slots, dtype=jnp.int32)
    dead = (slot >= image_count[0])[None, :, None] & (jnp.arange(2) == 0)[:, None, None]
    kv = jnp.where(dead, MARKER, image_key_values[:, 0]).astype(bf16)
    kv = kv.reshape(2, slots, M, 2, HEAD_WIDTH).transpose(2, 0, 3, 1, 4)
    kv = jnp.broadcast_to(kv[None], (Y,) + kv.shape).reshape((Y * M,) + kv.shape[1:])
    unit = lax.all_to_all(kv, ("y", "mp"), 0, 0, tiled=True)
    own = gather_z(unit.reshape((Y, M) + unit.shape[1:]))
    sib = [swap(u) for u in own]
    attended, grad_query, gown, gsoon, glate = attend(
        block_images, block_reads, pos, query, output_gradient, own, sib
    )
    soon = swap(gsoon)
    late = swap(lax.optimization_barrier((glate, soon))[0])
    total = reduce_z(gown, soon, late)
    total = total.reshape((Y * M,) + total.shape[2:])
    total = lax.all_to_all(total, ("y", "mp"), 0, 0, tiled=True)
    total = jnp.sum(total.reshape((Y, M) + total.shape[1:]).astype(f32), axis=0)
    grad_kv = total.transpose(1, 3, 0, 2, 4).reshape(image_key_values.shape)
    return attended, grad_query, grad_kv


def solution(mesh):
    fine = Mesh(np.asarray(mesh.devices).reshape(Y, Z, 2, M), SEQ + ("mp",))
    placed = (
        P(SEQ, "mp"),
        P(None, SEQ, "mp", None),
        P(SEQ),
        P(SEQ, None),
        P(SEQ),
        P(SEQ, "mp"),
    )
    return jax.shard_map(
        local,
        mesh=fine,
        in_specs=placed,
        out_specs=(P(SEQ, "mp"), P(SEQ, "mp"), P(None, SEQ, "mp", None)),
        check_vma=False,
    )
```

time: 126 us -> 118 us (0.937)
  waiting for transfers between devices: 51.8 us -> 46.1 us
  Pallas kernels: 13.8 us -> 9.43 us
    ppermute x18 -> x20, waiting for transfers between devices: 51.8 us -> 46.1 us  [shift(): return lax.ppermute(x, axis, [(i, (i + by) % size) for i in range(size)])]
    pallas_call x1, Pallas kernels: 13.8 us -> 9.43 us  [attend(): pl.pallas_call(attend_kernel, grid=(blocks,), in_specs=[smem] * 3 + [text...]
    ppermute x18 -> x20, starting transfers between devices: 27.2 us -> 28.4 us  [shift(): return lax.ppermute(x, axis, [(i, (i + by) % size) for i in range(size)])]
    unnamed x14 -> x12, local copies, waits for them, and re-layouts: 1.44 us -> 2.58 us
  transfers between devices with their start and end apart: 18 -> 20, of which waited for: 11 -> 13; matrix products, arithmetic and copies ran while one was open for 0% -> 1% of each run, Pallas kernels for 0% -> 0%
where the time goes in v2:
time: 118 us
  waiting for transfers between devices  46.1 us (39%)
  starting transfers between devices  28.4 us (24%)
  blocking collectives  26.2 us (22%)
  Pallas kernels  9.43 us (8%)
  local copies, waits for them, and re-layouts  4.4 us (4%)
  between operations  1.54 us (1%)
  other arithmetic  1.5 us (1%)
    ppermute x20, waiting for transfers between devices, shift(): return lax.ppermute(x, axis, [(i, (i + by) % size) for i in range(size)])  46.1 us
    ppermute x20, starting transfers between devices, shift(): return lax.ppermute(x, axis, [(i, (i + by) % size) for i in range(size)])  28.4 us
    all_to_all x1, blocking collectives, local(): unit = lax.all_to_all(kv, ('y', 'mp'), 0, 0, tiled=True)  14.6 us
    all_to_all x1, blocking collectives, local(): total = lax.all_to_all(total, ('y', 'mp'), 0, 0, tiled=True)  11.6 us
    pallas_call x1, Pallas kernels, attend(): pl.pallas_call(attend_kernel, grid=(blocks,), in_specs=[smem] * 3 + [text...  9.43 us
    unnamed x12, local copies, waits for them, and re-layouts  2.58 us
  transfers between devices with their start and end apart: 20, of which 13 were waited for; matrix products, arithmetic and copies ran while one was open for 1% of the time, Pallas kernels for 0%

profile of v2, /device:TPU:2, one launch (start us, length us, event | category | flops | bytes accessed | tf_op | source)
XLA Modules:
  0.0 117.5 jit_solution(15910223992551323356)
XLA Ops:
  2.5 14.6 %all_to_all.10 = bf16[16,2,2,16,128]{4,3,2,1,0:T(8,128)(2,1)S(1)} all-to-all(bf16[16,2,2,16,128]{4,3,2,1,0:T(8,128)(2,1)S(1)} %bitcast.49), channel_id=1, replica_groups=mesh['y'=4,'z'=8,'c'=2,'mp'=4] {'y','mp'}, dimensions={0} | all-to-all | bytes 524288 | tf_op jit(solution)/shard_map/all_to_all | solution.py:224
  17.1 1.9 %collective-permute-start.2 = (bf16[4,4,2,2,16,128]{5,4,3,2,1,0:T(8,128)(2,1)S(1)}, bf16[4,4,2,2,16,128]{5,4,3,2,1,0:T(8,128)(2,1)S(1)}, u32[]{:S(2)}, u32[]{:S(2)}) collective-permute-start(bf16[4,4,2,2,16,128]{5,4,3,2,1,0:T(8,128)(2,1)S(1)} %bitcast.50), channel_id=1, source_target_pairs={{0,8},{8,16},{16,24},{24,32},{32,40},{40,48},{48,56},{56,0},{1,9},... | collective-permute-start | bytes 786440 | tf_op jit(solution)/shard_map/ppermute | solution.py:179
  19.0 3.9 %collective-permute-start = (bf16[4,4,2,2,16,128]{5,4,3,2,1,0:T(8,128)(2,1)S(1)}, bf16[4,4,2,2,16,128]{5,4,3,2,1,0:T(8,128)(2,1)S(1)}, u32[]{:S(2)}, u32[]{:S(2)}) collective-permute-start(bf16[4,4,2,2,16,128]{5,4,3,2,1,0:T(8,128)(2,1)S(1)} %bitcast.51), channel_id=1, source_target_pairs={{0,56},{8,0},{16,8},{24,16},{32,24},{40,32},{48,40},{56,48},{1,57}... | collective-permute-start | bytes 786440 | tf_op jit(solution)/shard_map/ppermute | solution.py:179
  22.9 5.2 %collective-permute-done.2 = bf16[4,4,2,2,16,128]{5,4,3,2,1,0:T(8,128)(2,1)S(1)} collective-permute-done((bf16[4,4,2,2,16,128]{5,4,3,2,1,0:T(8,128)(2,1)S(1)}, bf16[4,4,2,2,16,128]{5,4,3,2,1,0:T(8,128)(2,1)S(1)}, u32[]{:S(2)}, u32[]{:S(2)}) %collective-permute-start.2) | collective-permute-done | bytes 262176 | tf_op jit(solution)/shard_map/ppermute | solution.py:179
  28.1 3.2 %collective-permute-start.1 = (bf16[4,4,2,2,16,128]{5,4,3,2,1,0:T(8,128)(2,1)S(1)}, bf16[4,4,2,2,16,128]{5,4,3,2,1,0:T(8,128)(2,1)S(1)}, u32[]{:S(2)}, u32[]{:S(2)}) collective-permute-start(bf16[4,4,2,2,16,128]{5,4,3,2,1,0:T(8,128)(2,1)S(1)} %collective-permute-done), channel_id=1, source_target_pairs={{0,56},{8,0},{16,8},{24,16},{32,24},{40,32},{48,40},{56,48},{1,57}... | collective-permute-start | bytes 786440 | tf_op jit(solution)/shard_map/ppermute | solution.py:179
  31.4 4.3 %collective-permute-done.3 = bf16[4,4,2,2,16,128]{5,4,3,2,1,0:T(8,128)(2,1)S(1)} collective-permute-done((bf16[4,4,2,2,16,128]{5,4,3,2,1,0:T(8,128)(2,1)S(1)}, bf16[4,4,2,2,16,128]{5,4,3,2,1,0:T(8,128)(2,1)S(1)}, u32[]{:S(2)}, u32[]{:S(2)}) %collective-permute-start.3) | collective-permute-done | bytes 262176 | tf_op jit(solution)/shard_map/ppermute | solution.py:179
  35.7 3.2 %collective-permute-start.4 = (bf16[4,4,2,2,16,128]{5,4,3,2,1,0:T(8,128)(2,1)S(1)}, bf16[4,4,2,2,16,128]{5,4,3,2,1,0:T(8,128)(2,1)S(1)}, u32[]{:S(2)}, u32[]{:S(2)}) collective-permute-start(bf16[4,4,2,2,16,128]{5,4,3,2,1,0:T(8,128)(2,1)S(1)} %collective-permute-done.1), channel_id=1, source_target_pairs={{0,56},{8,0},{16,8},{24,16},{32,24},{40,32},{48,40},{56,48},{1,57}... | collective-permute-start | bytes 786440 | tf_op jit(solution)/shard_map/ppermute | solution.py:179
  39.2 4.1 %collective-permute-done.5 = bf16[4,4,2,2,16,128]{5,4,3,2,1,0:T(8,128)(2,1)S(1)} collective-permute-done((bf16[4,4,2,2,16,128]{5,4,3,2,1,0:T(8,128)(2,1)S(1)}, bf16[4,4,2,2,16,128]{5,4,3,2,1,0:T(8,128)(2,1)S(1)}, u32[]{:S(2)}, u32[]{:S(2)}) %collective-permute-start.5) | collective-permute-done | bytes 262176 | tf_op jit(solution)/shard_map/ppermute | solution.py:179
  43.4 3.3 %collective-permute-start.7 = (bf16[2,4,2,2,16,128]{5,4,3,2,1,0:T(8,128)(2,1)S(1)}, bf16[2,4,2,2,16,128]{5,4,3,2,1,0:T(8,128)(2,1)S(1)}, u32[]{:S(2)}, u32[]{:S(2)}) collective-permute-start(bf16[2,4,2,2,16,128]{5,4,3,2,1,0:T(8,128)(2,1)S(1)} %slice.107), channel_id=1, source_target_pairs={{0,56},{8,0},{16,8},{24,16},{32,24},{40,32},{48,40},{56,48},{1,57}... | collective-permute-start | bytes 393224 | tf_op jit(solution)/shard_map/ppermute | solution.py:179
  46.7 2.8 %collective-permute-done.6 = bf16[2,4,2,2,16,128]{5,4,3,2,1,0:T(8,128)(2,1)S(1)} collective-permute-done((bf16[2,4,2,2,16,128]{5,4,3,2,1,0:T(8,128)(2,1)S(1)}, bf16[2,4,2,2,16,128]{5,4,3,2,1,0:T(8,128)(2,1)S(1)}, u32[]{:S(2)}, u32[]{:S(2)}) %collective-permute-start.6) | collective-permute-done | bytes 131104 | tf_op jit(solution)/shard_map/ppermute | solution.py:179
  50.0 2.3 %collective-permute-done.9.refs_3_ = bf16[3,4,4,2,2,16,128]{6,5,4,3,2,1,0:T(8,128)(2,1)} collective-permute-done((bf16[3,4,4,2,2,16,128]{6,5,4,3,2,1,0:T(8,128)(2,1)S(1)}, bf16[3,4,4,2,2,16,128]{6,5,4,3,2,1,0:T(8,128)(2,1)}, u32[]{:S(2)}, u32[]{:S(2)}) %collective-permute-start.9) | collective-permute-done | bytes 786464 | tf_op jit(solution)/shard_map/ppermute | solution.py:179
  54.8 9.4 %shard_map.85 = (bf16[256,2048]{1,0:T(8,128)(2,1)}, bf16[256,2048]{1,0:T(8,128)(2,1)}, bf16[32,4,2,2,16,128]{5,4,3,2,1,0:T(8,128)(2,1)S(1)}, bf16[12,4,2,2,16,12...) custom-call(s32[2,6]{1,0:T(2,128)S(1)} %copy-done.2, s32[2]{0:T(128)S(1)} %copy-done.3, ...), custom_call_target="tpu_custom_call" | custom-call | flops 2415919104 | bytes 12582912 | tf_op jit(solution)/shard_map/pallas_call | solution.py:148
  64.4 2.2 %collective-permute-done.10 = bf16[12,4,2,2,16,128]{5,4,3,2,1,0:T(8,128)(2,1)S(1)} collective-permute-done((bf16[12,4,2,2,16,128]{5,4,3,2,1,0:T(8,128)(2,1)S(1)}, bf16[12,4,2,2,16,128]{5,4,3,2,1,0:T(8,128)(2,1)S(1)}, u32[]{:S(2)}, u32[]{:S(2)}) %collective-permute-start.10) | collective-permute-done | bytes 786464 | tf_op jit(solution)/shard_map/ppermute | solution.py:179
  66.9 3.4 %collective-permute-start.13 = (bf16[2,4,2,2,16,128]{5,4,3,2,1,0:T(8,128)(2,1)S(1)}, bf16[2,4,2,2,16,128]{5,4,3,2,1,0:T(8,128)(2,1)S(1)}, u32[]{:S(2)}, u32[]{:S(2)}) collective-permute-start(bf16[2,4,2,2,16,128]{5,4,3,2,1,0:T(8,128)(2,1)S(1)} %get-tuple-element.40), channel_id=1, source_target_pairs={{0,56},{8,0},{16,8},{24,16},{32,24},{40,32},{48,40},{56,48},{1,57}... | collective-permute-start | bytes 393224 | tf_op jit(solution)/shard_map/ppermute | solution.py:179
  70.3 3.3 %collective-permute-done.13 = bf16[2,4,2,2,16,128]{5,4,3,2,1,0:T(8,128)(2,1)S(1)} collective-permute-done((bf16[2,4,2,2,16,128]{5,4,3,2,1,0:T(8,128)(2,1)S(1)}, bf16[2,4,2,2,16,128]{5,4,3,2,1,0:T(8,128)(2,1)S(1)}, u32[]{:S(2)}, u32[]{:S(2)}) %collective-permute-start.13) | collective-permute-done | bytes 131104 | tf_op jit(solution)/shard_map/ppermute | solution.py:179
  73.6 3.4 %collective-permute-done.12 = bf16[2,4,2,2,16,128]{5,4,3,2,1,0:T(8,128)(2,1)S(1)} collective-permute-done((bf16[2,4,2,2,16,128]{5,4,3,2,1,0:T(8,128)(2,1)S(1)}, bf16[2,4,2,2,16,128]{5,4,3,2,1,0:T(8,128)(2,1)S(1)}, u32[]{:S(2)}, u32[]{:S(2)}) %collective-permute-start.12) | collective-permute-done | bytes 131104 | tf_op jit(solution)/shard_map/ppermute | solution.py:179
  77.2 3.3 %collective-permute-start.15 = (bf16[4,4,2,2,16,128]{5,4,3,2,1,0:T(8,128)(2,1)S(1)}, bf16[4,4,2,2,16,128]{5,4,3,2,1,0:T(8,128)(2,1)S(1)}, u32[]{:S(2)}, u32[]{:S(2)}) collective-permute-start(bf16[4,4,2,2,16,128]{5,4,3,2,1,0:T(8,128)(2,1)S(1)} %pad_maximum_fusion.2), channel_id=1, source_target_pairs={{0,56},{8,0},{16,8},{24,16},{32,24},{40,32},{48,40},{56,48},{1,57}... | collective-permute-start | bytes 786440 | tf_op jit(solution)/shard_map/ppermute | solution.py:179
  80.5 5.3 %collective-permute-done.14 = bf16[4,4,2,2,16,128]{5,4,3,2,1,0:T(8,128)(2,1)S(1)} collective-permute-done((bf16[4,4,2,2,16,128]{5,4,3,2,1,0:T(8,128)(2,1)S(1)}, bf16[4,4,2,2,16,128]{5,4,3,2,1,0:T(8,128)(2,1)S(1)}, u32[]{:S(2)}, u32[]{:S(2)}) %collective-permute-start.14) | collective-permute-done | bytes 262176 | tf_op jit(solution)/shard_map/ppermute | solution.py:179
  86.1 3.1 %collective-permute-start.17 = (bf16[4,4,2,2,16,128]{5,4,3,2,1,0:T(8,128)(2,1)S(1)}, bf16[4,4,2,2,16,128]{5,4,3,2,1,0:T(8,128)(2,1)S(1)}, u32[]{:S(2)}, u32[]{:S(2)}) collective-permute-start(bf16[4,4,2,2,16,128]{5,4,3,2,1,0:T(8,128)(2,1)S(1)} %get-tuple-element.36), channel_id=1, source_target_pairs={{0,56},{8,0},{16,8},{24,16},{32,24},{40,32},{48,40},{56,48},{1,57}... | collective-permute-start | bytes 786440 | tf_op jit(solution)/shard_map/ppermute | solution.py:179
  89.3 3.9 %collective-permute-done.17 = bf16[4,4,2,2,16,128]{5,4,3,2,1,0:T(8,128)(2,1)S(1)} collective-permute-done((bf16[4,4,2,2,16,128]{5,4,3,2,1,0:T(8,128)(2,1)S(1)}, bf16[4,4,2,2,16,128]{5,4,3,2,1,0:T(8,128)(2,1)S(1)}, u32[]{:S(2)}, u32[]{:S(2)}) %collective-permute-start.17) | collective-permute-done | bytes 262176 | tf_op jit(solution)/shard_map/ppermute | solution.py:179
  93.2 3.7 %collective-permute-done.16 = bf16[4,4,2,2,16,128]{5,4,3,2,1,0:T(8,128)(2,1)S(1)} collective-permute-done((bf16[4,4,2,2,16,128]{5,4,3,2,1,0:T(8,128)(2,1)S(1)}, bf16[4,4,2,2,16,128]{5,4,3,2,1,0:T(8,128)(2,1)S(1)}, u32[]{:S(2)}, u32[]{:S(2)}) %collective-permute-start.16) | collective-permute-done | bytes 262176 | tf_op jit(solution)/shard_map/ppermute | solution.py:179
  97.2 2.0 %collective-permute-start.18 = (bf16[4,4,2,2,16,128]{5,4,3,2,1,0:T(8,128)(2,1)S(1)}, bf16[4,4,2,2,16,128]{5,4,3,2,1,0:T(8,128)(2,1)S(1)}, u32[]{:S(2)}, u32[]{:S(2)}) collective-permute-start(bf16[4,4,2,2,16,128]{5,4,3,2,1,0:T(8,128)(2,1)S(1)} %get-tuple-element.35), channel_id=1, source_target_pairs={{0,8},{8,16},{16,24},{24,32},{32,40},{40,48},{48,56},{56,0},{1,9},... | collective-permute-start | bytes 786440 | tf_op jit(solution)/shard_map/ppermute | solution.py:179
  99.2 4.3 %collective-permute-done.19 = bf16[4,4,2,2,16,128]{5,4,3,2,1,0:T(8,128)(2,1)S(1)} collective-permute-done((bf16[4,4,2,2,16,128]{5,4,3,2,1,0:T(8,128)(2,1)S(1)}, bf16[4,4,2,2,16,128]{5,4,3,2,1,0:T(8,128)(2,1)S(1)}, u32[]{:S(2)}, u32[]{:S(2)}) %collective-permute-start.19) | collective-permute-done | bytes 262176 | tf_op jit(solution)/shard_map/ppermute | solution.py:179
  105.1 11.6 %all_to_all.11 = bf16[16,2,2,16,128]{4,3,2,1,0:T(8,128)(2,1)S(1)} all-to-all(bf16[16,2,2,16,128]{4,3,2,1,0:T(8,128)(2,1)S(1)} %bitcast.48), channel_id=1, replica_groups=mesh['y'=4,'z'=8,'c'=2,'mp'=4] {'y','mp'}, dimensions={0} | all-to-all | bytes 524288 | tf_op jit(solution)/shard_map/all_to_all | solution.py:234
  (54 shorter events, 8.1 us)
Async XLA Ops:
  17.1 11.0 %collective-permute-start.2 = (bf16[4,4,2,2,16,128]{5,4,3,2,1,0:T(8,128)(2,1)S(1)}, bf16[4,4,2,2,16,128]{5,4,3,2,1,0:T(8,128)(2,1)S(1)}, u32[]{:S(2)}, u32[]{:S(2)}) collective-permute-start(bf16[4,4,2,2,16,128]{5,4,3,2,1,0:T(8,128)(2,1)S(1)} %bitcast.50), channel_id=1, source_target_pairs={{0,8},{8,16},{16,24},{24,32},{32,40},{40,48},{48,56},{56,0},{1,9},... | collective-permute-start | bytes 786440 | tf_op jit(solution)/shard_map/ppermute | solution.py:179
  19.0 9.1 %collective-permute-start = (bf16[4,4,2,2,16,128]{5,4,3,2,1,0:T(8,128)(2,1)S(1)}, bf16[4,4,2,2,16,128]{5,4,3,2,1,0:T(8,128)(2,1)S(1)}, u32[]{:S(2)}, u32[]{:S(2)}) collective-permute-start(bf16[4,4,2,2,16,128]{5,4,3,2,1,0:T(8,128)(2,1)S(1)} %bitcast.51), channel_id=1, source_target_pairs={{0,56},{8,0},{16,8},{24,16},{32,24},{40,32},{48,40},{56,48},{1,57}... | collective-permute-start | bytes 786440 | tf_op jit(solution)/shard_map/ppermute | solution.py:179
  28.1 7.6 %collective-permute-start.3 = (bf16[4,4,2,2,16,128]{5,4,3,2,1,0:T(8,128)(2,1)S(1)}, bf16[4,4,2,2,16,128]{5,4,3,2,1,0:T(8,128)(2,1)S(1)}, u32[]{:S(2)}, u32[]{:S(2)}) collective-permute-start(bf16[4,4,2,2,16,128]{5,4,3,2,1,0:T(8,128)(2,1)S(1)} %collective-permute-done.2), channel_id=1, source_target_pairs={{0,8},{8,16},{16,24},{24,32},{32,40},{40,48},{48,56},{56,0},{1,9},... | collective-permute-start | bytes 786440 | tf_op jit(solution)/shard_map/ppermute | solution.py:179
  28.1 7.6 %collective-permute-start.1 = (bf16[4,4,2,2,16,128]{5,4,3,2,1,0:T(8,128)(2,1)S(1)}, bf16[4,4,2,2,16,128]{5,4,3,2,1,0:T(8,128)(2,1)S(1)}, u32[]{:S(2)}, u32[]{:S(2)}) collective-permute-start(bf16[4,4,2,2,16,128]{5,4,3,2,1,0:T(8,128)(2,1)S(1)} %collective-permute-done), channel_id=1, source_target_pairs={{0,56},{8,0},{16,8},{24,16},{32,24},{40,32},{48,40},{56,48},{1,57}... | collective-permute-start | bytes 786440 | tf_op jit(solution)/shard_map/ppermute | solution.py:179
  35.7 7.6 %collective-permute-start.5 = (bf16[4,4,2,2,16,128]{5,4,3,2,1,0:T(8,128)(2,1)S(1)}, bf16[4,4,2,2,16,128]{5,4,3,2,1,0:T(8,128)(2,1)S(1)}, u32[]{:S(2)}, u32[]{:S(2)}) collective-permute-start(bf16[4,4,2,2,16,128]{5,4,3,2,1,0:T(8,128)(2,1)S(1)} %collective-permute-done.3), channel_id=1, source_target_pairs={{0,8},{8,16},{16,24},{24,32},{32,40},{40,48},{48,56},{56,0},{1,9},... | collective-permute-start | bytes 786440 | tf_op jit(solution)/shard_map/ppermute | solution.py:179
  35.7 7.7 %collective-permute-start.4 = (bf16[4,4,2,2,16,128]{5,4,3,2,1,0:T(8,128)(2,1)S(1)}, bf16[4,4,2,2,16,128]{5,4,3,2,1,0:T(8,128)(2,1)S(1)}, u32[]{:S(2)}, u32[]{:S(2)}) collective-permute-start(bf16[4,4,2,2,16,128]{5,4,3,2,1,0:T(8,128)(2,1)S(1)} %collective-permute-done.1), channel_id=1, source_target_pairs={{0,56},{8,0},{16,8},{24,16},{32,24},{40,32},{48,40},{56,48},{1,57}... | collective-permute-start | bytes 786440 | tf_op jit(solution)/shard_map/ppermute | solution.py:179
  39.1 13.3 %copy-start.2 = (s32[2,6]{1,0:T(2,128)S(1)}, s32[2,6]{1,0:T(2,128)}, u32[]{:S(2)}) copy-start(s32[2,6]{1,0:T(2,128)} %images.1) | copy-start | bytes 148
  39.1 13.3 %copy-start.3 = (s32[2]{0:T(128)S(1)}, s32[2]{0:T(128)}, u32[]{:S(2)}) copy-start(s32[2]{0:T(128)} %reads.1) | copy-start | bytes 28
  39.1 13.3 %collective-permute-start.8 = (bf16[5,4,4,2,2,16,128]{6,5,4,3,2,1,0:T(8,128)(2,1)S(1)}, bf16[5,4,4,2,2,16,128]{6,5,4,3,2,1,0:T(8,128)(2,1)S(1)}, u32[]{:S(2)}, u32[]{:S(2)}) collective-permute-start(bf16[5,4,4,2,2,16,128]{6,5,4,3,2,1,0:T(8,128)(2,1)S(1)} %bitcast_dynamic-update-slice_fusion.refs_0_), channel_id=1, source_target_pairs={{0,4},{4,0},{1,5},{5,1},{2,6},{6,2},{3,7},{7,3},{8,12},{12,8},{9,1... | collective-permute-start | bytes 3932168 | tf_op jit(solution)/shard_map/ppermute | solution.py:179
  43.3 6.3 %collective-permute-start.6 = (bf16[2,4,2,2,16,128]{5,4,3,2,1,0:T(8,128)(2,1)S(1)}, bf16[2,4,2,2,16,128]{5,4,3,2,1,0:T(8,128)(2,1)S(1)}, u32[]{:S(2)}, u32[]{:S(2)}) collective-permute-start(bf16[2,4,2,2,16,128]{5,4,3,2,1,0:T(8,128)(2,1)S(1)} %slice.106), channel_id=1, source_target_pairs={{0,8},{8,16},{16,24},{24,32},{32,40},{40,48},{48,56},{56,0},{1,9},... | collective-permute-start | bytes 393224 | tf_op jit(solution)/shard_map/ppermute | solution.py:179
  43.4 6.1 %collective-permute-start.7 = (bf16[2,4,2,2,16,128]{5,4,3,2,1,0:T(8,128)(2,1)S(1)}, bf16[2,4,2,2,16,128]{5,4,3,2,1,0:T(8,128)(2,1)S(1)}, u32[]{:S(2)}, u32[]{:S(2)}) collective-permute-start(bf16[2,4,2,2,16,128]{5,4,3,2,1,0:T(8,128)(2,1)S(1)} %slice.107), channel_id=1, source_target_pairs={{0,56},{8,0},{16,8},{24,16},{32,24},{40,32},{48,40},{56,48},{1,57}... | collective-permute-start | bytes 393224 | tf_op jit(solution)/shard_map/ppermute | solution.py:179
  49.7 2.7 %collective-permute-start.9 = (bf16[3,4,4,2,2,16,128]{6,5,4,3,2,1,0:T(8,128)(2,1)S(1)}, bf16[3,4,4,2,2,16,128]{6,5,4,3,2,1,0:T(8,128)(2,1)}, u32[]{:S(2)}, u32[]{:S(2)}) collective-permute-start(bf16[3,4,4,2,2,16,128]{6,5,4,3,2,1,0:T(8,128)(2,1)S(1)} %pad_maximum_fusion.refs_1_), channel_id=1, source_target_pairs={{0,4},{4,0},{1,5},{5,1},{2,6},{6,2},{3,7},{7,3},{8,12},{12,8},{9,1... | collective-permute-start | bytes 2359304 | tf_op jit(solution)/shard_map/ppermute | solution.py:179
  52.4 1.2 %copy-start = (bf16[256,2048]{1,0:T(8,128)(2,1)S(1)}, bf16[256,2048]{1,0:T(8,128)(2,1)}, u32[]{:S(2)}) copy-start(bf16[256,2048]{1,0:T(8,128)(2,1)} %q_ref.1) | copy-start | bytes 3145732
  53.6 1.2 %copy-start.1 = (bf16[256,2048]{1,0:T(8,128)(2,1)S(1)}, bf16[256,2048]{1,0:T(8,128)(2,1)}, u32[]{:S(2)}) copy-start(bf16[256,2048]{1,0:T(8,128)(2,1)} %g_ref.1) | copy-start | bytes 3145732
  64.2 2.3 %collective-permute-start.10 = (bf16[12,4,2,2,16,128]{5,4,3,2,1,0:T(8,128)(2,1)S(1)}, bf16[12,4,2,2,16,128]{5,4,3,2,1,0:T(8,128)(2,1)S(1)}, u32[]{:S(2)}, u32[]{:S(2)}) collective-permute-start(bf16[12,4,2,2,16,128]{5,4,3,2,1,0:T(8,128)(2,1)S(1)} %get-tuple-element.21), channel_id=1, source_target_pairs={{0,4},{4,0},{1,5},{5,1},{2,6},{6,2},{3,7},{7,3},{8,12},{12,8},{9,1... | collective-permute-start | bytes 2359304 | tf_op jit(solution)/shard_map/ppermute | solution.py:179
  66.5 19.3 %collective-permute-start.11 = (bf16[20,4,2,2,16,128]{5,4,3,2,1,0:T(8,128)(2,1)S(1)}, bf16[20,4,2,2,16,128]{5,4,3,2,1,0:T(8,128)(2,1)S(1)}, u32[]{:S(2)}, u32[]{:S(2)}) collective-permute-start(bf16[20,4,2,2,16,128]{5,4,3,2,1,0:T(8,128)(2,1)S(1)} %get-tuple-element.22), channel_id=1, source_target_pairs={{0,4},{4,0},{1,5},{5,1},{2,6},{6,2},{3,7},{7,3},{8,12},{12,8},{9,1... | collective-permute-start | bytes 3932168 | tf_op jit(solution)/shard_map/ppermute | solution.py:179
  66.9 6.7 %collective-permute-start.13 = (bf16[2,4,2,2,16,128]{5,4,3,2,1,0:T(8,128)(2,1)S(1)}, bf16[2,4,2,2,16,128]{5,4,3,2,1,0:T(8,128)(2,1)S(1)}, u32[]{:S(2)}, u32[]{:S(2)}) collective-permute-start(bf16[2,4,2,2,16,128]{5,4,3,2,1,0:T(8,128)(2,1)S(1)} %get-tuple-element.40), channel_id=1, source_target_pairs={{0,56},{8,0},{16,8},{24,16},{32,24},{40,32},{48,40},{56,48},{1,57}... | collective-permute-start | bytes 393224 | tf_op jit(solution)/shard_map/ppermute | solution.py:179
  70.3 6.7 %collective-permute-start.12 = (bf16[2,4,2,2,16,128]{5,4,3,2,1,0:T(8,128)(2,1)S(1)}, bf16[2,4,2,2,16,128]{5,4,3,2,1,0:T(8,128)(2,1)S(1)}, u32[]{:S(2)}, u32[]{:S(2)}) collective-permute-start(bf16[2,4,2,2,16,128]{5,4,3,2,1,0:T(8,128)(2,1)S(1)} %get-tuple-element.41), channel_id=1, source_target_pairs={{0,8},{8,16},{16,24},{24,32},{32,40},{40,48},{48,56},{56,0},{1,9},... | collective-permute-start | bytes 393224 | tf_op jit(solution)/shard_map/ppermute | solution.py:179
  77.1 8.7 %collective-permute-start.14 = (bf16[4,4,2,2,16,128]{5,4,3,2,1,0:T(8,128)(2,1)S(1)}, bf16[4,4,2,2,16,128]{5,4,3,2,1,0:T(8,128)(2,1)S(1)}, u32[]{:S(2)}, u32[]{:S(2)}) collective-permute-start(bf16[4,4,2,2,16,128]{5,4,3,2,1,0:T(8,128)(2,1)S(1)} %pad_maximum_fusion.1), channel_id=1, source_target_pairs={{0,8},{8,16},{16,24},{24,32},{32,40},{40,48},{48,56},{56,0},{1,9},... | collective-permute-start | bytes 786440 | tf_op jit(solution)/shard_map/ppermute | solution.py:179
  77.2 8.6 %collective-permute-start.15 = (bf16[4,4,2,2,16,128]{5,4,3,2,1,0:T(8,128)(2,1)S(1)}, bf16[4,4,2,2,16,128]{5,4,3,2,1,0:T(8,128)(2,1)S(1)}, u32[]{:S(2)}, u32[]{:S(2)}) collective-permute-start(bf16[4,4,2,2,16,128]{5,4,3,2,1,0:T(8,128)(2,1)S(1)} %pad_maximum_fusion.2), channel_id=1, source_target_pairs={{0,56},{8,0},{16,8},{24,16},{32,24},{40,32},{48,40},{56,48},{1,57}... | collective-permute-start | bytes 786440 | tf_op jit(solution)/shard_map/ppermute | solution.py:179
  86.1 7.0 %collective-permute-start.17 = (bf16[4,4,2,2,16,128]{5,4,3,2,1,0:T(8,128)(2,1)S(1)}, bf16[4,4,2,2,16,128]{5,4,3,2,1,0:T(8,128)(2,1)S(1)}, u32[]{:S(2)}, u32[]{:S(2)}) collective-permute-start(bf16[4,4,2,2,16,128]{5,4,3,2,1,0:T(8,128)(2,1)S(1)} %get-tuple-element.36), channel_id=1, source_target_pairs={{0,56},{8,0},{16,8},{24,16},{32,24},{40,32},{48,40},{56,48},{1,57}... | collective-permute-start | bytes 786440 | tf_op jit(solution)/shard_map/ppermute | solution.py:179
  89.3 7.6 %collective-permute-start.16 = (bf16[4,4,2,2,16,128]{5,4,3,2,1,0:T(8,128)(2,1)S(1)}, bf16[4,4,2,2,16,128]{5,4,3,2,1,0:T(8,128)(2,1)S(1)}, u32[]{:S(2)}, u32[]{:S(2)}) collective-permute-start(bf16[4,4,2,2,16,128]{5,4,3,2,1,0:T(8,128)(2,1)S(1)} %get-tuple-element.37), channel_id=1, source_target_pairs={{0,8},{8,16},{16,24},{24,32},{32,40},{40,48},{48,56},{56,0},{1,9},... | collective-permute-start | bytes 786440 | tf_op jit(solution)/shard_map/ppermute | solution.py:179
  97.1 6.5 %collective-permute-start.19 = (bf16[4,4,2,2,16,128]{5,4,3,2,1,0:T(8,128)(2,1)S(1)}, bf16[4,4,2,2,16,128]{5,4,3,2,1,0:T(8,128)(2,1)S(1)}, u32[]{:S(2)}, u32[]{:S(2)}) collective-permute-start(bf16[4,4,2,2,16,128]{5,4,3,2,1,0:T(8,128)(2,1)S(1)} %get-tuple-element.34), channel_id=1, source_target_pairs={{0,56},{8,0},{16,8},{24,16},{32,24},{40,32},{48,40},{56,48},{1,57}... | collective-permute-start | bytes 786440 | tf_op jit(solution)/shard_map/ppermute | solution.py:179
  97.2 7.7 %collective-permute-start.18 = (bf16[4,4,2,2,16,128]{5,4,3,2,1,0:T(8,128)(2,1)S(1)}, bf16[4,4,2,2,16,128]{5,4,3,2,1,0:T(8,128)(2,1)S(1)}, u32[]{:S(2)}, u32[]{:S(2)}) collective-permute-start(bf16[4,4,2,2,16,128]{5,4,3,2,1,0:T(8,128)(2,1)S(1)} %get-tuple-element.35), channel_id=1, source_target_pairs={{0,8},{8,16},{16,24},{24,32},{32,40},{40,48},{48,56},{56,0},{1,9},... | collective-permute-start | bytes 786440 | tf_op jit(solution)/shard_map/ppermute | solution.py:179

commit v3 on v2

--- a/solution.py
+++ b/solution.py
@@ -43,7 +43,6 @@
         image = images[b, r]
         mine = (image & 1) == c
         rel = ((image >> 1) + Z - z) & (Z - 1)
-        late = (rel >= 3) & (rel < 6)
         rows = pl.ds(r * IMAGE_TOKENS, IMAGE_TOKENS)
 
         def fetch(ref, at, image=image, rows=rows, r=r):
@@ -56,11 +55,10 @@
                     bias_s[rows, :] = jnp.where(dead, DEAD, unread)
                 v_s[h, rows, :] = ref[at, image >> 4, :, 1, h].reshape(IMAGE_TOKENS, HEAD_WIDTH)
 
+        early = (rel < 3) | (rel > 5)
         for group, here in ((own, mine), (sib, jnp.logical_not(mine))):
-            soon = jnp.logical_not(late)
-            at = jnp.where(rel < 3, rel, rel - 3)
-            pl.when(here & soon)(functools.partial(fetch, group[0], at))
-            pl.when(here & late)(functools.partial(fetch, group[1], rel - 3))
+            pl.when(here & early)(functools.partial(fetch, group[0], jnp.where(rel < 3, rel, rel - 3)))
+            pl.when(here & jnp.logical_not(early))(functools.partial(fetch, group[1], rel - 3))
     for h in range(heads):
         kt_s[h] = k_s[h].T
         vt_s[h] = v_s[h].T
@@ -118,6 +116,7 @@
             image = images[block, r]
             mine = (image & 1) == c
             rel = ((image >> 1) + Z - z) & (Z - 1)
+            rel = jnp.where((z & 1) == 0, rel, Z - rel) & (Z - 1)
             row = image >> 4
             rows = pl.ds(r * IMAGE_TOKENS, IMAGE_TOKENS)
 
@@ -129,12 +128,11 @@
                     ref[at, :, 0, h] = (ref[at, :, 0, h].astype(f32) + dk).astype(bf16)
                     ref[at, :, 1, h] = (ref[at, :, 1, h].astype(f32) + dv).astype(bf16)
 
-            other = jnp.logical_not(mine)
-            late = (rel < 3) | (rel > 5)
-            at = jnp.where(rel < 3, rel, rel - 3) * Y + row
+            other, soon = jnp.logical_not(mine), rel == Z // 2
+            at = jnp.where(rel < Z // 2, rel, rel - 1) * Y + row
             pl.when(mine)(functools.partial(add, gown_ref, rel * Y + row))
-            pl.when(other & late)(functools.partial(add, glate_ref, at))
-            pl.when(other & jnp.logical_not(late))(functools.partial(add, gsoon_ref, (rel - 3) * Y + row))
+            pl.when(other & soon)(functools.partial(add, gsoon_ref, row))
+            pl.when(other & jnp.logical_not(soon))(functools.partial(add, glate_ref, at))
 
 
 def attend(images, reads, pos, query, gradient, own, sib):
@@ -154,8 +152,8 @@
             jax.ShapeDtypeStruct(query.shape, bf16),
             jax.ShapeDtypeStruct(query.shape, bf16),
             jax.ShapeDtypeStruct((Y * Z,) + unit, bf16),
-            jax.ShapeDtypeStruct((3 * Y,) + unit, bf16),
-            jax.ShapeDtypeStruct((5 * Y,) + unit, bf16),
+            jax.ShapeDtypeStruct((Y,) + unit, bf16),
+            jax.ShapeDtypeStruct(((Z - 1) * Y,) + unit, bf16),
         ],
         scratch_shapes=[
             pltpu.VMEM((heads, KEYS, HEAD_WIDTH), bf16),
@@ -172,7 +170,7 @@
         cost_estimate=pl.CostEstimate(
             flops=12 * HEAD_WIDTH * pairs, bytes_accessed=12 * 2**20, transcendentals=pairs
         ),
-    )(images, reads, pos, query, gradient, *own, *sib)
+    )(images, reads, pos, pltpu.with_memory_space_constraint(query, pltpu.HBM), pltpu.with_memory_space_constraint(gradient, pltpu.HBM), *own, *sib)
 
 
 def shift(x, axis, size, by):
@@ -197,20 +195,22 @@
     return jnp.stack([unit, down[1], down[2], up[2], up[1]]), jnp.stack([down[3], far, up[3]])
 
 
+def exchange(a, b):
+    pairs = [[(z, (z + (1 if z % 2 == n else -1)) % Z) for z in range(Z)] for n in range(2)]
+    return lax.optimization_barrier((lax.ppermute(a, "z", pairs[0]), lax.ppermute(b, "z", pairs[1])))
+
+
 def reduce_z(own, soon, late):
     half = Y // 2
-    own, soon, late = (x.reshape((-1, Y) + x.shape[1:]) for x in (own, soon, late))
-
-    def sides(a, b):
-        return lax.optimization_barrier((shift(a, "z", Z, 1), shift(b, "z", Z, -1)))
-
-    up, down = sides(add(own[4, :half], soon[1, :half]), add(own[4, half:], soon[1, half:]))
-    up = jnp.concatenate([add(own[3, :half], soon[0, :half], up), add(own[3, half:], soon[0, half:])])
-    down = jnp.concatenate([add(own[5, :half], soon[2, :half]), add(own[5, half:], soon[2, half:], down)])
-    up, down = sides(up, down)
-    up, down = sides(add(own[2], late[2], up), add(own[6], late[3], down))
-    up, down = sides(add(own[1], late[1], up), add(own[7], late[4], down))
-    return add(own[0], late[0], up, down)
+    own, late = (x.reshape((-1, Y) + x.shape[1:]) for x in (own, late))
+    a, b = exchange(add(own[4, :half], soon[:half]), add(own[4, half:], soon[half:]))
+    a, b = exchange(
+        jnp.concatenate([add(own[3, :half], late[3, :half]), add(own[3, half:], late[3, half:], b)]),
+        jnp.concatenate([add(own[5, :half], late[4, :half], a), add(own[5, half:], late[4, half:])]),
+    )
+    a, b = exchange(add(own[2], late[2], b), add(own[6], late[5], a))
+    a, b = exchange(add(own[1], late[1], b), add(own[7], late[6], a))
+    return add(own[0], late[0], a, b)
 
 
 def local(query, image_key_values, image_count, block_images, block_reads, output_gradient):

time: 118 us -> 112 us (0.949)
  local copies, waits for them, and re-layouts: 4.4 us -> 1.96 us
  waiting for transfers between devices: 46.1 us -> 43.8 us
  starting transfers between devices: 28.4 us -> 26.8 us
    ppermute x20 -> x12, waiting for transfers between devices: 46.1 us -> 20.1 us  [shift(): return lax.ppermute(x, axis, [(i, (i + by) % size) for i in range(size)])]
    ppermute x0 -> x8, waiting for transfers between devices: none -> 23.7 us  [the longest x4 15.8 us: exchange(): lax.ppermute(b, 'z', pairs[1])]
    ppermute x20 -> x12, starting transfers between devices: 28.4 us -> 16.3 us  [shift(): return lax.ppermute(x, axis, [(i, (i + by) % size) for i in range(size)])]
    ppermute x0 -> x8, starting transfers between devices: none -> 10.5 us  [the longest x4 7.95 us: exchange(): lax.ppermute(b, 'z', pairs[1])]
    unnamed x12 -> x8, local copies, waits for them, and re-layouts: 2.58 us -> 0.14 us
  transfers between devices with their start and end apart: 20 -> 20, of which waited for: 13 -> 14; matrix products, arithmetic and copies ran while one was open for 1% -> 0% of each run, Pallas kernels for 0% -> 0%
where the time goes in v3:
time: 112 us
  waiting for transfers between devices  43.8 us (39%)
  starting transfers between devices  26.8 us (24%)
  blocking collectives  26.2 us (23%)
  Pallas kernels  9.76 us (9%)
  local copies, waits for them, and re-layouts  1.96 us (2%)
  between operations  1.51 us (1%)
  other arithmetic  1.43 us (1%)
    ppermute x12, waiting for transfers between devices, shift(): return lax.ppermute(x, axis, [(i, (i + by) % size) for i in range(size)])  20.1 us
    ppermute x12, starting transfers between devices, shift(): return lax.ppermute(x, axis, [(i, (i + by) % size) for i in range(size)])  16.3 us
    ppermute x4, waiting for transfers between devices, exchange(): lax.ppermute(b, 'z', pairs[1])  15.8 us
    all_to_all x1, blocking collectives, local(): unit = lax.all_to_all(kv, ('y', 'mp'), 0, 0, tiled=True)  14.6 us
    all_to_all x1, blocking collectives, local(): total = lax.all_to_all(total, ('y', 'mp'), 0, 0, tiled=True)  11.6 us
    pallas_call x1, Pallas kernels, attend(): pl.pallas_call(attend_kernel, grid=(blocks,), in_specs=[smem] * 3 + [text...  9.76 us
    ppermute x4, starting transfers between devices, exchange(): lax.ppermute(b, 'z', pairs[1])  7.95 us
    ppermute x4, waiting for transfers between devices, exchange(): lax.ppermute(a, 'z', pairs[0])  7.9 us
  transfers between devices with their start and end apart: 20, of which 14 were waited for; matrix products, arithmetic and copies ran while one was open for 0% of the time, Pallas kernels for 0%

profile of v3, /device:TPU:2, one launch (start us, length us, event | category | flops | bytes accessed | tf_op | source)
XLA Modules:
  0.0 111.5 jit_solution(16621210900469849617)
XLA Ops:
  2.5 14.6 %all_to_all.10 = bf16[16,2,2,16,128]{4,3,2,1,0:T(8,128)(2,1)S(1)} all-to-all(bf16[16,2,2,16,128]{4,3,2,1,0:T(8,128)(2,1)S(1)} %bitcast.58), channel_id=1, replica_groups=mesh['y'=4,'z'=8,'c'=2,'mp'=4] {'y','mp'}, dimensions={0} | all-to-all | bytes 524288 | tf_op jit(solution)/shard_map/all_to_all | solution.py:224
  17.1 1.9 %collective-permute-start.2 = (bf16[4,4,2,2,16,128]{5,4,3,2,1,0:T(8,128)(2,1)S(1)}, bf16[4,4,2,2,16,128]{5,4,3,2,1,0:T(8,128)(2,1)S(1)}, u32[]{:S(2)}, u32[]{:S(2)}) collective-permute-start(bf16[4,4,2,2,16,128]{5,4,3,2,1,0:T(8,128)(2,1)S(1)} %bitcast.59), channel_id=1, source_target_pairs={{0,8},{8,16},{16,24},{24,32},{32,40},{40,48},{48,56},{56,0},{1,9},... | collective-permute-start | bytes 786440 | tf_op jit(solution)/shard_map/ppermute | solution.py:177
  19.0 3.9 %collective-permute-start = (bf16[4,4,2,2,16,128]{5,4,3,2,1,0:T(8,128)(2,1)S(1)}, bf16[4,4,2,2,16,128]{5,4,3,2,1,0:T(8,128)(2,1)S(1)}, u32[]{:S(2)}, u32[]{:S(2)}) collective-permute-start(bf16[4,4,2,2,16,128]{5,4,3,2,1,0:T(8,128)(2,1)S(1)} %bitcast.60), channel_id=1, source_target_pairs={{0,56},{8,0},{16,8},{24,16},{32,24},{40,32},{48,40},{56,48},{1,57}... | collective-permute-start | bytes 786440 | tf_op jit(solution)/shard_map/ppermute | solution.py:177
  22.9 5.2 %collective-permute-done.2 = bf16[4,4,2,2,16,128]{5,4,3,2,1,0:T(8,128)(2,1)S(1)} collective-permute-done((bf16[4,4,2,2,16,128]{5,4,3,2,1,0:T(8,128)(2,1)S(1)}, bf16[4,4,2,2,16,128]{5,4,3,2,1,0:T(8,128)(2,1)S(1)}, u32[]{:S(2)}, u32[]{:S(2)}) %collective-permute-start.2) | collective-permute-done | bytes 262176 | tf_op jit(solution)/shard_map/ppermute | solution.py:177
  28.1 3.2 %collective-permute-start.1 = (bf16[4,4,2,2,16,128]{5,4,3,2,1,0:T(8,128)(2,1)S(1)}, bf16[4,4,2,2,16,128]{5,4,3,2,1,0:T(8,128)(2,1)S(1)}, u32[]{:S(2)}, u32[]{:S(2)}) collective-permute-start(bf16[4,4,2,2,16,128]{5,4,3,2,1,0:T(8,128)(2,1)S(1)} %collective-permute-done), channel_id=1, source_target_pairs={{0,56},{8,0},{16,8},{24,16},{32,24},{40,32},{48,40},{56,48},{1,57}... | collective-permute-start | bytes 786440 | tf_op jit(solution)/shard_map/ppermute | solution.py:177
  31.4 4.3 %collective-permute-done.3 = bf16[4,4,2,2,16,128]{5,4,3,2,1,0:T(8,128)(2,1)S(1)} collective-permute-done((bf16[4,4,2,2,16,128]{5,4,3,2,1,0:T(8,128)(2,1)S(1)}, bf16[4,4,2,2,16,128]{5,4,3,2,1,0:T(8,128)(2,1)S(1)}, u32[]{:S(2)}, u32[]{:S(2)}) %collective-permute-start.3) | collective-permute-done | bytes 262176 | tf_op jit(solution)/shard_map/ppermute | solution.py:177
  35.7 3.2 %collective-permute-start.4 = (bf16[4,4,2,2,16,128]{5,4,3,2,1,0:T(8,128)(2,1)S(1)}, bf16[4,4,2,2,16,128]{5,4,3,2,1,0:T(8,128)(2,1)S(1)}, u32[]{:S(2)}, u32[]{:S(2)}) collective-permute-start(bf16[4,4,2,2,16,128]{5,4,3,2,1,0:T(8,128)(2,1)S(1)} %collective-permute-done.1), channel_id=1, source_target_pairs={{0,56},{8,0},{16,8},{24,16},{32,24},{40,32},{48,40},{56,48},{1,57}... | collective-permute-start | bytes 786440 | tf_op jit(solution)/shard_map/ppermute | solution.py:177
  39.2 4.1 %collective-permute-done.5 = bf16[4,4,2,2,16,128]{5,4,3,2,1,0:T(8,128)(2,1)S(1)} collective-permute-done((bf16[4,4,2,2,16,128]{5,4,3,2,1,0:T(8,128)(2,1)S(1)}, bf16[4,4,2,2,16,128]{5,4,3,2,1,0:T(8,128)(2,1)S(1)}, u32[]{:S(2)}, u32[]{:S(2)}) %collective-permute-start.5) | collective-permute-done | bytes 262176 | tf_op jit(solution)/shard_map/ppermute | solution.py:177
  43.4 3.3 %collective-permute-start.7 = (bf16[2,4,2,2,16,128]{5,4,3,2,1,0:T(8,128)(2,1)S(1)}, bf16[2,4,2,2,16,128]{5,4,3,2,1,0:T(8,128)(2,1)S(1)}, u32[]{:S(2)}, u32[]{:S(2)}) collective-permute-start(bf16[2,4,2,2,16,128]{5,4,3,2,1,0:T(8,128)(2,1)S(1)} %slice.107), channel_id=1, source_target_pairs={{0,56},{8,0},{16,8},{24,16},{32,24},{40,32},{48,40},{56,48},{1,57}... | collective-permute-start | bytes 393224 | tf_op jit(solution)/shard_map/ppermute | solution.py:177
  46.7 2.8 %collective-permute-done.6 = bf16[2,4,2,2,16,128]{5,4,3,2,1,0:T(8,128)(2,1)S(1)} collective-permute-done((bf16[2,4,2,2,16,128]{5,4,3,2,1,0:T(8,128)(2,1)S(1)}, bf16[2,4,2,2,16,128]{5,4,3,2,1,0:T(8,128)(2,1)S(1)}, u32[]{:S(2)}, u32[]{:S(2)}) %collective-permute-start.6) | collective-permute-done | bytes 131104 | tf_op jit(solution)/shard_map/ppermute | solution.py:177
  50.0 2.3 %collective-permute-done.9.refs_3_ = bf16[3,4,4,2,2,16,128]{6,5,4,3,2,1,0:T(8,128)(2,1)} collective-permute-done((bf16[3,4,4,2,2,16,128]{6,5,4,3,2,1,0:T(8,128)(2,1)S(1)}, bf16[3,4,4,2,2,16,128]{6,5,4,3,2,1,0:T(8,128)(2,1)}, u32[]{:S(2)}, u32[]{:S(2)}) %collective-permute-start.9) | collective-permute-done | bytes 786464 | tf_op jit(solution)/shard_map/ppermute | solution.py:177
  52.4 9.8 %shard_map.85 = (bf16[256,2048]{1,0:T(8,128)(2,1)}, bf16[256,2048]{1,0:T(8,128)(2,1)}, bf16[32,4,2,2,16,128]{5,4,3,2,1,0:T(8,128)(2,1)S(1)}, bf16[4,4,2,2,16,128...) custom-call(s32[2,6]{1,0:T(2,128)S(1)} %copy-done, s32[2]{0:T(128)S(1)} %copy-done.1, s32[2]{0:T(128)S(1)} %pad_add_fusion.pos, ...), custom_call_target="tpu_custom_call" | custom-call | flops 2415919104 | bytes 12582912 | tf_op jit(solution)/shard_map/pallas_call | solution.py:146
  62.3 1.4 %collective-permute-done.10 = bf16[4,4,2,2,16,128]{5,4,3,2,1,0:T(8,128)(2,1)S(1)} collective-permute-done((bf16[4,4,2,2,16,128]{5,4,3,2,1,0:T(8,128)(2,1)S(1)}, bf16[4,4,2,2,16,128]{5,4,3,2,1,0:T(8,128)(2,1)S(1)}, u32[]{:S(2)}, u32[]{:S(2)}) %collective-permute-start.10) | collective-permute-done | bytes 262176 | tf_op jit(solution)/shard_map/ppermute | solution.py:177
  63.9 3.4 %collective-permute-start.13 = (bf16[2,4,2,2,16,128]{5,4,3,2,1,0:T(8,128)(2,1)S(1)}, bf16[2,4,2,2,16,128]{5,4,3,2,1,0:T(8,128)(2,1)S(1)}, u32[]{:S(2)}, u32[]{:S(2)}) collective-permute-start(bf16[2,4,2,2,16,128]{5,4,3,2,1,0:T(8,128)(2,1)S(1)} %get-tuple-element.42), channel_id=1, source_target_pairs={{0,56},{8,16},{16,8},{24,32},{32,24},{40,48},{48,40},{56,0},{1,57}... | collective-permute-start | bytes 393224 | tf_op jit(solution)/shard_map/ppermute | solution.py:200
  67.3 4.0 %collective-permute-done.13 = bf16[2,4,2,2,16,128]{5,4,3,2,1,0:T(8,128)(2,1)S(1)} collective-permute-done((bf16[2,4,2,2,16,128]{5,4,3,2,1,0:T(8,128)(2,1)S(1)}, bf16[2,4,2,2,16,128]{5,4,3,2,1,0:T(8,128)(2,1)S(1)}, u32[]{:S(2)}, u32[]{:S(2)}) %collective-permute-start.13) | collective-permute-done | bytes 131104 | tf_op jit(solution)/shard_map/ppermute | solution.py:200
  71.3 1.5 %collective-permute-done.12 = bf16[2,4,2,2,16,128]{5,4,3,2,1,0:T(8,128)(2,1)S(1)} collective-permute-done((bf16[2,4,2,2,16,128]{5,4,3,2,1,0:T(8,128)(2,1)S(1)}, bf16[2,4,2,2,16,128]{5,4,3,2,1,0:T(8,128)(2,1)S(1)}, u32[]{:S(2)}, u32[]{:S(2)}) %collective-permute-start.12) | collective-permute-done | bytes 131104 | tf_op jit(solution)/shard_map/ppermute | solution.py:200
  73.4 1.3 %collective-permute-start.15 = (bf16[4,4,2,2,16,128]{5,4,3,2,1,0:T(8,128)(2,1)S(1)}, bf16[4,4,2,2,16,128]{5,4,3,2,1,0:T(8,128)(2,1)S(1)}, u32[]{:S(2)}, u32[]{:S(2)}) collective-permute-start(bf16[4,4,2,2,16,128]{5,4,3,2,1,0:T(8,128)(2,1)S(1)} %pad_maximum_fusion.2), channel_id=1, source_target_pairs={{0,56},{8,16},{16,8},{24,32},{32,24},{40,48},{48,40},{56,0},{1,57}... | collective-permute-start | bytes 786440 | tf_op jit(solution)/shard_map/ppermute | solution.py:200
  74.7 5.8 %collective-permute-done.14 = bf16[4,4,2,2,16,128]{5,4,3,2,1,0:T(8,128)(2,1)S(1)} collective-permute-done((bf16[4,4,2,2,16,128]{5,4,3,2,1,0:T(8,128)(2,1)S(1)}, bf16[4,4,2,2,16,128]{5,4,3,2,1,0:T(8,128)(2,1)S(1)}, u32[]{:S(2)}, u32[]{:S(2)}) %collective-permute-start.14) | collective-permute-done | bytes 262176 | tf_op jit(solution)/shard_map/ppermute | solution.py:200
  80.6 1.6 %collective-permute-done.15 = bf16[4,4,2,2,16,128]{5,4,3,2,1,0:T(8,128)(2,1)S(1)} collective-permute-done((bf16[4,4,2,2,16,128]{5,4,3,2,1,0:T(8,128)(2,1)S(1)}, bf16[4,4,2,2,16,128]{5,4,3,2,1,0:T(8,128)(2,1)S(1)}, u32[]{:S(2)}, u32[]{:S(2)}) %collective-permute-start.15) | collective-permute-done | bytes 262176 | tf_op jit(solution)/shard_map/ppermute | solution.py:200
  82.5 1.6 %collective-permute-start.17 = (bf16[4,4,2,2,16,128]{5,4,3,2,1,0:T(8,128)(2,1)S(1)}, bf16[4,4,2,2,16,128]{5,4,3,2,1,0:T(8,128)(2,1)S(1)}, u32[]{:S(2)}, u32[]{:S(2)}) collective-permute-start(bf16[4,4,2,2,16,128]{5,4,3,2,1,0:T(8,128)(2,1)S(1)} %get-tuple-element.36), channel_id=1, source_target_pairs={{0,56},{8,16},{16,8},{24,32},{32,24},{40,48},{48,40},{56,0},{1,57}... | collective-permute-start | bytes 786440 | tf_op jit(solution)/shard_map/ppermute | solution.py:200
  85.3 5.0 %collective-permute-done.17 = bf16[4,4,2,2,16,128]{5,4,3,2,1,0:T(8,128)(2,1)S(1)} collective-permute-done((bf16[4,4,2,2,16,128]{5,4,3,2,1,0:T(8,128)(2,1)S(1)}, bf16[4,4,2,2,16,128]{5,4,3,2,1,0:T(8,128)(2,1)S(1)}, u32[]{:S(2)}, u32[]{:S(2)}) %collective-permute-start.17) | collective-permute-done | bytes 262176 | tf_op jit(solution)/shard_map/ppermute | solution.py:200
  90.9 1.6 %collective-permute-start.19 = (bf16[4,4,2,2,16,128]{5,4,3,2,1,0:T(8,128)(2,1)S(1)}, bf16[4,4,2,2,16,128]{5,4,3,2,1,0:T(8,128)(2,1)S(1)}, u32[]{:S(2)}, u32[]{:S(2)}) collective-permute-start(bf16[4,4,2,2,16,128]{5,4,3,2,1,0:T(8,128)(2,1)S(1)} %get-tuple-element.34), channel_id=1, source_target_pairs={{0,56},{8,16},{16,8},{24,32},{32,24},{40,48},{48,40},{56,0},{1,57}... | collective-permute-start | bytes 786440 | tf_op jit(solution)/shard_map/ppermute | solution.py:200
  93.4 5.1 %collective-permute-done.19 = bf16[4,4,2,2,16,128]{5,4,3,2,1,0:T(8,128)(2,1)S(1)} collective-permute-done((bf16[4,4,2,2,16,128]{5,4,3,2,1,0:T(8,128)(2,1)S(1)}, bf16[4,4,2,2,16,128]{5,4,3,2,1,0:T(8,128)(2,1)S(1)}, u32[]{:S(2)}, u32[]{:S(2)}) %collective-permute-start.19) | collective-permute-done | bytes 262176 | tf_op jit(solution)/shard_map/ppermute | solution.py:200
  99.0 11.6 %all_to_all.11 = bf16[16,2,2,16,128]{4,3,2,1,0:T(8,128)(2,1)S(1)} all-to-all(bf16[16,2,2,16,128]{4,3,2,1,0:T(8,128)(2,1)S(1)} %bitcast.57), channel_id=1, replica_groups=mesh['y'=4,'z'=8,'c'=2,'mp'=4] {'y','mp'}, dimensions={0} | all-to-all | bytes 524288 | tf_op jit(solution)/shard_map/all_to_all | solution.py:234
  (51 shorter events, 7.3 us)
Async XLA Ops:
  17.1 11.0 %collective-permute-start.2 = (bf16[4,4,2,2,16,128]{5,4,3,2,1,0:T(8,128)(2,1)S(1)}, bf16[4,4,2,2,16,128]{5,4,3,2,1,0:T(8,128)(2,1)S(1)}, u32[]{:S(2)}, u32[]{:S(2)}) collective-permute-start(bf16[4,4,2,2,16,128]{5,4,3,2,1,0:T(8,128)(2,1)S(1)} %bitcast.59), channel_id=1, source_target_pairs={{0,8},{8,16},{16,24},{24,32},{32,40},{40,48},{48,56},{56,0},{1,9},... | collective-permute-start | bytes 786440 | tf_op jit(solution)/shard_map/ppermute | solution.py:177
  19.0 9.1 %collective-permute-start = (bf16[4,4,2,2,16,128]{5,4,3,2,1,0:T(8,128)(2,1)S(1)}, bf16[4,4,2,2,16,128]{5,4,3,2,1,0:T(8,128)(2,1)S(1)}, u32[]{:S(2)}, u32[]{:S(2)}) collective-permute-start(bf16[4,4,2,2,16,128]{5,4,3,2,1,0:T(8,128)(2,1)S(1)} %bitcast.60), channel_id=1, source_target_pairs={{0,56},{8,0},{16,8},{24,16},{32,24},{40,32},{48,40},{56,48},{1,57}... | collective-permute-start | bytes 786440 | tf_op jit(solution)/shard_map/ppermute | solution.py:177
  28.1 7.6 %collective-permute-start.3 = (bf16[4,4,2,2,16,128]{5,4,3,2,1,0:T(8,128)(2,1)S(1)}, bf16[4,4,2,2,16,128]{5,4,3,2,1,0:T(8,128)(2,1)S(1)}, u32[]{:S(2)}, u32[]{:S(2)}) collective-permute-start(bf16[4,4,2,2,16,128]{5,4,3,2,1,0:T(8,128)(2,1)S(1)} %collective-permute-done.2), channel_id=1, source_target_pairs={{0,8},{8,16},{16,24},{24,32},{32,40},{40,48},{48,56},{56,0},{1,9},... | collective-permute-start | bytes 786440 | tf_op jit(solution)/shard_map/ppermute | solution.py:177
  28.1 7.6 %collective-permute-start.1 = (bf16[4,4,2,2,16,128]{5,4,3,2,1,0:T(8,128)(2,1)S(1)}, bf16[4,4,2,2,16,128]{5,4,3,2,1,0:T(8,128)(2,1)S(1)}, u32[]{:S(2)}, u32[]{:S(2)}) collective-permute-start(bf16[4,4,2,2,16,128]{5,4,3,2,1,0:T(8,128)(2,1)S(1)} %collective-permute-done), channel_id=1, source_target_pairs={{0,56},{8,0},{16,8},{24,16},{32,24},{40,32},{48,40},{56,48},{1,57}... | collective-permute-start | bytes 786440 | tf_op jit(solution)/shard_map/ppermute | solution.py:177
  35.7 7.6 %collective-permute-start.5 = (bf16[4,4,2,2,16,128]{5,4,3,2,1,0:T(8,128)(2,1)S(1)}, bf16[4,4,2,2,16,128]{5,4,3,2,1,0:T(8,128)(2,1)S(1)}, u32[]{:S(2)}, u32[]{:S(2)}) collective-permute-start(bf16[4,4,2,2,16,128]{5,4,3,2,1,0:T(8,128)(2,1)S(1)} %collective-permute-done.3), channel_id=1, source_target_pairs={{0,8},{8,16},{16,24},{24,32},{32,40},{40,48},{48,56},{56,0},{1,9},... | collective-permute-start | bytes 786440 | tf_op jit(solution)/shard_map/ppermute | solution.py:177
  35.7 7.7 %collective-permute-start.4 = (bf16[4,4,2,2,16,128]{5,4,3,2,1,0:T(8,128)(2,1)S(1)}, bf16[4,4,2,2,16,128]{5,4,3,2,1,0:T(8,128)(2,1)S(1)}, u32[]{:S(2)}, u32[]{:S(2)}) collective-permute-start(bf16[4,4,2,2,16,128]{5,4,3,2,1,0:T(8,128)(2,1)S(1)} %collective-permute-done.1), channel_id=1, source_target_pairs={{0,56},{8,0},{16,8},{24,16},{32,24},{40,32},{48,40},{56,48},{1,57}... | collective-permute-start | bytes 786440 | tf_op jit(solution)/shard_map/ppermute | solution.py:177
  39.1 13.3 %copy-start = (s32[2,6]{1,0:T(2,128)S(1)}, s32[2,6]{1,0:T(2,128)}, u32[]{:S(2)}) copy-start(s32[2,6]{1,0:T(2,128)} %images.1) | copy-start | bytes 148
  39.1 13.3 %copy-start.1 = (s32[2]{0:T(128)S(1)}, s32[2]{0:T(128)}, u32[]{:S(2)}) copy-start(s32[2]{0:T(128)} %reads.1) | copy-start | bytes 28
  39.1 13.3 %collective-permute-start.8 = (bf16[5,4,4,2,2,16,128]{6,5,4,3,2,1,0:T(8,128)(2,1)S(1)}, bf16[5,4,4,2,2,16,128]{6,5,4,3,2,1,0:T(8,128)(2,1)S(1)}, u32[]{:S(2)}, u32[]{:S(2)}) collective-permute-start(bf16[5,4,4,2,2,16,128]{6,5,4,3,2,1,0:T(8,128)(2,1)S(1)} %bitcast_dynamic-update-slice_fusion.refs_0_), channel_id=1, source_target_pairs={{0,4},{4,0},{1,5},{5,1},{2,6},{6,2},{3,7},{7,3},{8,12},{12,8},{9,1... | collective-permute-start | bytes 3932168 | tf_op jit(solution)/shard_map/ppermute | solution.py:177
  43.3 6.3 %collective-permute-start.6 = (bf16[2,4,2,2,16,128]{5,4,3,2,1,0:T(8,128)(2,1)S(1)}, bf16[2,4,2,2,16,128]{5,4,3,2,1,0:T(8,128)(2,1)S(1)}, u32[]{:S(2)}, u32[]{:S(2)}) collective-permute-start(bf16[2,4,2,2,16,128]{5,4,3,2,1,0:T(8,128)(2,1)S(1)} %slice.106), channel_id=1, source_target_pairs={{0,8},{8,16},{16,24},{24,32},{32,40},{40,48},{48,56},{56,0},{1,9},... | collective-permute-start | bytes 393224 | tf_op jit(solution)/shard_map/ppermute | solution.py:177
  43.4 6.1 %collective-permute-start.7 = (bf16[2,4,2,2,16,128]{5,4,3,2,1,0:T(8,128)(2,1)S(1)}, bf16[2,4,2,2,16,128]{5,4,3,2,1,0:T(8,128)(2,1)S(1)}, u32[]{:S(2)}, u32[]{:S(2)}) collective-permute-start(bf16[2,4,2,2,16,128]{5,4,3,2,1,0:T(8,128)(2,1)S(1)} %slice.107), channel_id=1, source_target_pairs={{0,56},{8,0},{16,8},{24,16},{32,24},{40,32},{48,40},{56,48},{1,57}... | collective-permute-start | bytes 393224 | tf_op jit(solution)/shard_map/ppermute | solution.py:177
  49.7 2.7 %collective-permute-start.9 = (bf16[3,4,4,2,2,16,128]{6,5,4,3,2,1,0:T(8,128)(2,1)S(1)}, bf16[3,4,4,2,2,16,128]{6,5,4,3,2,1,0:T(8,128)(2,1)}, u32[]{:S(2)}, u32[]{:S(2)}) collective-permute-start(bf16[3,4,4,2,2,16,128]{6,5,4,3,2,1,0:T(8,128)(2,1)S(1)} %pad_maximum_fusion.refs_1_), channel_id=1, source_target_pairs={{0,4},{4,0},{1,5},{5,1},{2,6},{6,2},{3,7},{7,3},{8,12},{12,8},{9,1... | collective-permute-start | bytes 2359304 | tf_op jit(solution)/shard_map/ppermute | solution.py:177
  62.1 1.5 %collective-permute-start.10 = (bf16[4,4,2,2,16,128]{5,4,3,2,1,0:T(8,128)(2,1)S(1)}, bf16[4,4,2,2,16,128]{5,4,3,2,1,0:T(8,128)(2,1)S(1)}, u32[]{:S(2)}, u32[]{:S(2)}) collective-permute-start(bf16[4,4,2,2,16,128]{5,4,3,2,1,0:T(8,128)(2,1)S(1)} %get-tuple-element.21), channel_id=1, source_target_pairs={{0,4},{4,0},{1,5},{5,1},{2,6},{6,2},{3,7},{7,3},{8,12},{12,8},{9,1... | collective-permute-start | bytes 786440 | tf_op jit(solution)/shard_map/ppermute | solution.py:177
  63.7 9.1 %collective-permute-start.11 = (bf16[28,4,2,2,16,128]{5,4,3,2,1,0:T(8,128)(2,1)S(1)}, bf16[28,4,2,2,16,128]{5,4,3,2,1,0:T(8,128)(2,1)S(1)}, u32[]{:S(2)}, u32[]{:S(2)}) collective-permute-start(bf16[28,4,2,2,16,128]{5,4,3,2,1,0:T(8,128)(2,1)S(1)} %get-tuple-element.22), channel_id=1, source_target_pairs={{0,4},{4,0},{1,5},{5,1},{2,6},{6,2},{3,7},{7,3},{8,12},{12,8},{9,1... | collective-permute-start | bytes 5505032 | tf_op jit(solution)/shard_map/ppermute | solution.py:177
  63.9 7.4 %collective-permute-start.13 = (bf16[2,4,2,2,16,128]{5,4,3,2,1,0:T(8,128)(2,1)S(1)}, bf16[2,4,2,2,16,128]{5,4,3,2,1,0:T(8,128)(2,1)S(1)}, u32[]{:S(2)}, u32[]{:S(2)}) collective-permute-start(bf16[2,4,2,2,16,128]{5,4,3,2,1,0:T(8,128)(2,1)S(1)} %get-tuple-element.42), channel_id=1, source_target_pairs={{0,56},{8,16},{16,8},{24,32},{32,24},{40,48},{48,40},{56,0},{1,57}... | collective-permute-start | bytes 393224 | tf_op jit(solution)/shard_map/ppermute | solution.py:200
  67.3 5.5 %collective-permute-start.12 = (bf16[2,4,2,2,16,128]{5,4,3,2,1,0:T(8,128)(2,1)S(1)}, bf16[2,4,2,2,16,128]{5,4,3,2,1,0:T(8,128)(2,1)S(1)}, u32[]{:S(2)}, u32[]{:S(2)}) collective-permute-start(bf16[2,4,2,2,16,128]{5,4,3,2,1,0:T(8,128)(2,1)S(1)} %get-tuple-element.43), channel_id=1, source_target_pairs={{0,8},{8,0},{16,24},{24,16},{32,40},{40,32},{48,56},{56,48},{1,9},... | collective-permute-start | bytes 393224 | tf_op jit(solution)/shard_map/ppermute | solution.py:200
  73.0 7.5 %collective-permute-start.14 = (bf16[4,4,2,2,16,128]{5,4,3,2,1,0:T(8,128)(2,1)S(1)}, bf16[4,4,2,2,16,128]{5,4,3,2,1,0:T(8,128)(2,1)S(1)}, u32[]{:S(2)}, u32[]{:S(2)}) collective-permute-start(bf16[4,4,2,2,16,128]{5,4,3,2,1,0:T(8,128)(2,1)S(1)} %pad_maximum_fusion.1), channel_id=1, source_target_pairs={{0,8},{8,0},{16,24},{24,16},{32,40},{40,32},{48,56},{56,48},{1,9},... | collective-permute-start | bytes 786440 | tf_op jit(solution)/shard_map/ppermute | solution.py:200
  73.4 8.8 %collective-permute-start.15 = (bf16[4,4,2,2,16,128]{5,4,3,2,1,0:T(8,128)(2,1)S(1)}, bf16[4,4,2,2,16,128]{5,4,3,2,1,0:T(8,128)(2,1)S(1)}, u32[]{:S(2)}, u32[]{:S(2)}) collective-permute-start(bf16[4,4,2,2,16,128]{5,4,3,2,1,0:T(8,128)(2,1)S(1)} %pad_maximum_fusion.2), channel_id=1, source_target_pairs={{0,56},{8,16},{16,8},{24,32},{32,24},{40,48},{48,40},{56,0},{1,57}... | collective-permute-start | bytes 786440 | tf_op jit(solution)/shard_map/ppermute | solution.py:200
  82.5 7.9 %collective-permute-start.17 = (bf16[4,4,2,2,16,128]{5,4,3,2,1,0:T(8,128)(2,1)S(1)}, bf16[4,4,2,2,16,128]{5,4,3,2,1,0:T(8,128)(2,1)S(1)}, u32[]{:S(2)}, u32[]{:S(2)}) collective-permute-start(bf16[4,4,2,2,16,128]{5,4,3,2,1,0:T(8,128)(2,1)S(1)} %get-tuple-element.36), channel_id=1, source_target_pairs={{0,56},{8,16},{16,8},{24,32},{32,24},{40,48},{48,40},{56,0},{1,57}... | collective-permute-start | bytes 786440 | tf_op jit(solution)/shard_map/ppermute | solution.py:200
  84.0 6.6 %collective-permute-start.16 = (bf16[4,4,2,2,16,128]{5,4,3,2,1,0:T(8,128)(2,1)S(1)}, bf16[4,4,2,2,16,128]{5,4,3,2,1,0:T(8,128)(2,1)S(1)}, u32[]{:S(2)}, u32[]{:S(2)}) collective-permute-start(bf16[4,4,2,2,16,128]{5,4,3,2,1,0:T(8,128)(2,1)S(1)} %get-tuple-element.37), channel_id=1, source_target_pairs={{0,8},{8,0},{16,24},{24,16},{32,40},{40,32},{48,56},{56,48},{1,9},... | collective-permute-start | bytes 786440 | tf_op jit(solution)/shard_map/ppermute | solution.py:200
  90.9 7.7 %collective-permute-start.19 = (bf16[4,4,2,2,16,128]{5,4,3,2,1,0:T(8,128)(2,1)S(1)}, bf16[4,4,2,2,16,128]{5,4,3,2,1,0:T(8,128)(2,1)S(1)}, u32[]{:S(2)}, u32[]{:S(2)}) collective-permute-start(bf16[4,4,2,2,16,128]{5,4,3,2,1,0:T(8,128)(2,1)S(1)} %get-tuple-element.34), channel_id=1, source_target_pairs={{0,56},{8,16},{16,8},{24,32},{32,24},{40,48},{48,40},{56,0},{1,57}... | collective-permute-start | bytes 786440 | tf_op jit(solution)/shard_map/ppermute | solution.py:200
  92.5 6.4 %collective-permute-start.18 = (bf16[4,4,2,2,16,128]{5,4,3,2,1,0:T(8,128)(2,1)S(1)}, bf16[4,4,2,2,16,128]{5,4,3,2,1,0:T(8,128)(2,1)S(1)}, u32[]{:S(2)}, u32[]{:S(2)}) collective-permute-start(bf16[4,4,2,2,16,128]{5,4,3,2,1,0:T(8,128)(2,1)S(1)} %get-tuple-element.35), channel_id=1, source_target_pairs={{0,8},{8,0},{16,24},{24,16},{32,40},{40,32},{48,56},{56,48},{1,9},... | collective-permute-start | bytes 786440 | tf_op jit(solution)/shard_map/ppermute | solution.py:200

commit v4 on v3

--- a/solution.py
+++ b/solution.py
@@ -219,7 +219,8 @@
     slot = lax.axis_index("mp") * slots + jnp.arange(slots, dtype=jnp.int32)
     dead = (slot >= image_count[0])[None, :, None] & (jnp.arange(2) == 0)[:, None, None]
     kv = jnp.where(dead, MARKER, image_key_values[:, 0]).astype(bf16)
-    kv = kv.reshape(2, slots, M, 2, HEAD_WIDTH).transpose(2, 0, 3, 1, 4)
+    kv = jnp.stack([kv[:, :, n * HEAD_WIDTH : (n + 1) * HEAD_WIDTH] for n in range(2 * M)])
+    kv = kv.reshape((M, 2) + kv.shape[1:]).swapaxes(1, 2)
     kv = jnp.broadcast_to(kv[None], (Y,) + kv.shape).reshape((Y * M,) + kv.shape[1:])
     unit = lax.all_to_all(kv, ("y", "mp"), 0, 0, tiled=True)
     own = gather_z(unit.reshape((Y, M) + unit.shape[1:]))
@@ -233,7 +234,8 @@
     total = total.reshape((Y * M,) + total.shape[2:])
     total = lax.all_to_all(total, ("y", "mp"), 0, 0, tiled=True)
     total = jnp.sum(total.reshape((Y, M) + total.shape[1:]).astype(f32), axis=0)
-    grad_kv = total.transpose(1, 3, 0, 2, 4).reshape(image_key_values.shape)
+    grad_kv = jnp.concatenate([total[n // 2, :, n % 2] for n in range(2 * M)], axis=-1)
+    grad_kv = grad_kv.reshape(image_key_values.shape)
     return attended, grad_query, grad_kv
 
 

time: 112 us -> 112 us (level)
  no operation moved by 1% of the time
where the time goes in v4:
time: 112 us; the launch traced here: 111 us
  waiting for transfers between devices  43.8 us (39%)
  starting transfers between devices  26.8 us (24%)
  blocking collectives  26.2 us (23%)
  Pallas kernels  9.75 us (9%)
  other arithmetic  2.21 us (2%)
  between operations  1.6 us (1%)
    ppermute x12, waiting for transfers between devices, shift(): return lax.ppermute(x, axis, [(i, (i + by) % size) for i in range(size)])  20.1 us
    ppermute x12, starting transfers between devices, shift(): return lax.ppermute(x, axis, [(i, (i + by) % size) for i in range(size)])  16.3 us
    ppermute x4, waiting for transfers between devices, exchange(): lax.ppermute(b, 'z', pairs[1])  15.8 us
    all_to_all x1, blocking collectives, local(): unit = lax.all_to_all(kv, ('y', 'mp'), 0, 0, tiled=True)  14.6 us
    all_to_all x1, blocking collectives, local(): total = lax.all_to_all(total, ('y', 'mp'), 0, 0, tiled=True)  11.6 us
    pallas_call x1, Pallas kernels, attend(): pl.pallas_call(attend_kernel, grid=(blocks,), in_specs=[smem] * 3 + [text...  9.75 us
    ppermute x4, starting transfers between devices, exchange(): lax.ppermute(b, 'z', pairs[1])  7.95 us
    ppermute x4, waiting for transfers between devices, exchange(): lax.ppermute(a, 'z', pairs[0])  7.9 us
  transfers between devices with their start and end apart: 20, of which 14 were waited for; matrix products, arithmetic and copies ran while one was open for 0% of the time, Pallas kernels for 0%

profile of v4, /device:TPU:2, one launch (start us, length us, event | category | flops | bytes accessed | tf_op | source)
XLA Modules:
  0.0 111.4 jit_solution(5412057379524540519)
XLA Ops:
  2.5 14.6 %all_to_all.10 = bf16[16,2,2,16,128]{4,3,2,1,0:T(8,128)(2,1)S(1)} all-to-all(bf16[16,2,2,16,128]{4,3,2,1,0:T(8,128)(2,1)S(1)} %bitcast.138), channel_id=1, replica_groups=mesh['y'=4,'z'=8,'c'=2,'mp'=4] {'y','mp'}, dimensions={0} | all-to-all | bytes 524288 | tf_op jit(solution)/shard_map/all_to_all | solution.py:225
  17.1 1.9 %collective-permute-start.2 = (bf16[4,4,2,2,16,128]{5,4,3,2,1,0:T(8,128)(2,1)S(1)}, bf16[4,4,2,2,16,128]{5,4,3,2,1,0:T(8,128)(2,1)S(1)}, u32[]{:S(2)}, u32[]{:S(2)}) collective-permute-start(bf16[4,4,2,2,16,128]{5,4,3,2,1,0:T(8,128)(2,1)S(1)} %bitcast.139), channel_id=1, source_target_pairs={{0,8},{8,16},{16,24},{24,32},{32,40},{40,48},{48,56},{56,0},{1,9},... | collective-permute-start | bytes 786440 | tf_op jit(solution)/shard_map/ppermute | solution.py:177
  19.0 3.9 %collective-permute-start = (bf16[4,4,2,2,16,128]{5,4,3,2,1,0:T(8,128)(2,1)S(1)}, bf16[4,4,2,2,16,128]{5,4,3,2,1,0:T(8,128)(2,1)S(1)}, u32[]{:S(2)}, u32[]{:S(2)}) collective-permute-start(bf16[4,4,2,2,16,128]{5,4,3,2,1,0:T(8,128)(2,1)S(1)} %bitcast.140), channel_id=1, source_target_pairs={{0,56},{8,0},{16,8},{24,16},{32,24},{40,32},{48,40},{56,48},{1,57}... | collective-permute-start | bytes 786440 | tf_op jit(solution)/shard_map/ppermute | solution.py:177
  22.9 5.2 %collective-permute-done.2 = bf16[4,4,2,2,16,128]{5,4,3,2,1,0:T(8,128)(2,1)S(1)} collective-permute-done((bf16[4,4,2,2,16,128]{5,4,3,2,1,0:T(8,128)(2,1)S(1)}, bf16[4,4,2,2,16,128]{5,4,3,2,1,0:T(8,128)(2,1)S(1)}, u32[]{:S(2)}, u32[]{:S(2)}) %collective-permute-start.2) | collective-permute-done | bytes 262176 | tf_op jit(solution)/shard_map/ppermute | solution.py:177
  28.1 3.2 %collective-permute-start.1 = (bf16[4,4,2,2,16,128]{5,4,3,2,1,0:T(8,128)(2,1)S(1)}, bf16[4,4,2,2,16,128]{5,4,3,2,1,0:T(8,128)(2,1)S(1)}, u32[]{:S(2)}, u32[]{:S(2)}) collective-permute-start(bf16[4,4,2,2,16,128]{5,4,3,2,1,0:T(8,128)(2,1)S(1)} %collective-permute-done), channel_id=1, source_target_pairs={{0,56},{8,0},{16,8},{24,16},{32,24},{40,32},{48,40},{56,48},{1,57}... | collective-permute-start | bytes 786440 | tf_op jit(solution)/shard_map/ppermute | solution.py:177
  31.4 4.3 %collective-permute-done.3 = bf16[4,4,2,2,16,128]{5,4,3,2,1,0:T(8,128)(2,1)S(1)} collective-permute-done((bf16[4,4,2,2,16,128]{5,4,3,2,1,0:T(8,128)(2,1)S(1)}, bf16[4,4,2,2,16,128]{5,4,3,2,1,0:T(8,128)(2,1)S(1)}, u32[]{:S(2)}, u32[]{:S(2)}) %collective-permute-start.3) | collective-permute-done | bytes 262176 | tf_op jit(solution)/shard_map/ppermute | solution.py:177
  35.7 3.2 %collective-permute-start.4 = (bf16[4,4,2,2,16,128]{5,4,3,2,1,0:T(8,128)(2,1)S(1)}, bf16[4,4,2,2,16,128]{5,4,3,2,1,0:T(8,128)(2,1)S(1)}, u32[]{:S(2)}, u32[]{:S(2)}) collective-permute-start(bf16[4,4,2,2,16,128]{5,4,3,2,1,0:T(8,128)(2,1)S(1)} %collective-permute-done.1), channel_id=1, source_target_pairs={{0,56},{8,0},{16,8},{24,16},{32,24},{40,32},{48,40},{56,48},{1,57}... | collective-permute-start | bytes 786440 | tf_op jit(solution)/shard_map/ppermute | solution.py:177
  39.2 4.1 %collective-permute-done.5 = bf16[4,4,2,2,16,128]{5,4,3,2,1,0:T(8,128)(2,1)S(1)} collective-permute-done((bf16[4,4,2,2,16,128]{5,4,3,2,1,0:T(8,128)(2,1)S(1)}, bf16[4,4,2,2,16,128]{5,4,3,2,1,0:T(8,128)(2,1)S(1)}, u32[]{:S(2)}, u32[]{:S(2)}) %collective-permute-start.5) | collective-permute-done | bytes 262176 | tf_op jit(solution)/shard_map/ppermute | solution.py:177
  43.4 3.3 %collective-permute-start.7 = (bf16[2,4,2,2,16,128]{5,4,3,2,1,0:T(8,128)(2,1)S(1)}, bf16[2,4,2,2,16,128]{5,4,3,2,1,0:T(8,128)(2,1)S(1)}, u32[]{:S(2)}, u32[]{:S(2)}) collective-permute-start(bf16[2,4,2,2,16,128]{5,4,3,2,1,0:T(8,128)(2,1)S(1)} %slice.179), channel_id=1, source_target_pairs={{0,56},{8,0},{16,8},{24,16},{32,24},{40,32},{48,40},{56,48},{1,57}... | collective-permute-start | bytes 393224 | tf_op jit(solution)/shard_map/ppermute | solution.py:177
  46.7 2.8 %collective-permute-done.6 = bf16[2,4,2,2,16,128]{5,4,3,2,1,0:T(8,128)(2,1)S(1)} collective-permute-done((bf16[2,4,2,2,16,128]{5,4,3,2,1,0:T(8,128)(2,1)S(1)}, bf16[2,4,2,2,16,128]{5,4,3,2,1,0:T(8,128)(2,1)S(1)}, u32[]{:S(2)}, u32[]{:S(2)}) %collective-permute-start.6) | collective-permute-done | bytes 131104 | tf_op jit(solution)/shard_map/ppermute | solution.py:177
  50.0 2.3 %collective-permute-done.9.refs_3_ = bf16[3,4,4,2,2,16,128]{6,5,4,3,2,1,0:T(8,128)(2,1)} collective-permute-done((bf16[3,4,4,2,2,16,128]{6,5,4,3,2,1,0:T(8,128)(2,1)S(1)}, bf16[3,4,4,2,2,16,128]{6,5,4,3,2,1,0:T(8,128)(2,1)}, u32[]{:S(2)}, u32[]{:S(2)}) %collective-permute-start.9) | collective-permute-done | bytes 786464 | tf_op jit(solution)/shard_map/ppermute | solution.py:177
  52.4 9.8 %shard_map.85 = (bf16[256,2048]{1,0:T(8,128)(2,1)}, bf16[256,2048]{1,0:T(8,128)(2,1)}, bf16[32,4,2,2,16,128]{5,4,3,2,1,0:T(8,128)(2,1)S(1)}, bf16[4,4,2,2,16,128...) custom-call(s32[2,6]{1,0:T(2,128)S(1)} %copy-done, s32[2]{0:T(128)S(1)} %copy-done.1, s32[2]{0:T(128)S(1)} %pad_add_fusion.pos, ...), custom_call_target="tpu_custom_call" | custom-call | flops 2415919104 | bytes 12582912 | tf_op jit(solution)/shard_map/pallas_call | solution.py:146
  62.3 1.4 %collective-permute-done.10 = bf16[4,4,2,2,16,128]{5,4,3,2,1,0:T(8,128)(2,1)S(1)} collective-permute-done((bf16[4,4,2,2,16,128]{5,4,3,2,1,0:T(8,128)(2,1)S(1)}, bf16[4,4,2,2,16,128]{5,4,3,2,1,0:T(8,128)(2,1)S(1)}, u32[]{:S(2)}, u32[]{:S(2)}) %collective-permute-start.10) | collective-permute-done | bytes 262176 | tf_op jit(solution)/shard_map/ppermute | solution.py:177
  63.9 3.4 %collective-permute-start.13 = (bf16[2,4,2,2,16,128]{5,4,3,2,1,0:T(8,128)(2,1)S(1)}, bf16[2,4,2,2,16,128]{5,4,3,2,1,0:T(8,128)(2,1)S(1)}, u32[]{:S(2)}, u32[]{:S(2)}) collective-permute-start(bf16[2,4,2,2,16,128]{5,4,3,2,1,0:T(8,128)(2,1)S(1)} %get-tuple-element.42), channel_id=1, source_target_pairs={{0,56},{8,16},{16,8},{24,32},{32,24},{40,48},{48,40},{56,0},{1,57}... | collective-permute-start | bytes 393224 | tf_op jit(solution)/shard_map/ppermute | solution.py:200
  67.3 4.0 %collective-permute-done.13 = bf16[2,4,2,2,16,128]{5,4,3,2,1,0:T(8,128)(2,1)S(1)} collective-permute-done((bf16[2,4,2,2,16,128]{5,4,3,2,1,0:T(8,128)(2,1)S(1)}, bf16[2,4,2,2,16,128]{5,4,3,2,1,0:T(8,128)(2,1)S(1)}, u32[]{:S(2)}, u32[]{:S(2)}) %collective-permute-start.13) | collective-permute-done | bytes 131104 | tf_op jit(solution)/shard_map/ppermute | solution.py:200
  71.3 1.5 %collective-permute-done.12 = bf16[2,4,2,2,16,128]{5,4,3,2,1,0:T(8,128)(2,1)S(1)} collective-permute-done((bf16[2,4,2,2,16,128]{5,4,3,2,1,0:T(8,128)(2,1)S(1)}, bf16[2,4,2,2,16,128]{5,4,3,2,1,0:T(8,128)(2,1)S(1)}, u32[]{:S(2)}, u32[]{:S(2)}) %collective-permute-start.12) | collective-permute-done | bytes 131104 | tf_op jit(solution)/shard_map/ppermute | solution.py:200
  73.4 1.3 %collective-permute-start.15 = (bf16[4,4,2,2,16,128]{5,4,3,2,1,0:T(8,128)(2,1)S(1)}, bf16[4,4,2,2,16,128]{5,4,3,2,1,0:T(8,128)(2,1)S(1)}, u32[]{:S(2)}, u32[]{:S(2)}) collective-permute-start(bf16[4,4,2,2,16,128]{5,4,3,2,1,0:T(8,128)(2,1)S(1)} %pad_maximum_fusion.2), channel_id=1, source_target_pairs={{0,56},{8,16},{16,8},{24,32},{32,24},{40,48},{48,40},{56,0},{1,57}... | collective-permute-start | bytes 786440 | tf_op jit(solution)/shard_map/ppermute | solution.py:200
  74.7 5.8 %collective-permute-done.14 = bf16[4,4,2,2,16,128]{5,4,3,2,1,0:T(8,128)(2,1)S(1)} collective-permute-done((bf16[4,4,2,2,16,128]{5,4,3,2,1,0:T(8,128)(2,1)S(1)}, bf16[4,4,2,2,16,128]{5,4,3,2,1,0:T(8,128)(2,1)S(1)}, u32[]{:S(2)}, u32[]{:S(2)}) %collective-permute-start.14) | collective-permute-done | bytes 262176 | tf_op jit(solution)/shard_map/ppermute | solution.py:200
  80.6 1.6 %collective-permute-done.15 = bf16[4,4,2,2,16,128]{5,4,3,2,1,0:T(8,128)(2,1)S(1)} collective-permute-done((bf16[4,4,2,2,16,128]{5,4,3,2,1,0:T(8,128)(2,1)S(1)}, bf16[4,4,2,2,16,128]{5,4,3,2,1,0:T(8,128)(2,1)S(1)}, u32[]{:S(2)}, u32[]{:S(2)}) %collective-permute-start.15) | collective-permute-done | bytes 262176 | tf_op jit(solution)/shard_map/ppermute | solution.py:200
  82.5 1.6 %collective-permute-start.17 = (bf16[4,4,2,2,16,128]{5,4,3,2,1,0:T(8,128)(2,1)S(1)}, bf16[4,4,2,2,16,128]{5,4,3,2,1,0:T(8,128)(2,1)S(1)}, u32[]{:S(2)}, u32[]{:S(2)}) collective-permute-start(bf16[4,4,2,2,16,128]{5,4,3,2,1,0:T(8,128)(2,1)S(1)} %get-tuple-element.36), channel_id=1, source_target_pairs={{0,56},{8,16},{16,8},{24,32},{32,24},{40,48},{48,40},{56,0},{1,57}... | collective-permute-start | bytes 786440 | tf_op jit(solution)/shard_map/ppermute | solution.py:200
  85.3 5.0 %collective-permute-done.17 = bf16[4,4,2,2,16,128]{5,4,3,2,1,0:T(8,128)(2,1)S(1)} collective-permute-done((bf16[4,4,2,2,16,128]{5,4,3,2,1,0:T(8,128)(2,1)S(1)}, bf16[4,4,2,2,16,128]{5,4,3,2,1,0:T(8,128)(2,1)S(1)}, u32[]{:S(2)}, u32[]{:S(2)}) %collective-permute-start.17) | collective-permute-done | bytes 262176 | tf_op jit(solution)/shard_map/ppermute | solution.py:200
  90.9 1.6 %collective-permute-start.19 = (bf16[4,4,2,2,16,128]{5,4,3,2,1,0:T(8,128)(2,1)S(1)}, bf16[4,4,2,2,16,128]{5,4,3,2,1,0:T(8,128)(2,1)S(1)}, u32[]{:S(2)}, u32[]{:S(2)}) collective-permute-start(bf16[4,4,2,2,16,128]{5,4,3,2,1,0:T(8,128)(2,1)S(1)} %get-tuple-element.34), channel_id=1, source_target_pairs={{0,56},{8,16},{16,8},{24,32},{32,24},{40,48},{48,40},{56,0},{1,57}... | collective-permute-start | bytes 786440 | tf_op jit(solution)/shard_map/ppermute | solution.py:200
  93.4 5.1 %collective-permute-done.19 = bf16[4,4,2,2,16,128]{5,4,3,2,1,0:T(8,128)(2,1)S(1)} collective-permute-done((bf16[4,4,2,2,16,128]{5,4,3,2,1,0:T(8,128)(2,1)S(1)}, bf16[4,4,2,2,16,128]{5,4,3,2,1,0:T(8,128)(2,1)S(1)}, u32[]{:S(2)}, u32[]{:S(2)}) %collective-permute-start.19) | collective-permute-done | bytes 262176 | tf_op jit(solution)/shard_map/ppermute | solution.py:200
  99.1 11.6 %all_to_all.11 = bf16[16,2,2,16,128]{4,3,2,1,0:T(8,128)(2,1)S(1)} all-to-all(bf16[16,2,2,16,128]{4,3,2,1,0:T(8,128)(2,1)S(1)} %bitcast.137), channel_id=1, replica_groups=mesh['y'=4,'z'=8,'c'=2,'mp'=4] {'y','mp'}, dimensions={0} | all-to-all | bytes 524288 | tf_op jit(solution)/shard_map/all_to_all | solution.py:235
  (66 shorter events, 7.1 us)
Async XLA Ops:
  17.1 11.0 %collective-permute-start.2 = (bf16[4,4,2,2,16,128]{5,4,3,2,1,0:T(8,128)(2,1)S(1)}, bf16[4,4,2,2,16,128]{5,4,3,2,1,0:T(8,128)(2,1)S(1)}, u32[]{:S(2)}, u32[]{:S(2)}) collective-permute-start(bf16[4,4,2,2,16,128]{5,4,3,2,1,0:T(8,128)(2,1)S(1)} %bitcast.139), channel_id=1, source_target_pairs={{0,8},{8,16},{16,24},{24,32},{32,40},{40,48},{48,56},{56,0},{1,9},... | collective-permute-start | bytes 786440 | tf_op jit(solution)/shard_map/ppermute | solution.py:177
  19.0 9.1 %collective-permute-start = (bf16[4,4,2,2,16,128]{5,4,3,2,1,0:T(8,128)(2,1)S(1)}, bf16[4,4,2,2,16,128]{5,4,3,2,1,0:T(8,128)(2,1)S(1)}, u32[]{:S(2)}, u32[]{:S(2)}) collective-permute-start(bf16[4,4,2,2,16,128]{5,4,3,2,1,0:T(8,128)(2,1)S(1)} %bitcast.140), channel_id=1, source_target_pairs={{0,56},{8,0},{16,8},{24,16},{32,24},{40,32},{48,40},{56,48},{1,57}... | collective-permute-start | bytes 786440 | tf_op jit(solution)/shard_map/ppermute | solution.py:177
  28.1 7.6 %collective-permute-start.3 = (bf16[4,4,2,2,16,128]{5,4,3,2,1,0:T(8,128)(2,1)S(1)}, bf16[4,4,2,2,16,128]{5,4,3,2,1,0:T(8,128)(2,1)S(1)}, u32[]{:S(2)}, u32[]{:S(2)}) collective-permute-start(bf16[4,4,2,2,16,128]{5,4,3,2,1,0:T(8,128)(2,1)S(1)} %collective-permute-done.2), channel_id=1, source_target_pairs={{0,8},{8,16},{16,24},{24,32},{32,40},{40,48},{48,56},{56,0},{1,9},... | collective-permute-start | bytes 786440 | tf_op jit(solution)/shard_map/ppermute | solution.py:177
  28.1 7.6 %collective-permute-start.1 = (bf16[4,4,2,2,16,128]{5,4,3,2,1,0:T(8,128)(2,1)S(1)}, bf16[4,4,2,2,16,128]{5,4,3,2,1,0:T(8,128)(2,1)S(1)}, u32[]{:S(2)}, u32[]{:S(2)}) collective-permute-start(bf16[4,4,2,2,16,128]{5,4,3,2,1,0:T(8,128)(2,1)S(1)} %collective-permute-done), channel_id=1, source_target_pairs={{0,56},{8,0},{16,8},{24,16},{32,24},{40,32},{48,40},{56,48},{1,57}... | collective-permute-start | bytes 786440 | tf_op jit(solution)/shard_map/ppermute | solution.py:177
  35.7 7.6 %collective-permute-start.5 = (bf16[4,4,2,2,16,128]{5,4,3,2,1,0:T(8,128)(2,1)S(1)}, bf16[4,4,2,2,16,128]{5,4,3,2,1,0:T(8,128)(2,1)S(1)}, u32[]{:S(2)}, u32[]{:S(2)}) collective-permute-start(bf16[4,4,2,2,16,128]{5,4,3,2,1,0:T(8,128)(2,1)S(1)} %collective-permute-done.3), channel_id=1, source_target_pairs={{0,8},{8,16},{16,24},{24,32},{32,40},{40,48},{48,56},{56,0},{1,9},... | collective-permute-start | bytes 786440 | tf_op jit(solution)/shard_map/ppermute | solution.py:177
  35.7 7.7 %collective-permute-start.4 = (bf16[4,4,2,2,16,128]{5,4,3,2,1,0:T(8,128)(2,1)S(1)}, bf16[4,4,2,2,16,128]{5,4,3,2,1,0:T(8,128)(2,1)S(1)}, u32[]{:S(2)}, u32[]{:S(2)}) collective-permute-start(bf16[4,4,2,2,16,128]{5,4,3,2,1,0:T(8,128)(2,1)S(1)} %collective-permute-done.1), channel_id=1, source_target_pairs={{0,56},{8,0},{16,8},{24,16},{32,24},{40,32},{48,40},{56,48},{1,57}... | collective-permute-start | bytes 786440 | tf_op jit(solution)/shard_map/ppermute | solution.py:177
  39.1 13.3 %copy-start = (s32[2,6]{1,0:T(2,128)S(1)}, s32[2,6]{1,0:T(2,128)}, u32[]{:S(2)}) copy-start(s32[2,6]{1,0:T(2,128)} %images.1) | copy-start | bytes 148
  39.1 13.3 %copy-start.1 = (s32[2]{0:T(128)S(1)}, s32[2]{0:T(128)}, u32[]{:S(2)}) copy-start(s32[2]{0:T(128)} %reads.1) | copy-start | bytes 28
  39.1 13.3 %collective-permute-start.8 = (bf16[5,4,4,2,2,16,128]{6,5,4,3,2,1,0:T(8,128)(2,1)S(1)}, bf16[5,4,4,2,2,16,128]{6,5,4,3,2,1,0:T(8,128)(2,1)S(1)}, u32[]{:S(2)}, u32[]{:S(2)}) collective-permute-start(bf16[5,4,4,2,2,16,128]{6,5,4,3,2,1,0:T(8,128)(2,1)S(1)} %bitcast_dynamic-update-slice_fusion.refs_0_), channel_id=1, source_target_pairs={{0,4},{4,0},{1,5},{5,1},{2,6},{6,2},{3,7},{7,3},{8,12},{12,8},{9,1... | collective-permute-start | bytes 3932168 | tf_op jit(solution)/shard_map/ppermute | solution.py:177
  43.3 6.3 %collective-permute-start.6 = (bf16[2,4,2,2,16,128]{5,4,3,2,1,0:T(8,128)(2,1)S(1)}, bf16[2,4,2,2,16,128]{5,4,3,2,1,0:T(8,128)(2,1)S(1)}, u32[]{:S(2)}, u32[]{:S(2)}) collective-permute-start(bf16[2,4,2,2,16,128]{5,4,3,2,1,0:T(8,128)(2,1)S(1)} %slice.178), channel_id=1, source_target_pairs={{0,8},{8,16},{16,24},{24,32},{32,40},{40,48},{48,56},{56,0},{1,9},... | collective-permute-start | bytes 393224 | tf_op jit(solution)/shard_map/ppermute | solution.py:177
  43.4 6.1 %collective-permute-start.7 = (bf16[2,4,2,2,16,128]{5,4,3,2,1,0:T(8,128)(2,1)S(1)}, bf16[2,4,2,2,16,128]{5,4,3,2,1,0:T(8,128)(2,1)S(1)}, u32[]{:S(2)}, u32[]{:S(2)}) collective-permute-start(bf16[2,4,2,2,16,128]{5,4,3,2,1,0:T(8,128)(2,1)S(1)} %slice.179), channel_id=1, source_target_pairs={{0,56},{8,0},{16,8},{24,16},{32,24},{40,32},{48,40},{56,48},{1,57}... | collective-permute-start | bytes 393224 | tf_op jit(solution)/shard_map/ppermute | solution.py:177
  49.7 2.7 %collective-permute-start.9 = (bf16[3,4,4,2,2,16,128]{6,5,4,3,2,1,0:T(8,128)(2,1)S(1)}, bf16[3,4,4,2,2,16,128]{6,5,4,3,2,1,0:T(8,128)(2,1)}, u32[]{:S(2)}, u32[]{:S(2)}) collective-permute-start(bf16[3,4,4,2,2,16,128]{6,5,4,3,2,1,0:T(8,128)(2,1)S(1)} %pad_maximum_fusion.refs_1_), channel_id=1, source_target_pairs={{0,4},{4,0},{1,5},{5,1},{2,6},{6,2},{3,7},{7,3},{8,12},{12,8},{9,1... | collective-permute-start | bytes 2359304 | tf_op jit(solution)/shard_map/ppermute | solution.py:177
  62.1 1.5 %collective-permute-start.10 = (bf16[4,4,2,2,16,128]{5,4,3,2,1,0:T(8,128)(2,1)S(1)}, bf16[4,4,2,2,16,128]{5,4,3,2,1,0:T(8,128)(2,1)S(1)}, u32[]{:S(2)}, u32[]{:S(2)}) collective-permute-start(bf16[4,4,2,2,16,128]{5,4,3,2,1,0:T(8,128)(2,1)S(1)} %get-tuple-element.21), channel_id=1, source_target_pairs={{0,4},{4,0},{1,5},{5,1},{2,6},{6,2},{3,7},{7,3},{8,12},{12,8},{9,1... | collective-permute-start | bytes 786440 | tf_op jit(solution)/shard_map/ppermute | solution.py:177
  63.7 9.1 %collective-permute-start.11 = (bf16[28,4,2,2,16,128]{5,4,3,2,1,0:T(8,128)(2,1)S(1)}, bf16[28,4,2,2,16,128]{5,4,3,2,1,0:T(8,128)(2,1)S(1)}, u32[]{:S(2)}, u32[]{:S(2)}) collective-permute-start(bf16[28,4,2,2,16,128]{5,4,3,2,1,0:T(8,128)(2,1)S(1)} %get-tuple-element.22), channel_id=1, source_target_pairs={{0,4},{4,0},{1,5},{5,1},{2,6},{6,2},{3,7},{7,3},{8,12},{12,8},{9,1... | collective-permute-start | bytes 5505032 | tf_op jit(solution)/shard_map/ppermute | solution.py:177
  63.9 7.5 %collective-permute-start.13 = (bf16[2,4,2,2,16,128]{5,4,3,2,1,0:T(8,128)(2,1)S(1)}, bf16[2,4,2,2,16,128]{5,4,3,2,1,0:T(8,128)(2,1)S(1)}, u32[]{:S(2)}, u32[]{:S(2)}) collective-permute-start(bf16[2,4,2,2,16,128]{5,4,3,2,1,0:T(8,128)(2,1)S(1)} %get-tuple-element.42), channel_id=1, source_target_pairs={{0,56},{8,16},{16,8},{24,32},{32,24},{40,48},{48,40},{56,0},{1,57}... | collective-permute-start | bytes 393224 | tf_op jit(solution)/shard_map/ppermute | solution.py:200
  67.3 5.5 %collective-permute-start.12 = (bf16[2,4,2,2,16,128]{5,4,3,2,1,0:T(8,128)(2,1)S(1)}, bf16[2,4,2,2,16,128]{5,4,3,2,1,0:T(8,128)(2,1)S(1)}, u32[]{:S(2)}, u32[]{:S(2)}) collective-permute-start(bf16[2,4,2,2,16,128]{5,4,3,2,1,0:T(8,128)(2,1)S(1)} %get-tuple-element.43), channel_id=1, source_target_pairs={{0,8},{8,0},{16,24},{24,16},{32,40},{40,32},{48,56},{56,48},{1,9},... | collective-permute-start | bytes 393224 | tf_op jit(solution)/shard_map/ppermute | solution.py:200
  73.0 7.5 %collective-permute-start.14 = (bf16[4,4,2,2,16,128]{5,4,3,2,1,0:T(8,128)(2,1)S(1)}, bf16[4,4,2,2,16,128]{5,4,3,2,1,0:T(8,128)(2,1)S(1)}, u32[]{:S(2)}, u32[]{:S(2)}) collective-permute-start(bf16[4,4,2,2,16,128]{5,4,3,2,1,0:T(8,128)(2,1)S(1)} %pad_maximum_fusion.1), channel_id=1, source_target_pairs={{0,8},{8,0},{16,24},{24,16},{32,40},{40,32},{48,56},{56,48},{1,9},... | collective-permute-start | bytes 786440 | tf_op jit(solution)/shard_map/ppermute | solution.py:200
  73.4 8.8 %collective-permute-start.15 = (bf16[4,4,2,2,16,128]{5,4,3,2,1,0:T(8,128)(2,1)S(1)}, bf16[4,4,2,2,16,128]{5,4,3,2,1,0:T(8,128)(2,1)S(1)}, u32[]{:S(2)}, u32[]{:S(2)}) collective-permute-start(bf16[4,4,2,2,16,128]{5,4,3,2,1,0:T(8,128)(2,1)S(1)} %pad_maximum_fusion.2), channel_id=1, source_target_pairs={{0,56},{8,16},{16,8},{24,32},{32,24},{40,48},{48,40},{56,0},{1,57}... | collective-permute-start | bytes 786440 | tf_op jit(solution)/shard_map/ppermute | solution.py:200
  82.5 7.9 %collective-permute-start.17 = (bf16[4,4,2,2,16,128]{5,4,3,2,1,0:T(8,128)(2,1)S(1)}, bf16[4,4,2,2,16,128]{5,4,3,2,1,0:T(8,128)(2,1)S(1)}, u32[]{:S(2)}, u32[]{:S(2)}) collective-permute-start(bf16[4,4,2,2,16,128]{5,4,3,2,1,0:T(8,128)(2,1)S(1)} %get-tuple-element.36), channel_id=1, source_target_pairs={{0,56},{8,16},{16,8},{24,32},{32,24},{40,48},{48,40},{56,0},{1,57}... | collective-permute-start | bytes 786440 | tf_op jit(solution)/shard_map/ppermute | solution.py:200
  84.1 6.6 %collective-permute-start.16 = (bf16[4,4,2,2,16,128]{5,4,3,2,1,0:T(8,128)(2,1)S(1)}, bf16[4,4,2,2,16,128]{5,4,3,2,1,0:T(8,128)(2,1)S(1)}, u32[]{:S(2)}, u32[]{:S(2)}) collective-permute-start(bf16[4,4,2,2,16,128]{5,4,3,2,1,0:T(8,128)(2,1)S(1)} %get-tuple-element.37), channel_id=1, source_target_pairs={{0,8},{8,0},{16,24},{24,16},{32,40},{40,32},{48,56},{56,48},{1,9},... | collective-permute-start | bytes 786440 | tf_op jit(solution)/shard_map/ppermute | solution.py:200
  90.9 7.7 %collective-permute-start.19 = (bf16[4,4,2,2,16,128]{5,4,3,2,1,0:T(8,128)(2,1)S(1)}, bf16[4,4,2,2,16,128]{5,4,3,2,1,0:T(8,128)(2,1)S(1)}, u32[]{:S(2)}, u32[]{:S(2)}) collective-permute-start(bf16[4,4,2,2,16,128]{5,4,3,2,1,0:T(8,128)(2,1)S(1)} %get-tuple-element.34), channel_id=1, source_target_pairs={{0,56},{8,16},{16,8},{24,32},{32,24},{40,48},{48,40},{56,0},{1,57}... | collective-permute-start | bytes 786440 | tf_op jit(solution)/shard_map/ppermute | solution.py:200
  92.5 6.4 %collective-permute-start.18 = (bf16[4,4,2,2,16,128]{5,4,3,2,1,0:T(8,128)(2,1)S(1)}, bf16[4,4,2,2,16,128]{5,4,3,2,1,0:T(8,128)(2,1)S(1)}, u32[]{:S(2)}, u32[]{:S(2)}) collective-permute-start(bf16[4,4,2,2,16,128]{5,4,3,2,1,0:T(8,128)(2,1)S(1)} %get-tuple-element.35), channel_id=1, source_target_pairs={{0,8},{8,0},{16,24},{24,16},{32,40},{40,32},{48,56},{56,48},{1,9},... | collective-permute-start | bytes 786440 | tf_op jit(solution)/shard_map/ppermute | solution.py:200
  110.8 0.7 copy-start.2

commit v5 on v4

--- a/solution.py
+++ b/solution.py
@@ -107,7 +107,10 @@
     for i in range(steps):
         clear(i)
         now, ahead = ahead, front(i + 1) if i + 1 < steps else None
-        back(i, *middle(*now))
+        if behind is not None:
+            back(i - 1, *behind)
+        behind = middle(*now)
+    back(steps - 1, *behind)
 
     @pl.when(b == blocks - 1)
     def _():

time: 112 us -> 112 us (level)
  no operation moved by 1% of the time
where the time goes in v5:
time: 112 us; the launch traced here: 111 us
  waiting for transfers between devices  43.9 us (39%)
  starting transfers between devices  26.8 us (24%)
  blocking collectives  26.2 us (23%)
  Pallas kernels  9.6 us (9%)
  other arithmetic  2.21 us (2%)
  between operations  1.6 us (1%)
    ppermute x12, waiting for transfers between devices, shift(): return lax.ppermute(x, axis, [(i, (i + by) % size) for i in range(size)])  20.1 us
    ppermute x12, starting transfers between devices, shift(): return lax.ppermute(x, axis, [(i, (i + by) % size) for i in range(size)])  16.3 us
    ppermute x4, waiting for transfers between devices, exchange(): lax.ppermute(b, 'z', pairs[1])  15.8 us
    all_to_all x1, blocking collectives, local(): unit = lax.all_to_all(kv, ('y', 'mp'), 0, 0, tiled=True)  14.6 us
    all_to_all x1, blocking collectives, local(): total = lax.all_to_all(total, ('y', 'mp'), 0, 0, tiled=True)  11.6 us
    pallas_call x1, Pallas kernels, attend(): pl.pallas_call(attend_kernel, grid=(blocks,), in_specs=[smem] * 3 + [text...  9.6 us
    ppermute x4, starting transfers between devices, exchange(): lax.ppermute(b, 'z', pairs[1])  7.96 us
    ppermute x4, waiting for transfers between devices, exchange(): lax.ppermute(a, 'z', pairs[0])  7.9 us
  transfers between devices with their start and end apart: 20, of which 14 were waited for; matrix products, arithmetic and copies ran while one was open for 0% of the time, Pallas kernels for 0%

profile of v5, /device:TPU:2, one launch (start us, length us, event | category | flops | bytes accessed | tf_op | source)
XLA Modules:
  0.0 111.3 jit_solution(2197784778954249072)
XLA Ops:
  2.5 14.6 %all_to_all.10 = bf16[16,2,2,16,128]{4,3,2,1,0:T(8,128)(2,1)S(1)} all-to-all(bf16[16,2,2,16,128]{4,3,2,1,0:T(8,128)(2,1)S(1)} %bitcast.138), channel_id=1, replica_groups=mesh['y'=4,'z'=8,'c'=2,'mp'=4] {'y','mp'}, dimensions={0} | all-to-all | bytes 524288 | tf_op jit(solution)/shard_map/all_to_all | solution.py:228
  17.1 1.9 %collective-permute-start.2 = (bf16[4,4,2,2,16,128]{5,4,3,2,1,0:T(8,128)(2,1)S(1)}, bf16[4,4,2,2,16,128]{5,4,3,2,1,0:T(8,128)(2,1)S(1)}, u32[]{:S(2)}, u32[]{:S(2)}) collective-permute-start(bf16[4,4,2,2,16,128]{5,4,3,2,1,0:T(8,128)(2,1)S(1)} %bitcast.139), channel_id=1, source_target_pairs={{0,8},{8,16},{16,24},{24,32},{32,40},{40,48},{48,56},{56,0},{1,9},... | collective-permute-start | bytes 786440 | tf_op jit(solution)/shard_map/ppermute | solution.py:180
  19.0 3.9 %collective-permute-start = (bf16[4,4,2,2,16,128]{5,4,3,2,1,0:T(8,128)(2,1)S(1)}, bf16[4,4,2,2,16,128]{5,4,3,2,1,0:T(8,128)(2,1)S(1)}, u32[]{:S(2)}, u32[]{:S(2)}) collective-permute-start(bf16[4,4,2,2,16,128]{5,4,3,2,1,0:T(8,128)(2,1)S(1)} %bitcast.140), channel_id=1, source_target_pairs={{0,56},{8,0},{16,8},{24,16},{32,24},{40,32},{48,40},{56,48},{1,57}... | collective-permute-start | bytes 786440 | tf_op jit(solution)/shard_map/ppermute | solution.py:180
  22.9 5.2 %collective-permute-done.2 = bf16[4,4,2,2,16,128]{5,4,3,2,1,0:T(8,128)(2,1)S(1)} collective-permute-done((bf16[4,4,2,2,16,128]{5,4,3,2,1,0:T(8,128)(2,1)S(1)}, bf16[4,4,2,2,16,128]{5,4,3,2,1,0:T(8,128)(2,1)S(1)}, u32[]{:S(2)}, u32[]{:S(2)}) %collective-permute-start.2) | collective-permute-done | bytes 262176 | tf_op jit(solution)/shard_map/ppermute | solution.py:180
  28.1 3.2 %collective-permute-start.1 = (bf16[4,4,2,2,16,128]{5,4,3,2,1,0:T(8,128)(2,1)S(1)}, bf16[4,4,2,2,16,128]{5,4,3,2,1,0:T(8,128)(2,1)S(1)}, u32[]{:S(2)}, u32[]{:S(2)}) collective-permute-start(bf16[4,4,2,2,16,128]{5,4,3,2,1,0:T(8,128)(2,1)S(1)} %collective-permute-done), channel_id=1, source_target_pairs={{0,56},{8,0},{16,8},{24,16},{32,24},{40,32},{48,40},{56,48},{1,57}... | collective-permute-start | bytes 786440 | tf_op jit(solution)/shard_map/ppermute | solution.py:180
  31.4 4.3 %collective-permute-done.3 = bf16[4,4,2,2,16,128]{5,4,3,2,1,0:T(8,128)(2,1)S(1)} collective-permute-done((bf16[4,4,2,2,16,128]{5,4,3,2,1,0:T(8,128)(2,1)S(1)}, bf16[4,4,2,2,16,128]{5,4,3,2,1,0:T(8,128)(2,1)S(1)}, u32[]{:S(2)}, u32[]{:S(2)}) %collective-permute-start.3) | collective-permute-done | bytes 262176 | tf_op jit(solution)/shard_map/ppermute | solution.py:180
  35.7 3.2 %collective-permute-start.4 = (bf16[4,4,2,2,16,128]{5,4,3,2,1,0:T(8,128)(2,1)S(1)}, bf16[4,4,2,2,16,128]{5,4,3,2,1,0:T(8,128)(2,1)S(1)}, u32[]{:S(2)}, u32[]{:S(2)}) collective-permute-start(bf16[4,4,2,2,16,128]{5,4,3,2,1,0:T(8,128)(2,1)S(1)} %collective-permute-done.1), channel_id=1, source_target_pairs={{0,56},{8,0},{16,8},{24,16},{32,24},{40,32},{48,40},{56,48},{1,57}... | collective-permute-start | bytes 786440 | tf_op jit(solution)/shard_map/ppermute | solution.py:180
  39.2 4.1 %collective-permute-done.5 = bf16[4,4,2,2,16,128]{5,4,3,2,1,0:T(8,128)(2,1)S(1)} collective-permute-done((bf16[4,4,2,2,16,128]{5,4,3,2,1,0:T(8,128)(2,1)S(1)}, bf16[4,4,2,2,16,128]{5,4,3,2,1,0:T(8,128)(2,1)S(1)}, u32[]{:S(2)}, u32[]{:S(2)}) %collective-permute-start.5) | collective-permute-done | bytes 262176 | tf_op jit(solution)/shard_map/ppermute | solution.py:180
  43.4 3.3 %collective-permute-start.7 = (bf16[2,4,2,2,16,128]{5,4,3,2,1,0:T(8,128)(2,1)S(1)}, bf16[2,4,2,2,16,128]{5,4,3,2,1,0:T(8,128)(2,1)S(1)}, u32[]{:S(2)}, u32[]{:S(2)}) collective-permute-start(bf16[2,4,2,2,16,128]{5,4,3,2,1,0:T(8,128)(2,1)S(1)} %slice.179), channel_id=1, source_target_pairs={{0,56},{8,0},{16,8},{24,16},{32,24},{40,32},{48,40},{56,48},{1,57}... | collective-permute-start | bytes 393224 | tf_op jit(solution)/shard_map/ppermute | solution.py:180
  46.7 2.8 %collective-permute-done.6 = bf16[2,4,2,2,16,128]{5,4,3,2,1,0:T(8,128)(2,1)S(1)} collective-permute-done((bf16[2,4,2,2,16,128]{5,4,3,2,1,0:T(8,128)(2,1)S(1)}, bf16[2,4,2,2,16,128]{5,4,3,2,1,0:T(8,128)(2,1)S(1)}, u32[]{:S(2)}, u32[]{:S(2)}) %collective-permute-start.6) | collective-permute-done | bytes 131104 | tf_op jit(solution)/shard_map/ppermute | solution.py:180
  50.0 2.3 %collective-permute-done.9.refs_3_ = bf16[3,4,4,2,2,16,128]{6,5,4,3,2,1,0:T(8,128)(2,1)} collective-permute-done((bf16[3,4,4,2,2,16,128]{6,5,4,3,2,1,0:T(8,128)(2,1)S(1)}, bf16[3,4,4,2,2,16,128]{6,5,4,3,2,1,0:T(8,128)(2,1)}, u32[]{:S(2)}, u32[]{:S(2)}) %collective-permute-start.9) | collective-permute-done | bytes 786464 | tf_op jit(solution)/shard_map/ppermute | solution.py:180
  52.4 9.6 %shard_map.85 = (bf16[256,2048]{1,0:T(8,128)(2,1)}, bf16[256,2048]{1,0:T(8,128)(2,1)}, bf16[32,4,2,2,16,128]{5,4,3,2,1,0:T(8,128)(2,1)S(1)}, bf16[4,4,2,2,16,128...) custom-call(s32[2,6]{1,0:T(2,128)S(1)} %copy-done, s32[2]{0:T(128)S(1)} %copy-done.1, s32[2]{0:T(128)S(1)} %pad_add_fusion.pos, ...), custom_call_target="tpu_custom_call" | custom-call | flops 2415919104 | bytes 12582912 | tf_op jit(solution)/shard_map/pallas_call | solution.py:149
  62.1 1.4 %collective-permute-done.10 = bf16[4,4,2,2,16,128]{5,4,3,2,1,0:T(8,128)(2,1)S(1)} collective-permute-done((bf16[4,4,2,2,16,128]{5,4,3,2,1,0:T(8,128)(2,1)S(1)}, bf16[4,4,2,2,16,128]{5,4,3,2,1,0:T(8,128)(2,1)S(1)}, u32[]{:S(2)}, u32[]{:S(2)}) %collective-permute-start.10) | collective-permute-done | bytes 262176 | tf_op jit(solution)/shard_map/ppermute | solution.py:180
  63.7 3.4 %collective-permute-start.13 = (bf16[2,4,2,2,16,128]{5,4,3,2,1,0:T(8,128)(2,1)S(1)}, bf16[2,4,2,2,16,128]{5,4,3,2,1,0:T(8,128)(2,1)S(1)}, u32[]{:S(2)}, u32[]{:S(2)}) collective-permute-start(bf16[2,4,2,2,16,128]{5,4,3,2,1,0:T(8,128)(2,1)S(1)} %get-tuple-element.42), channel_id=1, source_target_pairs={{0,56},{8,16},{16,8},{24,32},{32,24},{40,48},{48,40},{56,0},{1,57}... | collective-permute-start | bytes 393224 | tf_op jit(solution)/shard_map/ppermute | solution.py:203
  67.2 4.0 %collective-permute-done.13 = bf16[2,4,2,2,16,128]{5,4,3,2,1,0:T(8,128)(2,1)S(1)} collective-permute-done((bf16[2,4,2,2,16,128]{5,4,3,2,1,0:T(8,128)(2,1)S(1)}, bf16[2,4,2,2,16,128]{5,4,3,2,1,0:T(8,128)(2,1)S(1)}, u32[]{:S(2)}, u32[]{:S(2)}) %collective-permute-start.13) | collective-permute-done | bytes 131104 | tf_op jit(solution)/shard_map/ppermute | solution.py:203
  71.2 1.5 %collective-permute-done.12 = bf16[2,4,2,2,16,128]{5,4,3,2,1,0:T(8,128)(2,1)S(1)} collective-permute-done((bf16[2,4,2,2,16,128]{5,4,3,2,1,0:T(8,128)(2,1)S(1)}, bf16[2,4,2,2,16,128]{5,4,3,2,1,0:T(8,128)(2,1)S(1)}, u32[]{:S(2)}, u32[]{:S(2)}) %collective-permute-start.12) | collective-permute-done | bytes 131104 | tf_op jit(solution)/shard_map/ppermute | solution.py:203
  73.3 1.3 %collective-permute-start.15 = (bf16[4,4,2,2,16,128]{5,4,3,2,1,0:T(8,128)(2,1)S(1)}, bf16[4,4,2,2,16,128]{5,4,3,2,1,0:T(8,128)(2,1)S(1)}, u32[]{:S(2)}, u32[]{:S(2)}) collective-permute-start(bf16[4,4,2,2,16,128]{5,4,3,2,1,0:T(8,128)(2,1)S(1)} %pad_maximum_fusion.2), channel_id=1, source_target_pairs={{0,56},{8,16},{16,8},{24,32},{32,24},{40,48},{48,40},{56,0},{1,57}... | collective-permute-start | bytes 786440 | tf_op jit(solution)/shard_map/ppermute | solution.py:203
  74.6 5.8 %collective-permute-done.14 = bf16[4,4,2,2,16,128]{5,4,3,2,1,0:T(8,128)(2,1)S(1)} collective-permute-done((bf16[4,4,2,2,16,128]{5,4,3,2,1,0:T(8,128)(2,1)S(1)}, bf16[4,4,2,2,16,128]{5,4,3,2,1,0:T(8,128)(2,1)S(1)}, u32[]{:S(2)}, u32[]{:S(2)}) %collective-permute-start.14) | collective-permute-done | bytes 262176 | tf_op jit(solution)/shard_map/ppermute | solution.py:203
  80.4 1.6 %collective-permute-done.15 = bf16[4,4,2,2,16,128]{5,4,3,2,1,0:T(8,128)(2,1)S(1)} collective-permute-done((bf16[4,4,2,2,16,128]{5,4,3,2,1,0:T(8,128)(2,1)S(1)}, bf16[4,4,2,2,16,128]{5,4,3,2,1,0:T(8,128)(2,1)S(1)}, u32[]{:S(2)}, u32[]{:S(2)}) %collective-permute-start.15) | collective-permute-done | bytes 262176 | tf_op jit(solution)/shard_map/ppermute | solution.py:203
  82.3 1.6 %collective-permute-start.17 = (bf16[4,4,2,2,16,128]{5,4,3,2,1,0:T(8,128)(2,1)S(1)}, bf16[4,4,2,2,16,128]{5,4,3,2,1,0:T(8,128)(2,1)S(1)}, u32[]{:S(2)}, u32[]{:S(2)}) collective-permute-start(bf16[4,4,2,2,16,128]{5,4,3,2,1,0:T(8,128)(2,1)S(1)} %get-tuple-element.36), channel_id=1, source_target_pairs={{0,56},{8,16},{16,8},{24,32},{32,24},{40,48},{48,40},{56,0},{1,57}... | collective-permute-start | bytes 786440 | tf_op jit(solution)/shard_map/ppermute | solution.py:203
  85.1 5.0 %collective-permute-done.17 = bf16[4,4,2,2,16,128]{5,4,3,2,1,0:T(8,128)(2,1)S(1)} collective-permute-done((bf16[4,4,2,2,16,128]{5,4,3,2,1,0:T(8,128)(2,1)S(1)}, bf16[4,4,2,2,16,128]{5,4,3,2,1,0:T(8,128)(2,1)S(1)}, u32[]{:S(2)}, u32[]{:S(2)}) %collective-permute-start.17) | collective-permute-done | bytes 262176 | tf_op jit(solution)/shard_map/ppermute | solution.py:203
  90.7 1.6 %collective-permute-start.19 = (bf16[4,4,2,2,16,128]{5,4,3,2,1,0:T(8,128)(2,1)S(1)}, bf16[4,4,2,2,16,128]{5,4,3,2,1,0:T(8,128)(2,1)S(1)}, u32[]{:S(2)}, u32[]{:S(2)}) collective-permute-start(bf16[4,4,2,2,16,128]{5,4,3,2,1,0:T(8,128)(2,1)S(1)} %get-tuple-element.34), channel_id=1, source_target_pairs={{0,56},{8,16},{16,8},{24,32},{32,24},{40,48},{48,40},{56,0},{1,57}... | collective-permute-start | bytes 786440 | tf_op jit(solution)/shard_map/ppermute | solution.py:203
  93.3 5.1 %collective-permute-done.19 = bf16[4,4,2,2,16,128]{5,4,3,2,1,0:T(8,128)(2,1)S(1)} collective-permute-done((bf16[4,4,2,2,16,128]{5,4,3,2,1,0:T(8,128)(2,1)S(1)}, bf16[4,4,2,2,16,128]{5,4,3,2,1,0:T(8,128)(2,1)S(1)}, u32[]{:S(2)}, u32[]{:S(2)}) %collective-permute-start.19) | collective-permute-done | bytes 262176 | tf_op jit(solution)/shard_map/ppermute | solution.py:203
  98.9 11.6 %all_to_all.11 = bf16[16,2,2,16,128]{4,3,2,1,0:T(8,128)(2,1)S(1)} all-to-all(bf16[16,2,2,16,128]{4,3,2,1,0:T(8,128)(2,1)S(1)} %bitcast.137), channel_id=1, replica_groups=mesh['y'=4,'z'=8,'c'=2,'mp'=4] {'y','mp'}, dimensions={0} | all-to-all | bytes 524288 | tf_op jit(solution)/shard_map/all_to_all | solution.py:238
  (66 shorter events, 7.1 us)
Async XLA Ops:
  17.1 11.0 %collective-permute-start.2 = (bf16[4,4,2,2,16,128]{5,4,3,2,1,0:T(8,128)(2,1)S(1)}, bf16[4,4,2,2,16,128]{5,4,3,2,1,0:T(8,128)(2,1)S(1)}, u32[]{:S(2)}, u32[]{:S(2)}) collective-permute-start(bf16[4,4,2,2,16,128]{5,4,3,2,1,0:T(8,128)(2,1)S(1)} %bitcast.139), channel_id=1, source_target_pairs={{0,8},{8,16},{16,24},{24,32},{32,40},{40,48},{48,56},{56,0},{1,9},... | collective-permute-start | bytes 786440 | tf_op jit(solution)/shard_map/ppermute | solution.py:180
  19.0 9.1 %collective-permute-start = (bf16[4,4,2,2,16,128]{5,4,3,2,1,0:T(8,128)(2,1)S(1)}, bf16[4,4,2,2,16,128]{5,4,3,2,1,0:T(8,128)(2,1)S(1)}, u32[]{:S(2)}, u32[]{:S(2)}) collective-permute-start(bf16[4,4,2,2,16,128]{5,4,3,2,1,0:T(8,128)(2,1)S(1)} %bitcast.140), channel_id=1, source_target_pairs={{0,56},{8,0},{16,8},{24,16},{32,24},{40,32},{48,40},{56,48},{1,57}... | collective-permute-start | bytes 786440 | tf_op jit(solution)/shard_map/ppermute | solution.py:180
  28.1 7.6 %collective-permute-start.3 = (bf16[4,4,2,2,16,128]{5,4,3,2,1,0:T(8,128)(2,1)S(1)}, bf16[4,4,2,2,16,128]{5,4,3,2,1,0:T(8,128)(2,1)S(1)}, u32[]{:S(2)}, u32[]{:S(2)}) collective-permute-start(bf16[4,4,2,2,16,128]{5,4,3,2,1,0:T(8,128)(2,1)S(1)} %collective-permute-done.2), channel_id=1, source_target_pairs={{0,8},{8,16},{16,24},{24,32},{32,40},{40,48},{48,56},{56,0},{1,9},... | collective-permute-start | bytes 786440 | tf_op jit(solution)/shard_map/ppermute | solution.py:180
  28.1 7.6 %collective-permute-start.1 = (bf16[4,4,2,2,16,128]{5,4,3,2,1,0:T(8,128)(2,1)S(1)}, bf16[4,4,2,2,16,128]{5,4,3,2,1,0:T(8,128)(2,1)S(1)}, u32[]{:S(2)}, u32[]{:S(2)}) collective-permute-start(bf16[4,4,2,2,16,128]{5,4,3,2,1,0:T(8,128)(2,1)S(1)} %collective-permute-done), channel_id=1, source_target_pairs={{0,56},{8,0},{16,8},{24,16},{32,24},{40,32},{48,40},{56,48},{1,57}... | collective-permute-start | bytes 786440 | tf_op jit(solution)/shard_map/ppermute | solution.py:180
  35.7 7.6 %collective-permute-start.5 = (bf16[4,4,2,2,16,128]{5,4,3,2,1,0:T(8,128)(2,1)S(1)}, bf16[4,4,2,2,16,128]{5,4,3,2,1,0:T(8,128)(2,1)S(1)}, u32[]{:S(2)}, u32[]{:S(2)}) collective-permute-start(bf16[4,4,2,2,16,128]{5,4,3,2,1,0:T(8,128)(2,1)S(1)} %collective-permute-done.3), channel_id=1, source_target_pairs={{0,8},{8,16},{16,24},{24,32},{32,40},{40,48},{48,56},{56,0},{1,9},... | collective-permute-start | bytes 786440 | tf_op jit(solution)/shard_map/ppermute | solution.py:180
  35.7 7.7 %collective-permute-start.4 = (bf16[4,4,2,2,16,128]{5,4,3,2,1,0:T(8,128)(2,1)S(1)}, bf16[4,4,2,2,16,128]{5,4,3,2,1,0:T(8,128)(2,1)S(1)}, u32[]{:S(2)}, u32[]{:S(2)}) collective-permute-start(bf16[4,4,2,2,16,128]{5,4,3,2,1,0:T(8,128)(2,1)S(1)} %collective-permute-done.1), channel_id=1, source_target_pairs={{0,56},{8,0},{16,8},{24,16},{32,24},{40,32},{48,40},{56,48},{1,57}... | collective-permute-start | bytes 786440 | tf_op jit(solution)/shard_map/ppermute | solution.py:180
  39.1 13.3 %copy-start = (s32[2,6]{1,0:T(2,128)S(1)}, s32[2,6]{1,0:T(2,128)}, u32[]{:S(2)}) copy-start(s32[2,6]{1,0:T(2,128)} %images.1) | copy-start | bytes 148
  39.1 13.3 %copy-start.1 = (s32[2]{0:T(128)S(1)}, s32[2]{0:T(128)}, u32[]{:S(2)}) copy-start(s32[2]{0:T(128)} %reads.1) | copy-start | bytes 28
  39.1 13.3 %collective-permute-start.8 = (bf16[5,4,4,2,2,16,128]{6,5,4,3,2,1,0:T(8,128)(2,1)S(1)}, bf16[5,4,4,2,2,16,128]{6,5,4,3,2,1,0:T(8,128)(2,1)S(1)}, u32[]{:S(2)}, u32[]{:S(2)}) collective-permute-start(bf16[5,4,4,2,2,16,128]{6,5,4,3,2,1,0:T(8,128)(2,1)S(1)} %bitcast_dynamic-update-slice_fusion.refs_0_), channel_id=1, source_target_pairs={{0,4},{4,0},{1,5},{5,1},{2,6},{6,2},{3,7},{7,3},{8,12},{12,8},{9,1... | collective-permute-start | bytes 3932168 | tf_op jit(solution)/shard_map/ppermute | solution.py:180
  43.3 6.3 %collective-permute-start.6 = (bf16[2,4,2,2,16,128]{5,4,3,2,1,0:T(8,128)(2,1)S(1)}, bf16[2,4,2,2,16,128]{5,4,3,2,1,0:T(8,128)(2,1)S(1)}, u32[]{:S(2)}, u32[]{:S(2)}) collective-permute-start(bf16[2,4,2,2,16,128]{5,4,3,2,1,0:T(8,128)(2,1)S(1)} %slice.178), channel_id=1, source_target_pairs={{0,8},{8,16},{16,24},{24,32},{32,40},{40,48},{48,56},{56,0},{1,9},... | collective-permute-start | bytes 393224 | tf_op jit(solution)/shard_map/ppermute | solution.py:180
  43.4 6.1 %collective-permute-start.7 = (bf16[2,4,2,2,16,128]{5,4,3,2,1,0:T(8,128)(2,1)S(1)}, bf16[2,4,2,2,16,128]{5,4,3,2,1,0:T(8,128)(2,1)S(1)}, u32[]{:S(2)}, u32[]{:S(2)}) collective-permute-start(bf16[2,4,2,2,16,128]{5,4,3,2,1,0:T(8,128)(2,1)S(1)} %slice.179), channel_id=1, source_target_pairs={{0,56},{8,0},{16,8},{24,16},{32,24},{40,32},{48,40},{56,48},{1,57}... | collective-permute-start | bytes 393224 | tf_op jit(solution)/shard_map/ppermute | solution.py:180
  49.7 2.7 %collective-permute-start.9 = (bf16[3,4,4,2,2,16,128]{6,5,4,3,2,1,0:T(8,128)(2,1)S(1)}, bf16[3,4,4,2,2,16,128]{6,5,4,3,2,1,0:T(8,128)(2,1)}, u32[]{:S(2)}, u32[]{:S(2)}) collective-permute-start(bf16[3,4,4,2,2,16,128]{6,5,4,3,2,1,0:T(8,128)(2,1)S(1)} %pad_maximum_fusion.refs_1_), channel_id=1, source_target_pairs={{0,4},{4,0},{1,5},{5,1},{2,6},{6,2},{3,7},{7,3},{8,12},{12,8},{9,1... | collective-permute-start | bytes 2359304 | tf_op jit(solution)/shard_map/ppermute | solution.py:180
  62.0 1.5 %collective-permute-start.10 = (bf16[4,4,2,2,16,128]{5,4,3,2,1,0:T(8,128)(2,1)S(1)}, bf16[4,4,2,2,16,128]{5,4,3,2,1,0:T(8,128)(2,1)S(1)}, u32[]{:S(2)}, u32[]{:S(2)}) collective-permute-start(bf16[4,4,2,2,16,128]{5,4,3,2,1,0:T(8,128)(2,1)S(1)} %get-tuple-element.21), channel_id=1, source_target_pairs={{0,4},{4,0},{1,5},{5,1},{2,6},{6,2},{3,7},{7,3},{8,12},{12,8},{9,1... | collective-permute-start | bytes 786440 | tf_op jit(solution)/shard_map/ppermute | solution.py:180
  63.5 9.1 %collective-permute-start.11 = (bf16[28,4,2,2,16,128]{5,4,3,2,1,0:T(8,128)(2,1)S(1)}, bf16[28,4,2,2,16,128]{5,4,3,2,1,0:T(8,128)(2,1)S(1)}, u32[]{:S(2)}, u32[]{:S(2)}) collective-permute-start(bf16[28,4,2,2,16,128]{5,4,3,2,1,0:T(8,128)(2,1)S(1)} %get-tuple-element.22), channel_id=1, source_target_pairs={{0,4},{4,0},{1,5},{5,1},{2,6},{6,2},{3,7},{7,3},{8,12},{12,8},{9,1... | collective-permute-start | bytes 5505032 | tf_op jit(solution)/shard_map/ppermute | solution.py:180
  63.7 7.5 %collective-permute-start.13 = (bf16[2,4,2,2,16,128]{5,4,3,2,1,0:T(8,128)(2,1)S(1)}, bf16[2,4,2,2,16,128]{5,4,3,2,1,0:T(8,128)(2,1)S(1)}, u32[]{:S(2)}, u32[]{:S(2)}) collective-permute-start(bf16[2,4,2,2,16,128]{5,4,3,2,1,0:T(8,128)(2,1)S(1)} %get-tuple-element.42), channel_id=1, source_target_pairs={{0,56},{8,16},{16,8},{24,32},{32,24},{40,48},{48,40},{56,0},{1,57}... | collective-permute-start | bytes 393224 | tf_op jit(solution)/shard_map/ppermute | solution.py:203
  67.2 5.5 %collective-permute-start.12 = (bf16[2,4,2,2,16,128]{5,4,3,2,1,0:T(8,128)(2,1)S(1)}, bf16[2,4,2,2,16,128]{5,4,3,2,1,0:T(8,128)(2,1)S(1)}, u32[]{:S(2)}, u32[]{:S(2)}) collective-permute-start(bf16[2,4,2,2,16,128]{5,4,3,2,1,0:T(8,128)(2,1)S(1)} %get-tuple-element.43), channel_id=1, source_target_pairs={{0,8},{8,0},{16,24},{24,16},{32,40},{40,32},{48,56},{56,48},{1,9},... | collective-permute-start | bytes 393224 | tf_op jit(solution)/shard_map/ppermute | solution.py:203
  72.9 7.5 %collective-permute-start.14 = (bf16[4,4,2,2,16,128]{5,4,3,2,1,0:T(8,128)(2,1)S(1)}, bf16[4,4,2,2,16,128]{5,4,3,2,1,0:T(8,128)(2,1)S(1)}, u32[]{:S(2)}, u32[]{:S(2)}) collective-permute-start(bf16[4,4,2,2,16,128]{5,4,3,2,1,0:T(8,128)(2,1)S(1)} %pad_maximum_fusion.1), channel_id=1, source_target_pairs={{0,8},{8,0},{16,24},{24,16},{32,40},{40,32},{48,56},{56,48},{1,9},... | collective-permute-start | bytes 786440 | tf_op jit(solution)/shard_map/ppermute | solution.py:203
  73.3 8.8 %collective-permute-start.15 = (bf16[4,4,2,2,16,128]{5,4,3,2,1,0:T(8,128)(2,1)S(1)}, bf16[4,4,2,2,16,128]{5,4,3,2,1,0:T(8,128)(2,1)S(1)}, u32[]{:S(2)}, u32[]{:S(2)}) collective-permute-start(bf16[4,4,2,2,16,128]{5,4,3,2,1,0:T(8,128)(2,1)S(1)} %pad_maximum_fusion.2), channel_id=1, source_target_pairs={{0,56},{8,16},{16,8},{24,32},{32,24},{40,48},{48,40},{56,0},{1,57}... | collective-permute-start | bytes 786440 | tf_op jit(solution)/shard_map/ppermute | solution.py:203
  82.3 7.9 %collective-permute-start.17 = (bf16[4,4,2,2,16,128]{5,4,3,2,1,0:T(8,128)(2,1)S(1)}, bf16[4,4,2,2,16,128]{5,4,3,2,1,0:T(8,128)(2,1)S(1)}, u32[]{:S(2)}, u32[]{:S(2)}) collective-permute-start(bf16[4,4,2,2,16,128]{5,4,3,2,1,0:T(8,128)(2,1)S(1)} %get-tuple-element.36), channel_id=1, source_target_pairs={{0,56},{8,16},{16,8},{24,32},{32,24},{40,48},{48,40},{56,0},{1,57}... | collective-permute-start | bytes 786440 | tf_op jit(solution)/shard_map/ppermute | solution.py:203
  83.9 6.6 %collective-permute-start.16 = (bf16[4,4,2,2,16,128]{5,4,3,2,1,0:T(8,128)(2,1)S(1)}, bf16[4,4,2,2,16,128]{5,4,3,2,1,0:T(8,128)(2,1)S(1)}, u32[]{:S(2)}, u32[]{:S(2)}) collective-permute-start(bf16[4,4,2,2,16,128]{5,4,3,2,1,0:T(8,128)(2,1)S(1)} %get-tuple-element.37), channel_id=1, source_target_pairs={{0,8},{8,0},{16,24},{24,16},{32,40},{40,32},{48,56},{56,48},{1,9},... | collective-permute-start | bytes 786440 | tf_op jit(solution)/shard_map/ppermute | solution.py:203
  90.7 7.7 %collective-permute-start.19 = (bf16[4,4,2,2,16,128]{5,4,3,2,1,0:T(8,128)(2,1)S(1)}, bf16[4,4,2,2,16,128]{5,4,3,2,1,0:T(8,128)(2,1)S(1)}, u32[]{:S(2)}, u32[]{:S(2)}) collective-permute-start(bf16[4,4,2,2,16,128]{5,4,3,2,1,0:T(8,128)(2,1)S(1)} %get-tuple-element.34), channel_id=1, source_target_pairs={{0,56},{8,16},{16,8},{24,32},{32,24},{40,48},{48,40},{56,0},{1,57}... | collective-permute-start | bytes 786440 | tf_op jit(solution)/shard_map/ppermute | solution.py:203
  92.4 6.4 %collective-permute-start.18 = (bf16[4,4,2,2,16,128]{5,4,3,2,1,0:T(8,128)(2,1)S(1)}, bf16[4,4,2,2,16,128]{5,4,3,2,1,0:T(8,128)(2,1)S(1)}, u32[]{:S(2)}, u32[]{:S(2)}) collective-permute-start(bf16[4,4,2,2,16,128]{5,4,3,2,1,0:T(8,128)(2,1)S(1)} %get-tuple-element.35), channel_id=1, source_target_pairs={{0,8},{8,0},{16,24},{24,16},{32,40},{40,32},{48,56},{56,48},{1,9},... | collective-permute-start | bytes 786440 | tf_op jit(solution)/shard_map/ppermute | solution.py:203
  110.6 0.7 copy-start.2

commit v6 on v5

--- a/solution.py
+++ b/solution.py
@@ -106,9 +106,9 @@
     ahead, behind = front(0), None
     for i in range(steps):
         clear(i)
-        now, ahead = ahead, front(i + 1) if i + 1 < steps else None
         if behind is not None:
             back(i - 1, *behind)
+        now, ahead = ahead, front(i + 1) if i + 1 < steps else None
         behind = middle(*now)
     back(steps - 1, *behind)
 

time: 112 us -> 112 us (level)
  no operation moved by 1% of the time
where the time goes in v6:
time: 112 us; the launch traced here: 111 us
  waiting for transfers between devices  43.9 us (39%)
  starting transfers between devices  26.8 us (24%)
  blocking collectives  26.2 us (23%)
  Pallas kernels  9.78 us (9%)
  other arithmetic  2.21 us (2%)
  between operations  1.6 us (1%)
    ppermute x12, waiting for transfers between devices, shift(): return lax.ppermute(x, axis, [(i, (i + by) % size) for i in range(size)])  20.1 us
    ppermute x12, starting transfers between devices, shift(): return lax.ppermute(x, axis, [(i, (i + by) % size) for i in range(size)])  16.3 us
    ppermute x4, waiting for transfers between devices, exchange(): lax.ppermute(b, 'z', pairs[1])  15.8 us
    all_to_all x1, blocking collectives, local(): unit = lax.all_to_all(kv, ('y', 'mp'), 0, 0, tiled=True)  14.6 us
    all_to_all x1, blocking collectives, local(): total = lax.all_to_all(total, ('y', 'mp'), 0, 0, tiled=True)  11.6 us
    pallas_call x1, Pallas kernels, attend(): pl.pallas_call(attend_kernel, grid=(blocks,), in_specs=[smem] * 3 + [text...  9.78 us
    ppermute x4, starting transfers between devices, exchange(): lax.ppermute(b, 'z', pairs[1])  7.96 us
    ppermute x4, waiting for transfers between devices, exchange(): lax.ppermute(a, 'z', pairs[0])  7.9 us
  transfers between devices with their start and end apart: 20, of which 14 were waited for; matrix products, arithmetic and copies ran while one was open for 0% of the time, Pallas kernels for 0%

profile of v6, /device:TPU:2, one launch (start us, length us, event | category | flops | bytes accessed | tf_op | source)
XLA Modules:
  0.0 111.5 jit_solution(8906685924057807917)
XLA Ops:
  2.5 14.6 %all_to_all.10 = bf16[16,2,2,16,128]{4,3,2,1,0:T(8,128)(2,1)S(1)} all-to-all(bf16[16,2,2,16,128]{4,3,2,1,0:T(8,128)(2,1)S(1)} %bitcast.138), channel_id=1, replica_groups=mesh['y'=4,'z'=8,'c'=2,'mp'=4] {'y','mp'}, dimensions={0} | all-to-all | bytes 524288 | tf_op jit(solution)/shard_map/all_to_all | solution.py:228
  17.1 1.9 %collective-permute-start.2 = (bf16[4,4,2,2,16,128]{5,4,3,2,1,0:T(8,128)(2,1)S(1)}, bf16[4,4,2,2,16,128]{5,4,3,2,1,0:T(8,128)(2,1)S(1)}, u32[]{:S(2)}, u32[]{:S(2)}) collective-permute-start(bf16[4,4,2,2,16,128]{5,4,3,2,1,0:T(8,128)(2,1)S(1)} %bitcast.139), channel_id=1, source_target_pairs={{0,8},{8,16},{16,24},{24,32},{32,40},{40,48},{48,56},{56,0},{1,9},... | collective-permute-start | bytes 786440 | tf_op jit(solution)/shard_map/ppermute | solution.py:180
  19.0 3.9 %collective-permute-start = (bf16[4,4,2,2,16,128]{5,4,3,2,1,0:T(8,128)(2,1)S(1)}, bf16[4,4,2,2,16,128]{5,4,3,2,1,0:T(8,128)(2,1)S(1)}, u32[]{:S(2)}, u32[]{:S(2)}) collective-permute-start(bf16[4,4,2,2,16,128]{5,4,3,2,1,0:T(8,128)(2,1)S(1)} %bitcast.140), channel_id=1, source_target_pairs={{0,56},{8,0},{16,8},{24,16},{32,24},{40,32},{48,40},{56,48},{1,57}... | collective-permute-start | bytes 786440 | tf_op jit(solution)/shard_map/ppermute | solution.py:180
  22.9 5.2 %collective-permute-done.2 = bf16[4,4,2,2,16,128]{5,4,3,2,1,0:T(8,128)(2,1)S(1)} collective-permute-done((bf16[4,4,2,2,16,128]{5,4,3,2,1,0:T(8,128)(2,1)S(1)}, bf16[4,4,2,2,16,128]{5,4,3,2,1,0:T(8,128)(2,1)S(1)}, u32[]{:S(2)}, u32[]{:S(2)}) %collective-permute-start.2) | collective-permute-done | bytes 262176 | tf_op jit(solution)/shard_map/ppermute | solution.py:180
  28.1 3.2 %collective-permute-start.1 = (bf16[4,4,2,2,16,128]{5,4,3,2,1,0:T(8,128)(2,1)S(1)}, bf16[4,4,2,2,16,128]{5,4,3,2,1,0:T(8,128)(2,1)S(1)}, u32[]{:S(2)}, u32[]{:S(2)}) collective-permute-start(bf16[4,4,2,2,16,128]{5,4,3,2,1,0:T(8,128)(2,1)S(1)} %collective-permute-done), channel_id=1, source_target_pairs={{0,56},{8,0},{16,8},{24,16},{32,24},{40,32},{48,40},{56,48},{1,57}... | collective-permute-start | bytes 786440 | tf_op jit(solution)/shard_map/ppermute | solution.py:180
  31.4 4.3 %collective-permute-done.3 = bf16[4,4,2,2,16,128]{5,4,3,2,1,0:T(8,128)(2,1)S(1)} collective-permute-done((bf16[4,4,2,2,16,128]{5,4,3,2,1,0:T(8,128)(2,1)S(1)}, bf16[4,4,2,2,16,128]{5,4,3,2,1,0:T(8,128)(2,1)S(1)}, u32[]{:S(2)}, u32[]{:S(2)}) %collective-permute-start.3) | collective-permute-done | bytes 262176 | tf_op jit(solution)/shard_map/ppermute | solution.py:180
  35.7 3.2 %collective-permute-start.4 = (bf16[4,4,2,2,16,128]{5,4,3,2,1,0:T(8,128)(2,1)S(1)}, bf16[4,4,2,2,16,128]{5,4,3,2,1,0:T(8,128)(2,1)S(1)}, u32[]{:S(2)}, u32[]{:S(2)}) collective-permute-start(bf16[4,4,2,2,16,128]{5,4,3,2,1,0:T(8,128)(2,1)S(1)} %collective-permute-done.1), channel_id=1, source_target_pairs={{0,56},{8,0},{16,8},{24,16},{32,24},{40,32},{48,40},{56,48},{1,57}... | collective-permute-start | bytes 786440 | tf_op jit(solution)/shard_map/ppermute | solution.py:180
  39.2 4.1 %collective-permute-done.5 = bf16[4,4,2,2,16,128]{5,4,3,2,1,0:T(8,128)(2,1)S(1)} collective-permute-done((bf16[4,4,2,2,16,128]{5,4,3,2,1,0:T(8,128)(2,1)S(1)}, bf16[4,4,2,2,16,128]{5,4,3,2,1,0:T(8,128)(2,1)S(1)}, u32[]{:S(2)}, u32[]{:S(2)}) %collective-permute-start.5) | collective-permute-done | bytes 262176 | tf_op jit(solution)/shard_map/ppermute | solution.py:180
  43.4 3.3 %collective-permute-start.7 = (bf16[2,4,2,2,16,128]{5,4,3,2,1,0:T(8,128)(2,1)S(1)}, bf16[2,4,2,2,16,128]{5,4,3,2,1,0:T(8,128)(2,1)S(1)}, u32[]{:S(2)}, u32[]{:S(2)}) collective-permute-start(bf16[2,4,2,2,16,128]{5,4,3,2,1,0:T(8,128)(2,1)S(1)} %slice.179), channel_id=1, source_target_pairs={{0,56},{8,0},{16,8},{24,16},{32,24},{40,32},{48,40},{56,48},{1,57}... | collective-permute-start | bytes 393224 | tf_op jit(solution)/shard_map/ppermute | solution.py:180
  46.7 2.8 %collective-permute-done.6 = bf16[2,4,2,2,16,128]{5,4,3,2,1,0:T(8,128)(2,1)S(1)} collective-permute-done((bf16[2,4,2,2,16,128]{5,4,3,2,1,0:T(8,128)(2,1)S(1)}, bf16[2,4,2,2,16,128]{5,4,3,2,1,0:T(8,128)(2,1)S(1)}, u32[]{:S(2)}, u32[]{:S(2)}) %collective-permute-start.6) | collective-permute-done | bytes 131104 | tf_op jit(solution)/shard_map/ppermute | solution.py:180
  50.0 2.3 %collective-permute-done.9.refs_3_ = bf16[3,4,4,2,2,16,128]{6,5,4,3,2,1,0:T(8,128)(2,1)} collective-permute-done((bf16[3,4,4,2,2,16,128]{6,5,4,3,2,1,0:T(8,128)(2,1)S(1)}, bf16[3,4,4,2,2,16,128]{6,5,4,3,2,1,0:T(8,128)(2,1)}, u32[]{:S(2)}, u32[]{:S(2)}) %collective-permute-start.9) | collective-permute-done | bytes 786464 | tf_op jit(solution)/shard_map/ppermute | solution.py:180
  52.4 9.8 %shard_map.85 = (bf16[256,2048]{1,0:T(8,128)(2,1)}, bf16[256,2048]{1,0:T(8,128)(2,1)}, bf16[32,4,2,2,16,128]{5,4,3,2,1,0:T(8,128)(2,1)S(1)}, bf16[4,4,2,2,16,128...) custom-call(s32[2,6]{1,0:T(2,128)S(1)} %copy-done, s32[2]{0:T(128)S(1)} %copy-done.1, s32[2]{0:T(128)S(1)} %pad_add_fusion.pos, ...), custom_call_target="tpu_custom_call" | custom-call | flops 2415919104 | bytes 12582912 | tf_op jit(solution)/shard_map/pallas_call | solution.py:149
  62.3 1.4 %collective-permute-done.10 = bf16[4,4,2,2,16,128]{5,4,3,2,1,0:T(8,128)(2,1)S(1)} collective-permute-done((bf16[4,4,2,2,16,128]{5,4,3,2,1,0:T(8,128)(2,1)S(1)}, bf16[4,4,2,2,16,128]{5,4,3,2,1,0:T(8,128)(2,1)S(1)}, u32[]{:S(2)}, u32[]{:S(2)}) %collective-permute-start.10) | collective-permute-done | bytes 262176 | tf_op jit(solution)/shard_map/ppermute | solution.py:180
  63.9 3.4 %collective-permute-start.13 = (bf16[2,4,2,2,16,128]{5,4,3,2,1,0:T(8,128)(2,1)S(1)}, bf16[2,4,2,2,16,128]{5,4,3,2,1,0:T(8,128)(2,1)S(1)}, u32[]{:S(2)}, u32[]{:S(2)}) collective-permute-start(bf16[2,4,2,2,16,128]{5,4,3,2,1,0:T(8,128)(2,1)S(1)} %get-tuple-element.42), channel_id=1, source_target_pairs={{0,56},{8,16},{16,8},{24,32},{32,24},{40,48},{48,40},{56,0},{1,57}... | collective-permute-start | bytes 393224 | tf_op jit(solution)/shard_map/ppermute | solution.py:203
  67.3 4.0 %collective-permute-done.13 = bf16[2,4,2,2,16,128]{5,4,3,2,1,0:T(8,128)(2,1)S(1)} collective-permute-done((bf16[2,4,2,2,16,128]{5,4,3,2,1,0:T(8,128)(2,1)S(1)}, bf16[2,4,2,2,16,128]{5,4,3,2,1,0:T(8,128)(2,1)S(1)}, u32[]{:S(2)}, u32[]{:S(2)}) %collective-permute-start.13) | collective-permute-done | bytes 131104 | tf_op jit(solution)/shard_map/ppermute | solution.py:203
  71.4 1.5 %collective-permute-done.12 = bf16[2,4,2,2,16,128]{5,4,3,2,1,0:T(8,128)(2,1)S(1)} collective-permute-done((bf16[2,4,2,2,16,128]{5,4,3,2,1,0:T(8,128)(2,1)S(1)}, bf16[2,4,2,2,16,128]{5,4,3,2,1,0:T(8,128)(2,1)S(1)}, u32[]{:S(2)}, u32[]{:S(2)}) %collective-permute-start.12) | collective-permute-done | bytes 131104 | tf_op jit(solution)/shard_map/ppermute | solution.py:203
  73.5 1.3 %collective-permute-start.15 = (bf16[4,4,2,2,16,128]{5,4,3,2,1,0:T(8,128)(2,1)S(1)}, bf16[4,4,2,2,16,128]{5,4,3,2,1,0:T(8,128)(2,1)S(1)}, u32[]{:S(2)}, u32[]{:S(2)}) collective-permute-start(bf16[4,4,2,2,16,128]{5,4,3,2,1,0:T(8,128)(2,1)S(1)} %pad_maximum_fusion.2), channel_id=1, source_target_pairs={{0,56},{8,16},{16,8},{24,32},{32,24},{40,48},{48,40},{56,0},{1,57}... | collective-permute-start | bytes 786440 | tf_op jit(solution)/shard_map/ppermute | solution.py:203
  74.8 5.8 %collective-permute-done.14 = bf16[4,4,2,2,16,128]{5,4,3,2,1,0:T(8,128)(2,1)S(1)} collective-permute-done((bf16[4,4,2,2,16,128]{5,4,3,2,1,0:T(8,128)(2,1)S(1)}, bf16[4,4,2,2,16,128]{5,4,3,2,1,0:T(8,128)(2,1)S(1)}, u32[]{:S(2)}, u32[]{:S(2)}) %collective-permute-start.14) | collective-permute-done | bytes 262176 | tf_op jit(solution)/shard_map/ppermute | solution.py:203
  80.6 1.6 %collective-permute-done.15 = bf16[4,4,2,2,16,128]{5,4,3,2,1,0:T(8,128)(2,1)S(1)} collective-permute-done((bf16[4,4,2,2,16,128]{5,4,3,2,1,0:T(8,128)(2,1)S(1)}, bf16[4,4,2,2,16,128]{5,4,3,2,1,0:T(8,128)(2,1)S(1)}, u32[]{:S(2)}, u32[]{:S(2)}) %collective-permute-start.15) | collective-permute-done | bytes 262176 | tf_op jit(solution)/shard_map/ppermute | solution.py:203
  82.5 1.6 %collective-permute-start.17 = (bf16[4,4,2,2,16,128]{5,4,3,2,1,0:T(8,128)(2,1)S(1)}, bf16[4,4,2,2,16,128]{5,4,3,2,1,0:T(8,128)(2,1)S(1)}, u32[]{:S(2)}, u32[]{:S(2)}) collective-permute-start(bf16[4,4,2,2,16,128]{5,4,3,2,1,0:T(8,128)(2,1)S(1)} %get-tuple-element.36), channel_id=1, source_target_pairs={{0,56},{8,16},{16,8},{24,32},{32,24},{40,48},{48,40},{56,0},{1,57}... | collective-permute-start | bytes 786440 | tf_op jit(solution)/shard_map/ppermute | solution.py:203
  85.3 5.0 %collective-permute-done.17 = bf16[4,4,2,2,16,128]{5,4,3,2,1,0:T(8,128)(2,1)S(1)} collective-permute-done((bf16[4,4,2,2,16,128]{5,4,3,2,1,0:T(8,128)(2,1)S(1)}, bf16[4,4,2,2,16,128]{5,4,3,2,1,0:T(8,128)(2,1)S(1)}, u32[]{:S(2)}, u32[]{:S(2)}) %collective-permute-start.17) | collective-permute-done | bytes 262176 | tf_op jit(solution)/shard_map/ppermute | solution.py:203
  90.9 1.6 %collective-permute-start.19 = (bf16[4,4,2,2,16,128]{5,4,3,2,1,0:T(8,128)(2,1)S(1)}, bf16[4,4,2,2,16,128]{5,4,3,2,1,0:T(8,128)(2,1)S(1)}, u32[]{:S(2)}, u32[]{:S(2)}) collective-permute-start(bf16[4,4,2,2,16,128]{5,4,3,2,1,0:T(8,128)(2,1)S(1)} %get-tuple-element.34), channel_id=1, source_target_pairs={{0,56},{8,16},{16,8},{24,32},{32,24},{40,48},{48,40},{56,0},{1,57}... | collective-permute-start | bytes 786440 | tf_op jit(solution)/shard_map/ppermute | solution.py:203
  93.5 5.1 %collective-permute-done.19 = bf16[4,4,2,2,16,128]{5,4,3,2,1,0:T(8,128)(2,1)S(1)} collective-permute-done((bf16[4,4,2,2,16,128]{5,4,3,2,1,0:T(8,128)(2,1)S(1)}, bf16[4,4,2,2,16,128]{5,4,3,2,1,0:T(8,128)(2,1)S(1)}, u32[]{:S(2)}, u32[]{:S(2)}) %collective-permute-start.19) | collective-permute-done | bytes 262176 | tf_op jit(solution)/shard_map/ppermute | solution.py:203
  99.1 11.6 %all_to_all.11 = bf16[16,2,2,16,128]{4,3,2,1,0:T(8,128)(2,1)S(1)} all-to-all(bf16[16,2,2,16,128]{4,3,2,1,0:T(8,128)(2,1)S(1)} %bitcast.137), channel_id=1, replica_groups=mesh['y'=4,'z'=8,'c'=2,'mp'=4] {'y','mp'}, dimensions={0} | all-to-all | bytes 524288 | tf_op jit(solution)/shard_map/all_to_all | solution.py:238
  (66 shorter events, 7.1 us)
Async XLA Ops:
  17.1 11.0 %collective-permute-start.2 = (bf16[4,4,2,2,16,128]{5,4,3,2,1,0:T(8,128)(2,1)S(1)}, bf16[4,4,2,2,16,128]{5,4,3,2,1,0:T(8,128)(2,1)S(1)}, u32[]{:S(2)}, u32[]{:S(2)}) collective-permute-start(bf16[4,4,2,2,16,128]{5,4,3,2,1,0:T(8,128)(2,1)S(1)} %bitcast.139), channel_id=1, source_target_pairs={{0,8},{8,16},{16,24},{24,32},{32,40},{40,48},{48,56},{56,0},{1,9},... | collective-permute-start | bytes 786440 | tf_op jit(solution)/shard_map/ppermute | solution.py:180
  19.0 9.1 %collective-permute-start = (bf16[4,4,2,2,16,128]{5,4,3,2,1,0:T(8,128)(2,1)S(1)}, bf16[4,4,2,2,16,128]{5,4,3,2,1,0:T(8,128)(2,1)S(1)}, u32[]{:S(2)}, u32[]{:S(2)}) collective-permute-start(bf16[4,4,2,2,16,128]{5,4,3,2,1,0:T(8,128)(2,1)S(1)} %bitcast.140), channel_id=1, source_target_pairs={{0,56},{8,0},{16,8},{24,16},{32,24},{40,32},{48,40},{56,48},{1,57}... | collective-permute-start | bytes 786440 | tf_op jit(solution)/shard_map/ppermute | solution.py:180
  28.1 7.6 %collective-permute-start.3 = (bf16[4,4,2,2,16,128]{5,4,3,2,1,0:T(8,128)(2,1)S(1)}, bf16[4,4,2,2,16,128]{5,4,3,2,1,0:T(8,128)(2,1)S(1)}, u32[]{:S(2)}, u32[]{:S(2)}) collective-permute-start(bf16[4,4,2,2,16,128]{5,4,3,2,1,0:T(8,128)(2,1)S(1)} %collective-permute-done.2), channel_id=1, source_target_pairs={{0,8},{8,16},{16,24},{24,32},{32,40},{40,48},{48,56},{56,0},{1,9},... | collective-permute-start | bytes 786440 | tf_op jit(solution)/shard_map/ppermute | solution.py:180
  28.1 7.6 %collective-permute-start.1 = (bf16[4,4,2,2,16,128]{5,4,3,2,1,0:T(8,128)(2,1)S(1)}, bf16[4,4,2,2,16,128]{5,4,3,2,1,0:T(8,128)(2,1)S(1)}, u32[]{:S(2)}, u32[]{:S(2)}) collective-permute-start(bf16[4,4,2,2,16,128]{5,4,3,2,1,0:T(8,128)(2,1)S(1)} %collective-permute-done), channel_id=1, source_target_pairs={{0,56},{8,0},{16,8},{24,16},{32,24},{40,32},{48,40},{56,48},{1,57}... | collective-permute-start | bytes 786440 | tf_op jit(solution)/shard_map/ppermute | solution.py:180
  35.7 7.6 %collective-permute-start.5 = (bf16[4,4,2,2,16,128]{5,4,3,2,1,0:T(8,128)(2,1)S(1)}, bf16[4,4,2,2,16,128]{5,4,3,2,1,0:T(8,128)(2,1)S(1)}, u32[]{:S(2)}, u32[]{:S(2)}) collective-permute-start(bf16[4,4,2,2,16,128]{5,4,3,2,1,0:T(8,128)(2,1)S(1)} %collective-permute-done.3), channel_id=1, source_target_pairs={{0,8},{8,16},{16,24},{24,32},{32,40},{40,48},{48,56},{56,0},{1,9},... | collective-permute-start | bytes 786440 | tf_op jit(solution)/shard_map/ppermute | solution.py:180
  35.7 7.7 %collective-permute-start.4 = (bf16[4,4,2,2,16,128]{5,4,3,2,1,0:T(8,128)(2,1)S(1)}, bf16[4,4,2,2,16,128]{5,4,3,2,1,0:T(8,128)(2,1)S(1)}, u32[]{:S(2)}, u32[]{:S(2)}) collective-permute-start(bf16[4,4,2,2,16,128]{5,4,3,2,1,0:T(8,128)(2,1)S(1)} %collective-permute-done.1), channel_id=1, source_target_pairs={{0,56},{8,0},{16,8},{24,16},{32,24},{40,32},{48,40},{56,48},{1,57}... | collective-permute-start | bytes 786440 | tf_op jit(solution)/shard_map/ppermute | solution.py:180
  39.1 13.3 %copy-start = (s32[2,6]{1,0:T(2,128)S(1)}, s32[2,6]{1,0:T(2,128)}, u32[]{:S(2)}) copy-start(s32[2,6]{1,0:T(2,128)} %images.1) | copy-start | bytes 148
  39.1 13.3 %copy-start.1 = (s32[2]{0:T(128)S(1)}, s32[2]{0:T(128)}, u32[]{:S(2)}) copy-start(s32[2]{0:T(128)} %reads.1) | copy-start | bytes 28
  39.1 13.3 %collective-permute-start.8 = (bf16[5,4,4,2,2,16,128]{6,5,4,3,2,1,0:T(8,128)(2,1)S(1)}, bf16[5,4,4,2,2,16,128]{6,5,4,3,2,1,0:T(8,128)(2,1)S(1)}, u32[]{:S(2)}, u32[]{:S(2)}) collective-permute-start(bf16[5,4,4,2,2,16,128]{6,5,4,3,2,1,0:T(8,128)(2,1)S(1)} %bitcast_dynamic-update-slice_fusion.refs_0_), channel_id=1, source_target_pairs={{0,4},{4,0},{1,5},{5,1},{2,6},{6,2},{3,7},{7,3},{8,12},{12,8},{9,1... | collective-permute-start | bytes 3932168 | tf_op jit(solution)/shard_map/ppermute | solution.py:180
  43.3 6.3 %collective-permute-start.6 = (bf16[2,4,2,2,16,128]{5,4,3,2,1,0:T(8,128)(2,1)S(1)}, bf16[2,4,2,2,16,128]{5,4,3,2,1,0:T(8,128)(2,1)S(1)}, u32[]{:S(2)}, u32[]{:S(2)}) collective-permute-start(bf16[2,4,2,2,16,128]{5,4,3,2,1,0:T(8,128)(2,1)S(1)} %slice.178), channel_id=1, source_target_pairs={{0,8},{8,16},{16,24},{24,32},{32,40},{40,48},{48,56},{56,0},{1,9},... | collective-permute-start | bytes 393224 | tf_op jit(solution)/shard_map/ppermute | solution.py:180
  43.4 6.1 %collective-permute-start.7 = (bf16[2,4,2,2,16,128]{5,4,3,2,1,0:T(8,128)(2,1)S(1)}, bf16[2,4,2,2,16,128]{5,4,3,2,1,0:T(8,128)(2,1)S(1)}, u32[]{:S(2)}, u32[]{:S(2)}) collective-permute-start(bf16[2,4,2,2,16,128]{5,4,3,2,1,0:T(8,128)(2,1)S(1)} %slice.179), channel_id=1, source_target_pairs={{0,56},{8,0},{16,8},{24,16},{32,24},{40,32},{48,40},{56,48},{1,57}... | collective-permute-start | bytes 393224 | tf_op jit(solution)/shard_map/ppermute | solution.py:180
  49.7 2.7 %collective-permute-start.9 = (bf16[3,4,4,2,2,16,128]{6,5,4,3,2,1,0:T(8,128)(2,1)S(1)}, bf16[3,4,4,2,2,16,128]{6,5,4,3,2,1,0:T(8,128)(2,1)}, u32[]{:S(2)}, u32[]{:S(2)}) collective-permute-start(bf16[3,4,4,2,2,16,128]{6,5,4,3,2,1,0:T(8,128)(2,1)S(1)} %pad_maximum_fusion.refs_1_), channel_id=1, source_target_pairs={{0,4},{4,0},{1,5},{5,1},{2,6},{6,2},{3,7},{7,3},{8,12},{12,8},{9,1... | collective-permute-start | bytes 2359304 | tf_op jit(solution)/shard_map/ppermute | solution.py:180
  62.2 1.5 %collective-permute-start.10 = (bf16[4,4,2,2,16,128]{5,4,3,2,1,0:T(8,128)(2,1)S(1)}, bf16[4,4,2,2,16,128]{5,4,3,2,1,0:T(8,128)(2,1)S(1)}, u32[]{:S(2)}, u32[]{:S(2)}) collective-permute-start(bf16[4,4,2,2,16,128]{5,4,3,2,1,0:T(8,128)(2,1)S(1)} %get-tuple-element.21), channel_id=1, source_target_pairs={{0,4},{4,0},{1,5},{5,1},{2,6},{6,2},{3,7},{7,3},{8,12},{12,8},{9,1... | collective-permute-start | bytes 786440 | tf_op jit(solution)/shard_map/ppermute | solution.py:180
  63.7 9.1 %collective-permute-start.11 = (bf16[28,4,2,2,16,128]{5,4,3,2,1,0:T(8,128)(2,1)S(1)}, bf16[28,4,2,2,16,128]{5,4,3,2,1,0:T(8,128)(2,1)S(1)}, u32[]{:S(2)}, u32[]{:S(2)}) collective-permute-start(bf16[28,4,2,2,16,128]{5,4,3,2,1,0:T(8,128)(2,1)S(1)} %get-tuple-element.22), channel_id=1, source_target_pairs={{0,4},{4,0},{1,5},{5,1},{2,6},{6,2},{3,7},{7,3},{8,12},{12,8},{9,1... | collective-permute-start | bytes 5505032 | tf_op jit(solution)/shard_map/ppermute | solution.py:180
  63.9 7.5 %collective-permute-start.13 = (bf16[2,4,2,2,16,128]{5,4,3,2,1,0:T(8,128)(2,1)S(1)}, bf16[2,4,2,2,16,128]{5,4,3,2,1,0:T(8,128)(2,1)S(1)}, u32[]{:S(2)}, u32[]{:S(2)}) collective-permute-start(bf16[2,4,2,2,16,128]{5,4,3,2,1,0:T(8,128)(2,1)S(1)} %get-tuple-element.42), channel_id=1, source_target_pairs={{0,56},{8,16},{16,8},{24,32},{32,24},{40,48},{48,40},{56,0},{1,57}... | collective-permute-start | bytes 393224 | tf_op jit(solution)/shard_map/ppermute | solution.py:203
  67.3 5.5 %collective-permute-start.12 = (bf16[2,4,2,2,16,128]{5,4,3,2,1,0:T(8,128)(2,1)S(1)}, bf16[2,4,2,2,16,128]{5,4,3,2,1,0:T(8,128)(2,1)S(1)}, u32[]{:S(2)}, u32[]{:S(2)}) collective-permute-start(bf16[2,4,2,2,16,128]{5,4,3,2,1,0:T(8,128)(2,1)S(1)} %get-tuple-element.43), channel_id=1, source_target_pairs={{0,8},{8,0},{16,24},{24,16},{32,40},{40,32},{48,56},{56,48},{1,9},... | collective-permute-start | bytes 393224 | tf_op jit(solution)/shard_map/ppermute | solution.py:203
  73.1 7.5 %collective-permute-start.14 = (bf16[4,4,2,2,16,128]{5,4,3,2,1,0:T(8,128)(2,1)S(1)}, bf16[4,4,2,2,16,128]{5,4,3,2,1,0:T(8,128)(2,1)S(1)}, u32[]{:S(2)}, u32[]{:S(2)}) collective-permute-start(bf16[4,4,2,2,16,128]{5,4,3,2,1,0:T(8,128)(2,1)S(1)} %pad_maximum_fusion.1), channel_id=1, source_target_pairs={{0,8},{8,0},{16,24},{24,16},{32,40},{40,32},{48,56},{56,48},{1,9},... | collective-permute-start | bytes 786440 | tf_op jit(solution)/shard_map/ppermute | solution.py:203
  73.5 8.8 %collective-permute-start.15 = (bf16[4,4,2,2,16,128]{5,4,3,2,1,0:T(8,128)(2,1)S(1)}, bf16[4,4,2,2,16,128]{5,4,3,2,1,0:T(8,128)(2,1)S(1)}, u32[]{:S(2)}, u32[]{:S(2)}) collective-permute-start(bf16[4,4,2,2,16,128]{5,4,3,2,1,0:T(8,128)(2,1)S(1)} %pad_maximum_fusion.2), channel_id=1, source_target_pairs={{0,56},{8,16},{16,8},{24,32},{32,24},{40,48},{48,40},{56,0},{1,57}... | collective-permute-start | bytes 786440 | tf_op jit(solution)/shard_map/ppermute | solution.py:203
  82.5 7.9 %collective-permute-start.17 = (bf16[4,4,2,2,16,128]{5,4,3,2,1,0:T(8,128)(2,1)S(1)}, bf16[4,4,2,2,16,128]{5,4,3,2,1,0:T(8,128)(2,1)S(1)}, u32[]{:S(2)}, u32[]{:S(2)}) collective-permute-start(bf16[4,4,2,2,16,128]{5,4,3,2,1,0:T(8,128)(2,1)S(1)} %get-tuple-element.36), channel_id=1, source_target_pairs={{0,56},{8,16},{16,8},{24,32},{32,24},{40,48},{48,40},{56,0},{1,57}... | collective-permute-start | bytes 786440 | tf_op jit(solution)/shard_map/ppermute | solution.py:203
  84.1 6.6 %collective-permute-start.16 = (bf16[4,4,2,2,16,128]{5,4,3,2,1,0:T(8,128)(2,1)S(1)}, bf16[4,4,2,2,16,128]{5,4,3,2,1,0:T(8,128)(2,1)S(1)}, u32[]{:S(2)}, u32[]{:S(2)}) collective-permute-start(bf16[4,4,2,2,16,128]{5,4,3,2,1,0:T(8,128)(2,1)S(1)} %get-tuple-element.37), channel_id=1, source_target_pairs={{0,8},{8,0},{16,24},{24,16},{32,40},{40,32},{48,56},{56,48},{1,9},... | collective-permute-start | bytes 786440 | tf_op jit(solution)/shard_map/ppermute | solution.py:203
  90.9 7.7 %collective-permute-start.19 = (bf16[4,4,2,2,16,128]{5,4,3,2,1,0:T(8,128)(2,1)S(1)}, bf16[4,4,2,2,16,128]{5,4,3,2,1,0:T(8,128)(2,1)S(1)}, u32[]{:S(2)}, u32[]{:S(2)}) collective-permute-start(bf16[4,4,2,2,16,128]{5,4,3,2,1,0:T(8,128)(2,1)S(1)} %get-tuple-element.34), channel_id=1, source_target_pairs={{0,56},{8,16},{16,8},{24,32},{32,24},{40,48},{48,40},{56,0},{1,57}... | collective-permute-start | bytes 786440 | tf_op jit(solution)/shard_map/ppermute | solution.py:203
  92.5 6.4 %collective-permute-start.18 = (bf16[4,4,2,2,16,128]{5,4,3,2,1,0:T(8,128)(2,1)S(1)}, bf16[4,4,2,2,16,128]{5,4,3,2,1,0:T(8,128)(2,1)S(1)}, u32[]{:S(2)}, u32[]{:S(2)}) collective-permute-start(bf16[4,4,2,2,16,128]{5,4,3,2,1,0:T(8,128)(2,1)S(1)} %get-tuple-element.35), channel_id=1, source_target_pairs={{0,8},{8,0},{16,24},{24,16},{32,40},{40,32},{48,56},{56,48},{1,9},... | collective-permute-start | bytes 786440 | tf_op jit(solution)/shard_map/ppermute | solution.py:203
  110.8 0.7 copy-start.2
